TPU v7x, 256 devices: a whole 4x4x8 slice. The times are simulated.
256 devices in a mesh: group: 8 (over z_lo, core), expert: 32 (over x, y, z_hi).
Axes of the slice: x: 4, y: 4, z: 8 (z_hi: 2, z_lo: 4; z = z_hi * 4 + z_lo), core: 2. Of those that a mesh axis runs over, the one named last changes fastest.
Arguments:
- q_latent: bfloat16 [2048, 64, 512], P('group', 'expert'), may hold values from -4 to 4
- q_rope: bfloat16 [2048, 4096], P('group', 'expert'), may hold values from -14 to 14
- self_latent: bfloat16 [2048, 512], P('group'), may hold values from -4 to 4
- self_rope: bfloat16 [2048, 64], P('group'), may hold values from -4 to 4
- cache_latent: bfloat16 [8, 512, 512], P('group'), may hold values from -4 to 4
- cache_rope: bfloat16 [8, 64, 512], P('group'), may hold values from -4 to 4
- prompt_of_sample: int32 [2048], P('group'), may hold values from 0 to 7, as said below
- w_uv: bfloat16 [64, 512, 128], P('expert'), may hold values from -0.25 to 0.25
- w_out: bfloat16 [8192, 7168], P('expert'), may hold values from -0.0625 to 0.0625
- residual: bfloat16 [2048, 7168], P(('group', 'expert')), may hold values from -40 to 40
- norm_gain: float32 [7168], replicated, may hold values from 0.1 to 1.9
- expert_ids: int32 [2048, 8], P(('group', 'expert')), may hold values from 0 to 31, all different within a row; in each aligned block of 8 rows (0 to 7, 8 to 15, ...) at most 3 rows name the same one
- gate_weight: float32 [2048, 8], P(('group', 'expert')), may hold values from 0.1 to 0.6
- w_gate: bfloat16 [32, 7168, 1024], P('expert', 'group'), may hold values from -0.0625 to 0.0625
- w_up: bfloat16 [32, 7168, 1024], P('expert', 'group'), may hold values from -0.0625 to 0.0625
- w_down: bfloat16 [32, 1024, 7168], P('expert', None, 'group'), may hold values from -0.1875 to 0.1875
Outputs:
- attn_proj: bfloat16 [2048, 7168], P(('group', 'expert'))
- moe_out: bfloat16 [2048, 7168], P(('group', 'expert'))
Inputs may be any that keep to these rules, and one draw needn't show every extreme that they name: `expert_ids`: in the rows of one device, each expert is named at most 3 times. `prompt_of_sample`: the 256 samples of each sample group form 8 * 4 consecutive blocks of equal size; all samples of a block share one prompt, and each prompt owns exactly 4 blocks of each group.
All inputs are finite; a program needn't handle non-finite values.
Results may differ from a plain program's by a relative error of at most 0.04.
Values may be sent and summed in bfloat16 or wider, within the bound.
No kernel may reach another device: no remote copies, remote signals or barrier semaphores. Data moves between devices by JAX's collectives and lax.ppermute only.
A program may use at most 64 MiB of HBM per device.

v0:
```python
import jax
import jax.numpy as jnp
from jax import lax
from jax.sharding import PartitionSpec as P

ROPE = 64
VD = 128


NORM_EPS = 1e-06


def attend_one(q_lat, q_pos_flat, self_lat, self_pos, cache_lat, cache_pos):
    score_scale = (VD + ROPE) ** (-0.5)
    q_pos = q_pos_flat.reshape(q_lat.shape[0], q_lat.shape[1], -1)
    self_scores = (
        jnp.einsum("shc,sc->sh", q_lat, self_lat, preferred_element_type=jnp.float32)
        + jnp.einsum("shr,sr->sh", q_pos, self_pos, preferred_element_type=jnp.float32)
    ) * score_scale
    scores = (
        jnp.einsum("shc,tc->sht", q_lat, cache_lat, preferred_element_type=jnp.float32)
        + jnp.einsum("shr,rt->sht", q_pos, cache_pos, preferred_element_type=jnp.float32)
    ) * score_scale
    top_score = jnp.maximum(jnp.max(scores, axis=-1), self_scores)
    weights = jnp.exp(scores - top_score[..., None])
    self_weight = jnp.exp(self_scores - top_score)
    totals = jnp.sum(weights, axis=-1) + self_weight
    summed = jnp.einsum(
        "sht,tc->shc", weights.astype(jnp.bfloat16), cache_lat, preferred_element_type=jnp.float32
    )
    self_b = lax.optimization_barrier(self_weight.astype(jnp.bfloat16)).astype(jnp.float32)
    summed = summed + self_b[..., None] * self_lat.astype(jnp.float32)[:, None, :]
    return summed / totals[..., None]


def body(
    q_latent,
    q_rope,
    self_latent,
    self_rope,
    cache_latent,
    cache_rope,
    prompt_of_sample,
    w_uv,
    w_out,
    residual,
    norm_gain,
    expert_ids,
    gate_weight,
    w_gate,
    w_up,
    w_down,
):
    groups = lax.axis_size("group")
    experts = lax.axis_size("expert")
    sample_count = q_latent.shape[0]
    per_prompt = sample_count // groups
    flat_order = jnp.argsort(prompt_of_sample, stable=True)
    prompt_rows = flat_order.reshape(groups, per_prompt)
    initial = jnp.zeros(q_latent.shape, jnp.float32)
    carry = initial
    pieces = (
        lax.all_gather(cache_latent, "group", axis=0, tiled=True),
        lax.all_gather(cache_rope, "group", axis=0, tiled=True),
    )
    start = jnp.int32(0)
    for inner in range(pieces[0].shape[0]):
        wanted = start + inner
        rows_pick = lax.dynamic_index_in_dim(prompt_rows, wanted, 0, keepdims=False)
        result = attend_one(
            jnp.take(q_latent, rows_pick, axis=0),
            jnp.take(q_rope, rows_pick, axis=0),
            jnp.take(self_latent, rows_pick, axis=0),
            jnp.take(self_rope, rows_pick, axis=0),
            pieces[0][inner],
            pieces[1][inner],
        )
        carry = carry.at[rows_pick].add(result)
    latent_out = carry.astype(jnp.bfloat16)
    head_value = jnp.einsum(
        "shc,hcv->shv", latent_out, w_uv, preferred_element_type=jnp.float32
    ).astype(jnp.bfloat16)
    value_rows = head_value.reshape(head_value.shape[0], -1)
    attn_proj = lax.psum_scatter(
        jnp.dot(value_rows, w_out, preferred_element_type=jnp.float32).astype(jnp.bfloat16),
        "expert",
        scatter_dimension=0,
        tiled=True,
    )
    mixed = residual.astype(jnp.float32) + lax.optimization_barrier(attn_proj).astype(jnp.float32)
    normed = (
        mixed * lax.rsqrt(jnp.mean(mixed * mixed, axis=-1, keepdims=True) + NORM_EPS) * norm_gain
    ).astype(jnp.bfloat16)
    tokens_here = normed.shape[0]
    top_count = expert_ids.shape[1]
    capacity = tokens_here * top_count // experts + 1
    flat_ids = expert_ids.reshape(-1)
    pair_count = flat_ids.shape[0]
    onehot = (flat_ids[:, None] == jnp.arange(experts, dtype=jnp.int32)[None, :]).astype(jnp.int32)
    earlier = jnp.cumsum(onehot, axis=0) - onehot
    slot_of = jnp.sum(earlier * onehot, axis=1)
    target = flat_ids * capacity + slot_of
    slot_rows = experts * capacity
    to_slot = (target[None, :] == jnp.arange(slot_rows, dtype=jnp.int32)[:, None]).astype(
        jnp.float32
    )
    from_token = (
        jnp.arange(pair_count, dtype=jnp.int32)[:, None] // top_count
        == jnp.arange(tokens_here, dtype=jnp.int32)[None, :]
    ).astype(jnp.float32)
    routing = jnp.dot(to_slot, from_token, preferred_element_type=jnp.float32).astype(jnp.bfloat16)
    dispatch_rows = jnp.dot(routing, normed, preferred_element_type=jnp.float32).astype(
        jnp.bfloat16
    )
    feature_share = normed.shape[1] // groups
    outgoing = dispatch_rows.reshape(experts, capacity, groups, feature_share)
    arrived = lax.all_to_all(
        lax.all_to_all(outgoing, "group", split_axis=2, concat_axis=2, tiled=True),
        "expert",
        split_axis=0,
        concat_axis=0,
        tiled=True,
    )
    rows_in = arrived.reshape(-1, feature_share)
    gate_part = jnp.dot(rows_in, w_gate[0], preferred_element_type=jnp.float32)
    up_part = jnp.dot(rows_in, w_up[0], preferred_element_type=jnp.float32)
    gate_sum, up_sum = (
        lax.psum(gate_part.astype(jnp.bfloat16), "group").astype(jnp.float32),
        lax.psum(up_part.astype(jnp.bfloat16), "group").astype(jnp.float32),
    )
    hidden = (jax.nn.silu(gate_sum) * up_sum).astype(jnp.bfloat16)
    expert_part = jnp.dot(hidden, w_down[0], preferred_element_type=jnp.float32)
    expert_out = expert_part.astype(jnp.bfloat16).reshape(experts, capacity, groups, feature_share)
    returned = lax.all_to_all(
        lax.all_to_all(expert_out, "group", split_axis=2, concat_axis=2, tiled=True),
        "expert",
        split_axis=0,
        concat_axis=0,
        tiled=True,
    )
    slot_out = returned.reshape(slot_rows, -1)
    picked = jnp.take(slot_out, target, axis=0).reshape(tokens_here, top_count, -1)
    moe_out = jnp.sum(picked.astype(jnp.float32) * gate_weight[:, :, None], axis=1).astype(
        jnp.bfloat16
    )
    return (attn_proj, moe_out)


def solution(mesh):
    in_specs = (
        P("group", "expert", None),
        P("group", "expert"),
        P("group", None),
        P("group", None),
        P("group", None, None),
        P("group", None, None),
        P("group"),
        P("expert", None, None),
        P("expert", None),
        P(("group", "expert"), None),
        P(),
        P(("group", "expert"), None),
        P(("group", "expert"), None),
        P("expert", "group", None),
        P("expert", "group", None),
        P("expert", None, "group"),
    )
    out_specs = (P(("group", "expert"), None), P(("group", "expert"), None))
    return jax.shard_map(body, mesh=mesh, in_specs=in_specs, out_specs=out_specs, check_vma=False)
```

profile of v0, /device:TPU:32, one launch (start us, length us, event | category | flops | bytes accessed | tf_op | source)
XLA Modules:
  0.0 672.2 jit_solution(1794750633724801514)
XLA Ops:
  8.0 3.8 sort.17
  12.1 1.4 gather_fusion.26
  13.5 1.4 gather_fusion.30
  14.9 0.9 copy.162
  17.0 1.4 gather_fusion.22
  19.0 1.4 gather_fusion.18
  21.1 1.4 gather_fusion.14
  23.1 1.4 gather_fusion.10
  25.2 1.4 gather_fusion.2
  26.6 1.4 gather_fusion.6
  29.1 1.6 gather_fusion.3
  30.8 1.6 gather_fusion.7
  32.4 1.6 gather_fusion.11
  38.4 0.7 gather_fusion.1
  39.1 0.7 gather_fusion.5
  39.8 0.7 gather_fusion.9
  40.5 0.7 gather_fusion.13
  41.2 0.7 gather_fusion.17
  41.9 0.7 gather_fusion.21
  43.3 0.7 gather_fusion.29
  50.7 0.7 fusion.145
  53.3 0.7 fusion.141
  56.0 0.7 fusion.137
  56.7 0.9 broadcast_select_fusion.4
  60.0 0.7 fusion.133
  63.3 16.1 %all_gather.7 = bf16[8,64,512]{2,1,0:T(8,128)(2,1)S(1)} all-gather(bf16[1,64,512]{2,1,0:T(8,128)(2,1)S(1)} %copy-done.12), channel_id=1, replica_groups=mesh['group'=8,'expert'=32] {'group'}, dimensions={0}, use_global_device_ids=true | all-gather | bytes 589824 | tf_op jit(solution)/shard_map/all_gather | solution.py:64
  80.0 0.8 fusion.69
  80.9 0.8 fusion.70
  81.8 0.8 fusion.71
  82.7 1.6 fusion.190
  85.8 1.3 fusion.21
  87.2 1.4 fusion.189
  90.2 1.3 fusion.23
  92.2 1.1 fusion.25
  96.4 0.8 copy.171
  98.0 0.8 copy.167
  99.6 0.8 copy.163
  100.7 3.2 scatter_fusion
  103.9 3.2 scatter_fusion.1
  107.1 3.2 scatter_fusion.2
  110.4 1.9 scatter_fusion.3
  112.3 1.8 scatter_fusion.4
  114.1 1.8 scatter_fusion.5
  115.9 1.8 scatter_fusion.6
  117.7 1.8 scatter_fusion.7
  119.9 1.3 convolution_convert_fusion.2
  121.2 5.0 convolution_convert_fusion
  127.3 266.0 %reduce-scatter.2.cloned.1.call-done = bf16[8,7168]{1,0:T(8,128)(2,1)} async-done(((bf16[256,7168]{1,0:T(8,128)(2,1)}), bf16[8,7168]{1,0:T(8,128)(2,1)}) %reduce-scatter.2.cloned.1.call-update) | async-done | bytes 114704 | tf_op jit(solution)/shard_map/reduce_scatter | solution.py:84
  393.3 1.1 multiply_reduce_fusion.1
  394.4 1.8 convolution_convert_fusion.1
  396.5 35.1 %all_to_all.20 = bf16[32,3,8,896]{3,0,1,2:T(8,128)(2,1)S(1)} all-to-all(bf16[32,3,8,896]{3,0,1,2:T(8,128)(2,1)S(1)} %copy.194), channel_id=1, replica_groups=mesh['group'=8,'expert'=32] {'group'}, dimensions={2} | all-to-all | bytes 2752512 | tf_op jit(solution)/shard_map/all_to_all | solution.py:118
  432.0 43.3 %all_to_all.21 = bf16[32,3,8,896]{3,2,1,0:T(8,128)(2,1)S(1)} all-to-all(bf16[32,3,8,896]{3,2,1,0:T(8,128)(2,1)S(1)} %copy.195), channel_id=1, replica_groups=mesh['group'=8,'expert'=32] {'expert'}, dimensions={0} | all-to-all | bytes 2752512 | tf_op jit(solution)/shard_map/all_to_all | solution.py:117
  475.3 3.0 fusion.14
  478.3 3.0 fusion.11
  481.2 81.3 %all-reduce.3.cloned.1.call-done = (bf16[768,1024]{1,0:T(8,128)(2,1)}, bf16[768,1024]{1,0:T(8,128)(2,1)}) async-done(((bf16[768,1024]{1,0:T(8,128)(2,1)}, bf16[768,1024]{1,0:T(8,128)(2,1)}), (bf16[768,1024]{1,0:T(8,128)(2,1)}, bf16[768,1024]{1,0:T(8,128)(2,1)})) %all-reduce.3.cloned.1.call-update) | async-done | bytes 3145744 | tf_op jit(solution)/shard_map/psum | solution.py:129
  562.5 4.4 fusion.17
  567.1 38.7 %all_to_all.22 = bf16[32,3,8,896]{3,0,1,2:T(8,128)(2,1)S(1)} all-to-all(bf16[32,3,8,896]{3,0,1,2:T(8,128)(2,1)S(1)} %copy.196), channel_id=1, replica_groups=mesh['group'=8,'expert'=32] {'group'}, dimensions={2} | all-to-all | bytes 2752512 | tf_op jit(solution)/shard_map/all_to_all | solution.py:135
  605.9 1.5 copy.197
  607.4 11.0 %all-to-all-start.3 = ((bf16[32,3,8,896]{3,2,1,0:T(8,128)(2,1)}), bf16[32,3,8,896]{3,2,1,0:T(8,128)(2,1)S(1)}, u32[]{:S(2)}, u32[]{:S(2)}) async-start(bf16[32,3,8,896]{3,2,1,0:T(8,128)(2,1)} %copy.197), calls=%async_computation.4 | async-start | bytes 2752512 | tf_op jit(solution)/shard_map/all_to_all | solution.py:134
  618.7 39.7 %all-to-all-done.3 = bf16[32,3,8,896]{3,2,1,0:T(8,128)(2,1)S(1)} async-done(((bf16[32,3,8,896]{3,2,1,0:T(8,128)(2,1)}), bf16[32,3,8,896]{3,2,1,0:T(8,128)(2,1)S(1)}, u32[]{:S(2)}, u32[]{:S(2)}) %all-to-all-start.3) | async-done | bytes 1376288 | tf_op jit(solution)/shard_map/all_to_all | solution.py:134
  658.4 1.1 copy-done.2
  659.5 1.6 copy.232
  661.1 2.1 gather_fusion
  663.1 2.5 multiply_reduce_fusion
  (268 shorter events, 37.9 us)
Async XLA Ops:
  7.2 468.1 %copy-start = (bf16[1,896,1024]{2,1,0:T(8,128)(2,1)S(1)}, bf16[1,896,1024]{2,1,0:T(8,128)(2,1)}, u32[]{:S(2)}) copy-start(bf16[1,896,1024]{2,1,0:T(8,128)(2,1)} %param.38) | copy-start | bytes 5505028
  7.2 26.8 %copy-start.1 = (bf16[256,512]{1,0:T(8,128)(2,1)S(1)}, bf16[256,512]{1,0:T(8,128)(2,1)}, u32[]{:S(2)}) copy-start(bf16[256,512]{1,0:T(8,128)(2,1)} %param.26) | copy-start | bytes 786436
  7.2 31.2 %copy-start.4 = (bf16[256,2,512]{2,1,0:T(2,128)(2,1)S(1)}, bf16[256,2,512]{2,1,0:T(2,128)(2,1)}, u32[]{:S(2)}) copy-start(bf16[256,2,512]{2,1,0:T(2,128)(2,1)} %param.24) | copy-start | bytes 1572868
  7.2 75.5 %all-gather.2.cloned.1.call-start = ((), (), s32[]{:S(2)}) async-start(), calls=%async_computation.5 | async-start | bytes 4718592 | tf_op jit(solution)/shard_map/all_gather | solution.py:63
  7.9 385.3 %reduce-scatter.2.cloned.1.call-start = ((), (), s32[]{:S(2)}) async-start(), calls=%async_computation.6 | async-start | bytes 3784704 | tf_op jit(solution)/shard_map/reduce_scatter | solution.py:84
  11.9 1.6 copy-start.44
  11.9 1.6 copy-start.46
  11.9 9.1 %copy-start.48 = (s32[32]{0:T(128)}, s32[32]{0:T(128)S(1)}, u32[]{:S(2)}) copy-start(s32[32]{0:T(128)S(1)} %get-tuple-element.61) | copy-start | bytes 388
  11.9 11.2 %copy-start.53 = (s32[32]{0:T(128)}, s32[32]{0:T(128)S(1)}, u32[]{:S(2)}) copy-start(s32[32]{0:T(128)S(1)} %get-tuple-element.67) | copy-start | bytes 388
  12.0 16.1 %copy-start.50 = (s32[32]{0:T(128)}, s32[32]{0:T(128)S(1)}, u32[]{:S(2)}) copy-start(s32[32]{0:T(128)S(1)} %get-tuple-element.63) | copy-start | bytes 388
  12.0 16.1 %copy-start.52 = (s32[32]{0:T(128)}, s32[32]{0:T(128)S(1)}, u32[]{:S(2)}) copy-start(s32[32]{0:T(128)S(1)} %get-tuple-element.65) | copy-start | bytes 388
  12.0 16.1 %copy-start.54 = (s32[32]{0:T(128)}, s32[32]{0:T(128)S(1)}, u32[]{:S(2)}) copy-start(s32[32]{0:T(128)S(1)} %get-tuple-element.69) | copy-start | bytes 388
  12.0 16.1 %copy-start.55 = (s32[32]{0:T(128)}, s32[32]{0:T(128)S(1)}, u32[]{:S(2)}) copy-start(s32[32]{0:T(128)S(1)} %get-tuple-element.71) | copy-start | bytes 388
  12.0 38.0 %copy-start.26 = (pred[32]{0:T(512)(128)(4,1)}, pred[32]{0:T(512)(128)(4,1)S(1)}, u32[]{:S(2)}) copy-start(pred[32]{0:T(512)(128)(4,1)S(1)} %get-tuple-element.68) | copy-start | bytes 100
  12.0 38.0 %copy-start.28 = (pred[32]{0:T(512)(128)(4,1)}, pred[32]{0:T(512)(128)(4,1)S(1)}, u32[]{:S(2)}) copy-start(pred[32]{0:T(512)(128)(4,1)S(1)} %get-tuple-element.70) | copy-start | bytes 100
  12.0 44.0 %copy-start.30 = (pred[32]{0:T(512)(128)(4,1)}, pred[32]{0:T(512)(128)(4,1)S(1)}, u32[]{:S(2)}) copy-start(pred[32]{0:T(512)(128)(4,1)S(1)} %get-tuple-element.64) | copy-start | bytes 100
  12.0 44.0 %copy-start.31 = (pred[32]{0:T(512)(128)(4,1)}, pred[32]{0:T(512)(128)(4,1)S(1)}, u32[]{:S(2)}) copy-start(pred[32]{0:T(512)(128)(4,1)S(1)} %get-tuple-element.66) | copy-start | bytes 100
  28.4 12.8 %copy-start.19 = (bf16[32,2,64]{2,1,0:T(2,128)(2,1)}, bf16[32,2,64]{2,1,0:T(2,128)(2,1)S(1)}, u32[]{:S(2)}) copy-start(bf16[32,2,64]{2,1,0:T(2,128)(2,1)S(1)} %reshape.260) | copy-start | bytes 24580
  44.0 6.6 copy-start.21
  44.4 6.3 copy-start.23
  44.5 8.0 %copy-start.22 = (bf16[32,2,64]{2,1,0:T(2,128)(2,1)}, bf16[32,2,64]{2,1,0:T(2,128)(2,1)S(1)}, u32[]{:S(2)}) copy-start(bf16[32,2,64]{2,1,0:T(2,128)(2,1)S(1)} %reshape.253) | copy-start | bytes 24580
  50.7 9.3 %copy-start.27 = (pred[32]{0:T(512)(128)(4,1)S(1)}, pred[32]{0:T(512)(128)(4,1)}, u32[]{:S(2)}) copy-start(pred[32]{0:T(512)(128)(4,1)} %copy-done.26) | copy-start | bytes 100
  50.7 9.3 %copy-start.29 = (pred[32]{0:T(512)(128)(4,1)S(1)}, pred[32]{0:T(512)(128)(4,1)}, u32[]{:S(2)}) copy-start(pred[32]{0:T(512)(128)(4,1)} %copy-done.28) | copy-start | bytes 100
  51.6 11.6 %copy-start.12 = (bf16[1,64,512]{2,1,0:T(8,128)(2,1)S(1)}, bf16[1,64,512]{2,1,0:T(8,128)(2,1)}, u32[]{:S(2)}) copy-start(bf16[1,64,512]{2,1,0:T(8,128)(2,1)} %param.29) | copy-start | bytes 196612
  52.5 26.9 %copy-start.20 = (bf16[32,2,64]{2,1,0:T(2,128)(2,1)S(1)}, bf16[32,2,64]{2,1,0:T(2,128)(2,1)}, u32[]{:S(2)}) copy-start(bf16[32,2,64]{2,1,0:T(2,128)(2,1)} %copy-done.19) | copy-start | bytes 24580
  57.6 0.6 copy-start.10
  57.6 28.2 %copy-start.18 = (f32[32,512]{1,0:T(8,128)S(1)}, f32[32,512]{1,0:T(8,128)}, u32[]{:S(2)}) copy-start(f32[32,512]{1,0:T(8,128)} %get-tuple-element.103) | copy-start | bytes 196612
  60.9 0.6 copy-start.6
  60.9 19.1 %copy-start.8 = (bf16[32,2,512]{2,1,0:T(2,128)(2,1)}, bf16[32,2,512]{2,1,0:T(2,128)(2,1)S(1)}, u32[]{:S(2)}) copy-start(bf16[32,2,512]{2,1,0:T(2,128)(2,1)S(1)} %get-tuple-element.94) | copy-start | bytes 196612
  62.4 27.8 %copy-start.17 = (f32[32,512]{1,0:T(8,128)S(1)}, f32[32,512]{1,0:T(8,128)}, u32[]{:S(2)}) copy-start(f32[32,512]{1,0:T(8,128)} %get-tuple-element.28) | copy-start | bytes 196612
  80.9 11.1 %copy-start.37 = (f32[32,1,2]{0,2,1:T(2,128)S(1)}, f32[32,1,2]{0,2,1:T(2,128)}, u32[]{:S(2)}) copy-start(f32[32,1,2]{0,2,1:T(2,128)} %copy.221) | copy-start | bytes 772
  80.9 11.1 %copy-start.43 = (f32[32,1,2]{0,2,1:T(2,128)S(1)}, f32[32,1,2]{0,2,1:T(2,128)}, u32[]{:S(2)}) copy-start(f32[32,1,2]{0,2,1:T(2,128)} %copy.219) | copy-start | bytes 772
  82.7 8.9 %copy-start.3 = (bf16[8,512,512]{2,1,0:T(8,128)(2,1)S(1)}, bf16[8,512,512]{2,1,0:T(8,128)(2,1)}, u32[]{:S(2)}) copy-start(bf16[8,512,512]{2,1,0:T(8,128)(2,1)} %all-gather.2.cloned.1.call-done) | copy-start | bytes 12582916
  87.1 6.7 %copy-start.38 = (f32[32,1,2]{0,2,1:T(2,128)S(1)}, f32[32,1,2]{0,2,1:T(2,128)}, u32[]{:S(2)}) copy-start(f32[32,1,2]{0,2,1:T(2,128)} %copy.217) | copy-start | bytes 772
  87.1 6.7 %copy-start.41 = (f32[32,1,2]{0,2,1:T(2,128)S(1)}, f32[32,1,2]{0,2,1:T(2,128)}, u32[]{:S(2)}) copy-start(f32[32,1,2]{0,2,1:T(2,128)} %copy.215) | copy-start | bytes 772
  87.1 6.9 %copy-start.16 = (f32[32,512]{1,0:T(8,128)S(1)}, f32[32,512]{1,0:T(8,128)}, u32[]{:S(2)}) copy-start(f32[32,512]{1,0:T(8,128)} %get-tuple-element.32) | copy-start | bytes 196612
  91.5 3.4 copy-start.35
  91.5 3.4 copy-start.42
  92.2 3.3 copy-start.11
  93.3 2.5 copy-start.34
  93.3 2.5 copy-start.39
  93.4 2.7 copy-start.15
  94.1 3.0 copy-start.9
  94.3 3.1 copy-start.33
  94.4 3.1 copy-start.40
  94.4 3.3 copy-start.14
  95.1 3.7 copy-start.7
  95.3 3.8 copy-start.32
  95.4 3.8 copy-start.36
  95.4 4.0 copy-start.13
  97.7 14.6 %copy-start.51 = (s32[32]{0:T(128)S(1)}, s32[32]{0:T(128)}, u32[]{:S(2)}) copy-start(s32[32]{0:T(128)} %copy-done.50) | copy-start | bytes 388
  98.0 16.1 %copy-start.49 = (s32[32]{0:T(128)S(1)}, s32[32]{0:T(128)}, u32[]{:S(2)}) copy-start(s32[32]{0:T(128)} %copy-done.48) | copy-start | bytes 388
  98.0 17.9 %copy-start.47 = (s32[32]{0:T(128)S(1)}, s32[32]{0:T(128)}, u32[]{:S(2)}) copy-start(s32[32]{0:T(128)} %copy-done.46) | copy-start | bytes 388
  98.8 18.9 %copy-start.45 = (s32[32]{0:T(128)S(1)}, s32[32]{0:T(128)}, u32[]{:S(2)}) copy-start(s32[32]{0:T(128)} %copy-done.44) | copy-start | bytes 388
  126.1 0.7 copy-start.24
  126.1 267.1 %copy-start.5 = (bf16[8,7168]{1,0:T(8,128)(2,1)S(1)}, bf16[8,7168]{1,0:T(8,128)(2,1)}, u32[]{:S(2)}) copy-start(bf16[8,7168]{1,0:T(8,128)(2,1)} %param.33) | copy-start | bytes 344068
  126.1 268.2 %copy-start.25 = (f32[7168]{0:T(1024)S(1)}, f32[7168]{0:T(1024)}, u32[]{:S(2)}) copy-start(f32[7168]{0:T(1024)} %param.34) | copy-start | bytes 86020
  126.2 436.4 %all-reduce.3.cloned.1.call-start = ((), (), s32[]{:S(2)}) async-start(), calls=%async_computation.7 | async-start | bytes 6291456 | tf_op jit(solution)/shard_map/psum | solution.py:129
  475.3 3.0 copy-start.57
  607.4 51.0 %all-to-all-start.3 = ((bf16[32,3,8,896]{3,2,1,0:T(8,128)(2,1)}), bf16[32,3,8,896]{3,2,1,0:T(8,128)(2,1)S(1)}, u32[]{:S(2)}, u32[]{:S(2)}) async-start(bf16[32,3,8,896]{3,2,1,0:T(8,128)(2,1)} %copy.197), calls=%async_computation.4 | async-start | bytes 2752512 | tf_op jit(solution)/shard_map/all_to_all | solution.py:134
  658.4 1.1 copy-start.2
  661.1 2.1 copy-start.56
Sparse Core Ops, SparseCore 0:
  9.8 53.0 all-gather.1
  126.3 266.9 reduce-scatter.1
  481.4 81.1 all-reduce.2
where the time goes:
time: 674 us; the launch traced here: 672 us
  waiting for transfers between devices  388 us (58%)
  blocking collectives  133 us (20%)
  local copies, waits for them, and re-layouts  54.3 us (8%)
  other arithmetic  36.3 us (5%)
  matrix products  34.6 us (5%)
  between operations  14.9 us (2%)
  starting transfers between devices  11.2 us (2%)
    reduce_scatter x1, waiting for transfers between devices, body(): lax.psum_scatter(jnp.dot(value_rows, w_out, preferred_element_type=jnp.fl...  266 us
    psum x1, waiting for transfers between devices, body(): lax.psum(up_part.astype(jnp.bfloat16), 'group').astype(jnp.float32)  81.3 us
    all_to_all x1, blocking collectives, body(): lax.all_to_all(lax.all_to_all(outgoing, 'group', split_axis=2, concat_axi...  43.3 us
    all_to_all x1, waiting for transfers between devices, body(): lax.all_to_all(lax.all_to_all(expert_out, 'group', split_axis=2, concat_a...  39.7 us
    all_to_all x1, blocking collectives, body(): lax.all_to_all(expert_out, 'group', split_axis=2, concat_axis=2, tiled=True)  38.7 us
    all_to_all x1, blocking collectives, body(): lax.all_to_all(outgoing, 'group', split_axis=2, concat_axis=2, tiled=True)  35.1 us
    scatter-add x8, other arithmetic, body(): carry = carry.at[rows_pick].add(result)  18.8 us
    all_gather x1, blocking collectives, body(): lax.all_gather(cache_rope, 'group', axis=0, tiled=True)  16.1 us
  transfers between devices with their start and end apart: 4, of which 3 were waited for; matrix products, arithmetic and copies ran while one was open for 9% of the time, Pallas kernels for 0%

commit v1 on v0

v1 whole, which is shorter than its diff:
```python
import jax
import jax.numpy as jnp
from jax import lax
from jax.sharding import Mesh, PartitionSpec as P

ROPE = 64
VD = 128
NORM_EPS = 1e-06
RUNS = 4
CAP = 3

GROUP = ("zlo", "core")
XY = ("x", "y")
BF = jnp.bfloat16
F32 = jnp.float32


def dot(a, b):
    return jnp.dot(a, b, preferred_element_type=F32)


def dot_t(a, b):
    return lax.dot_general(a, b, (((1,), (1,)), ((), ())), preferred_element_type=F32)


def split3(value):
    one = value.astype(BF)
    rest = value - one.astype(F32)
    two = rest.astype(BF)
    three = (rest - two.astype(F32)).astype(BF)
    return one, two, three


def exchange(value, axes):
    return lax.all_to_all(value, axes, 0, 0, tiled=True)


def block_permutation(prompt_of_sample, prompts):
    samples = prompt_of_sample.shape[0]
    block = samples // (prompts * RUNS)
    own = prompt_of_sample.reshape(-1, block)[:, 0]
    blocks = own.shape[0]
    at = jnp.arange(blocks, dtype=jnp.int32)
    same = (own[:, None] == own[None, :]) & (at[None, :] < at[:, None])
    rank = own * RUNS + jnp.sum(same.astype(jnp.int32), axis=1)
    rank_of_sample = jnp.repeat(rank, block) * block + jnp.arange(samples, dtype=jnp.int32) % block
    return rank_of_sample


def body(
    q_latent,
    q_rope,
    self_latent,
    self_rope,
    cache_latent,
    cache_rope,
    prompt_of_sample,
    w_uv,
    w_out,
    residual,
    norm_gain,
    expert_ids,
    gate_weight,
    w_gate,
    w_up,
    w_down,
):
    groups = lax.axis_size(GROUP)
    halves = lax.axis_size("zhi")
    planes = lax.axis_size(XY)
    my_half = lax.axis_index("zhi")
    my_core = lax.axis_index("core")
    samples, heads, lat = q_latent.shape
    experts = planes * halves
    rows_here = residual.shape[0]
    width = residual.shape[1]
    share = width // groups
    scale = (VD + ROPE) ** (-0.5)

    table = jnp.concatenate([expert_ids.astype(F32), gate_weight], axis=1)
    table = lax.all_gather(table, GROUP + ("zhi",), axis=0, tiled=True)
    tokens = table.shape[0]
    top = expert_ids.shape[1]
    ids = table[:, :top].astype(jnp.int32)
    gates = table[:, top:]
    wanted = jnp.arange(planes, dtype=jnp.int32) * halves + my_half
    hit = ids[:, :, None] == wanted[None, None, :]
    member = jnp.any(hit, axis=1)
    gate_of = jnp.sum(jnp.where(hit, gates[:, :, None], 0.0), axis=1)
    before = jnp.cumsum(member.astype(jnp.int32), axis=0) - member.astype(jnp.int32)
    slots = tokens // rows_here * CAP
    place = jnp.where(member, before, -1).T
    routed = place[:, None, :] == jnp.arange(slots, dtype=jnp.int32)[None, :, None]
    routing = routed.reshape(planes * slots, tokens).astype(BF)
    weights = jnp.where(routed, gate_of.T[:, None, :], 0.0).reshape(planes * slots, tokens)
    gate_hi = weights.astype(BF)
    gate_lo = (weights - gate_hi.astype(F32)).astype(BF)

    rank = block_permutation(prompt_of_sample, groups)
    to_rank = (rank[None, :] == jnp.arange(samples, dtype=jnp.int32)[:, None]).astype(BF)
    q_all = jnp.concatenate([q_latent.reshape(samples, heads * lat), q_rope], axis=1)
    q_sorted = dot(to_rank, q_all).astype(BF)
    q_here = exchange(q_sorted, GROUP)
    keys = cache_latent[0]
    rope_keys = cache_rope[0]
    outs = []
    stats = []
    for head in range(heads):
        q_head = q_here[:, head * lat : (head + 1) * lat]
        r_head = q_here[:, heads * lat + head * ROPE : heads * lat + (head + 1) * ROPE]
        score = (dot_t(q_head, keys) + dot(r_head, rope_keys)) * scale
        best = jnp.max(score, axis=-1, keepdims=True)
        weight = jnp.exp(score - best)
        total = jnp.sum(weight, axis=-1, keepdims=True)
        latent = (dot(weight.astype(BF), keys) / total).astype(BF)
        outs.append(dot(latent, w_uv[head]).astype(BF))
        stats.extend(split3(best + jnp.log(total)))
    pad = jnp.zeros((samples, VD - len(stats)), BF)
    back = exchange(jnp.concatenate(outs + stats + [pad], axis=1), GROUP)
    back = lax.dot_general(to_rank, back, (((0,), (0,)), ((), ())), preferred_element_type=F32)
    values = []
    self_wide = self_latent.astype(F32)
    for head in range(heads):
        self_score = (
            jnp.sum(q_latent[:, head].astype(F32) * self_wide, axis=-1, keepdims=True)
            + jnp.sum(
                q_rope[:, head * ROPE : (head + 1) * ROPE].astype(F32) * self_rope.astype(F32),
                axis=-1,
                keepdims=True,
            )
        ) * scale
        at = heads * VD + 3 * head
        lse = back[:, at : at + 1] + back[:, at + 1 : at + 2] + back[:, at + 2 : at + 3]
        best = jnp.maximum(lse, self_score)
        cache_part = jnp.exp(lse - best)
        self_part = jnp.exp(self_score - best)
        own_value = dot(self_latent, w_uv[head])
        mixed_value = cache_part * back[:, head * VD : (head + 1) * VD] + self_part * own_value
        values.append((mixed_value / (cache_part + self_part)).astype(BF))
    head_value = jnp.concatenate(values, axis=1)

    partial = dot(head_value, w_out).astype(BF)
    arrived = exchange(partial, XY).reshape(planes, halves * rows_here, width)
    near = jnp.sum(arrived.astype(F32), axis=0).reshape(halves, rows_here, width)
    is_mine = (jnp.arange(halves) == my_half)[:, None, None]
    with_residual = near + jnp.where(is_mine, residual.astype(F32)[None], 0.0)
    far = lax.ppermute(with_residual.astype(BF), "zhi", [(0, 1), (1, 0)]).astype(F32)
    attn_proj = lax.dynamic_index_in_dim(near + far, my_half, 0, keepdims=False).astype(BF)
    mixed = with_residual + far
    normed = (
        mixed * lax.rsqrt(jnp.mean(mixed * mixed, axis=-1, keepdims=True) + NORM_EPS) * norm_gain
    ).astype(BF)

    by_block = normed.reshape(halves * rows_here, groups, share).transpose(1, 0, 2)
    token_rows = exchange(by_block, GROUP).reshape(tokens, share)
    rows_in = exchange(dot(routing, token_rows).astype(BF), XY)

    half_rows = rows_in.shape[0] // 2
    w_both = (w_gate[0], w_up[0])

    def both(rows):
        return jnp.concatenate([dot(rows, w).astype(BF) for w in w_both], axis=1)

    other_rows = lax.dynamic_slice_in_dim(rows_in, (1 - my_core) * half_rows, half_rows, 0)
    own_rows = lax.dynamic_slice_in_dim(rows_in, my_core * half_rows, half_rows, 0)
    from_core = lax.ppermute(both(other_rows), "core", [(0, 1), (1, 0)])
    chip_sum = (both(own_rows).astype(F32) + from_core.astype(F32)).astype(BF)
    lines = lax.axis_size("zlo")
    parts = exchange(chip_sum, "zlo").reshape(lines, half_rows // lines, -1)
    sums = jnp.sum(parts.astype(F32), axis=0)
    ffe = sums.shape[1] // 2
    hidden = (jax.nn.silu(sums[:, :ffe]) * sums[:, ffe:]).astype(BF)
    hidden = lax.all_gather(hidden, ("core", "zlo"), axis=0, tiled=True)
    expert_out = dot(hidden, w_down[0]).astype(BF)

    returned = exchange(expert_out, XY)
    over_rows = (((0,), (0,)), ((), ()))
    moe = lax.dot_general(gate_hi, returned, over_rows, preferred_element_type=F32)
    moe = moe + lax.dot_general(gate_lo, returned, over_rows, preferred_element_type=F32)
    moe = exchange(moe.astype(BF), GROUP + ("zhi",))
    moe = jnp.sum(moe.reshape(groups, halves, rows_here, share).astype(F32), axis=1).astype(BF)
    moe_out = moe.transpose(1, 0, 2).reshape(rows_here, width)
    return (attn_proj, moe_out)


def solution(mesh):
    fine = Mesh(mesh.devices.reshape(4, 2, 4, 4, 2), ("zlo", "core", "x", "y", "zhi"))
    g = GROUP
    e = XY + ("zhi",)
    in_specs = (
        P(g, e, None),
        P(g, e),
        P(g, None),
        P(g, None),
        P(g, None, None),
        P(g, None, None),
        P(g),
        P(e, None, None),
        P(e, None),
        P(g + e, None),
        P(),
        P(g + e, None),
        P(g + e, None),
        P(e, g, None),
        P(e, g, None),
        P(e, None, g),
    )
    out_specs = (P(g + e, None), P(g + e, None))
    return jax.shard_map(body, mesh=fine, in_specs=in_specs, out_specs=out_specs, check_vma=False)
```

time: 674 us -> 340 us (0.50)
  waiting for transfers between devices: 388 us -> 129 us
  blocking collectives: 133 us -> 81.2 us
  starting transfers between devices: 11.2 us -> 60.6 us
  local copies, waits for them, and re-layouts: 54.3 us -> 12.9 us
  other arithmetic: 36.3 us -> 12.2 us
  matrix products: 34.6 us -> 27.1 us
    reduce_scatter x1 -> x0, waiting for transfers between devices: 266 us -> none  [body(): lax.psum_scatter(jnp.dot(value_rows, w_out, preferred_element_type=jnp.fl...]
    psum x1 -> x0, waiting for transfers between devices: 81.3 us -> none  [body(): lax.psum(up_part.astype(jnp.bfloat16), 'group').astype(jnp.float32)]
    all_to_all x3 -> x1, blocking collectives: 117 us -> 40.1 us  [exchange(): return lax.all_to_all(value, axes, 0, 0, tiled=True)]
    all_to_all x1 -> x7, starting transfers between devices: 11 us -> 55.7 us  [exchange(): return lax.all_to_all(value, axes, 0, 0, tiled=True)]
    all_to_all x1 -> x7, waiting for transfers between devices: 39.7 us -> 81.9 us  [exchange(): return lax.all_to_all(value, axes, 0, 0, tiled=True)]
    all_gather x1, waiting for transfers between devices: 0.02 us -> 41.4 us  [body(): hidden = lax.all_gather(hidden, ('core', 'zlo'), axis=0, tiled=True)]
    gather x33 -> x0, local copies, waits for them, and re-layouts: 31.8 us -> none  [the longest x8 11.4 us: body(): jnp.take(q_rope, rows_pick, axis=0)]
    all_gather x1, blocking collectives: 16.1 us -> 41.1 us  [body(): table = lax.all_gather(table, GROUP + ('zhi',), axis=0, tiled=True)]
  transfers between devices with their start and end apart: 4 -> 10, of which waited for: 3 -> 10; matrix products, arithmetic and copies ran while one was open for 9% -> 2% of each run, Pallas kernels for 0% -> 0%
where the time goes in v1:
time: 340 us; the launch traced here: 338 us
  waiting for transfers between devices  129 us (38%)
  blocking collectives  81.2 us (24%)
  starting transfers between devices  60.6 us (18%)
  matrix products  27.1 us (8%)
  between operations  14.4 us (4%)
  local copies, waits for them, and re-layouts  12.9 us (4%)
  other arithmetic  12.2 us (4%)
    all_to_all x7, waiting for transfers between devices, exchange(): return lax.all_to_all(value, axes, 0, 0, tiled=True)  81.9 us
    all_to_all x7, starting transfers between devices, exchange(): return lax.all_to_all(value, axes, 0, 0, tiled=True)  55.7 us
    all_gather x1, waiting for transfers between devices, body(): hidden = lax.all_gather(hidden, ('core', 'zlo'), axis=0, tiled=True)  41.4 us
    all_gather x1, blocking collectives, body(): table = lax.all_gather(table, GROUP + ('zhi',), axis=0, tiled=True)  41.1 us
    all_to_all x1, blocking collectives, exchange(): return lax.all_to_all(value, axes, 0, 0, tiled=True)  40.1 us
    dot_general x14, matrix products, dot(): return jnp.dot(a, b, preferred_element_type=F32)  24.7 us
  transfers between devices with their start and end apart: 10, of which 10 were waited for; matrix products, arithmetic and copies ran while one was open for 2% of the time, Pallas kernels for 0%

profile of v1, /device:TPU:32, one launch (start us, length us, event | category | flops | bytes accessed | tf_op | source)
XLA Modules:
  0.0 337.6 jit_solution(12725598926880659737)
XLA Ops:
  7.2 0.9 reshape.339
  8.2 0.2 convert_reduce_fusion.2
  8.6 1.1 copy.157
  9.7 2.1 convolution_convert_fusion.1
  11.8 6.1 %all-to-all-start = ((bf16[8,32,1152]{2,1,0:T(8,128)(2,1)}), bf16[8,32,1152]{2,1,0:T(8,128)(2,1)S(1)}, u32[]{:S(2)}, u32[]{:S(2)}) async-start(bf16[8,32,1152]{2,1,0:T(8,128)(2,1)} %bitcast.146), calls=%async_computation | async-start | bytes 1179648 | tf_op jit(solution)/shard_map/all_to_all | solution.py:35
  17.9 0.7 fusion.135
  18.7 1.7 fusion.132
  20.4 10.9 %all-to-all-done = bf16[8,32,1152]{2,1,0:T(8,128)(2,1)S(1)} async-done(((bf16[8,32,1152]{2,1,0:T(8,128)(2,1)}), bf16[8,32,1152]{2,1,0:T(8,128)(2,1)S(1)}, u32[]{:S(2)}, u32[]{:S(2)}) %all-to-all-start) | async-done | bytes 589856 | tf_op jit(solution)/shard_map/all_to_all | solution.py:35
  31.2 0.3 fusion.53
  31.6 0.3 fusion.57
  31.9 0.4 fusion.137
  32.3 0.8 copy-done.6
  33.1 0.2 fusion.61
  33.3 2.2 fusion.41
  35.5 0.3 fusion.136
  35.8 0.8 copy-done.7
  36.6 0.2 fusion.59
  36.8 2.2 fusion.40
  40.0 0.6 broadcast_in_dim.46
  40.7 1.8 concatenate.26
  42.5 6.9 %all-to-all-start.1 = ((bf16[8,32,384]{2,1,0:T(8,128)(2,1)}), bf16[8,32,384]{2,1,0:T(8,128)(2,1)S(1)}, u32[]{:S(2)}, u32[]{:S(2)}) async-start(bf16[8,32,384]{2,1,0:T(8,128)(2,1)} %concatenate.26), calls=%async_computation.1 | async-start | bytes 393216 | tf_op jit(solution)/shard_map/all_to_all | solution.py:35
  49.4 0.2 fusion.49
  49.9 6.2 %all-to-all-done.1 = bf16[8,32,384]{2,1,0:T(8,128)(2,1)S(1)} async-done(((bf16[8,32,384]{2,1,0:T(8,128)(2,1)}), bf16[8,32,384]{2,1,0:T(8,128)(2,1)S(1)}, u32[]{:S(2)}, u32[]{:S(2)}) %all-to-all-start.1) | async-done | bytes 196640 | tf_op jit(solution)/shard_map/all_to_all | solution.py:35
  56.1 0.3 fusion.79
  56.4 0.2 fusion.133
  57.2 1.1 fusion.38
  58.3 1.1 fusion.39
  59.5 5.0 %convolution_convert_fusion = bf16[256,7168]{1,0:T(8,128)(2,1)} fusion(bf16[256,7168]{1,0:T(8,128)(2,1)} %param.24, bf16[256,128]{1,0:T(8,128)(2,1)S(1)} %fusion.39, bf16[256,128]{1,0:T(8,128)(2,1)S(1)} %fusion.38), kind=kOutput, calls=%fused_computation | convolution fusion | flops 941621248 | bytes 7471104 | tf_op jit(solution)/shard_map/dot_general | solution.py:19
  64.5 7.2 %all-to-all-start.2 = ((bf16[16,16,7168]{2,1,0:T(8,128)(2,1)}), bf16[16,16,7168]{2,1,0:T(8,128)(2,1)}, u32[]{:S(2)}, u32[]{:S(2)}) async-start(bf16[16,16,7168]{2,1,0:T(8,128)(2,1)} %bitcast.129), calls=%async_computation.2 | async-start | bytes 7340032 | tf_op jit(solution)/shard_map/all_to_all | solution.py:35
  71.9 41.1 %all_gather.6 = f32[128,16]{1,0:T(8,128)S(1)} all-gather(f32[8,16]{1,0:T(8,128)S(1)} %pad_maximum_fusion.1), channel_id=1, replica_groups=mesh['zlo'=4,'core'=2,'x'=4,'y'=4,'zhi'=2] {'zlo','core','zhi'}, dimensions={0}, use_global_device_ids=true | all-gather | bytes 8704 | tf_op jit(solution)/shard_map/all_gather | solution.py:81
  112.9 7.2 %all-to-all-done.2 = bf16[16,16,7168]{2,1,0:T(8,128)(2,1)} async-done(((bf16[16,16,7168]{2,1,0:T(8,128)(2,1)}), bf16[16,16,7168]{2,1,0:T(8,128)(2,1)}, u32[]{:S(2)}, u32[]{:S(2)}) %all-to-all-start.2) | async-done | bytes 3670048 | tf_op jit(solution)/shard_map/all_to_all | solution.py:35
  120.2 2.6 convert_reduce_fusion
  122.9 4.8 %collective-permute-start = (bf16[2,8,7168]{2,1,0:T(8,128)(2,1)S(1)}, bf16[2,8,7168]{2,1,0:T(8,128)(2,1)S(1)}, u32[]{:S(2)}, u32[]{:S(2)}) collective-permute-start(bf16[2,8,7168]{2,1,0:T(8,128)(2,1)S(1)} %fusion.64), channel_id=1, source_target_pairs={{0,1},{1,0},{2,3},{3,2},{4,5},{5,4},{6,7},{7,6},{8,9},{9,8},{10,11... | collective-permute-start | bytes 688136 | tf_op jit(solution)/shard_map/ppermute | solution.py:147
  128.4 4.5 %collective-permute-done = bf16[2,8,7168]{2,1,0:T(8,128)(2,1)S(1)} collective-permute-done((bf16[2,8,7168]{2,1,0:T(8,128)(2,1)S(1)}, bf16[2,8,7168]{2,1,0:T(8,128)(2,1)S(1)}, u32[]{:S(2)}, u32[]{:S(2)}) %collective-permute-start) | collective-permute-done | bytes 229408 | tf_op jit(solution)/shard_map/ppermute | solution.py:147
  132.9 0.3 multiply_reduce_fusion
  133.4 0.7 copy.143
  134.1 12.0 %all-to-all-start.3 = ((bf16[8,16,896]{2,1,0:T(8,128)(2,1)}), bf16[8,16,896]{2,1,0:T(8,128)(2,1)S(1)}, u32[]{:S(2)}, u32[]{:S(2)}) async-start(bf16[8,16,896]{2,1,0:T(8,128)(2,1)} %copy.143), calls=%async_computation.3 | async-start | bytes 458752 | tf_op jit(solution)/shard_map/all_to_all | solution.py:35
  146.3 7.1 %all-to-all-done.3 = bf16[8,16,896]{2,1,0:T(8,128)(2,1)S(1)} async-done(((bf16[8,16,896]{2,1,0:T(8,128)(2,1)}), bf16[8,16,896]{2,1,0:T(8,128)(2,1)S(1)}, u32[]{:S(2)}, u32[]{:S(2)}) %all-to-all-start.3) | async-done | bytes 229408 | tf_op jit(solution)/shard_map/all_to_all | solution.py:35
  153.4 1.6 convolution_convert_fusion.2
  155.0 9.3 %all-to-all-start.4 = ((bf16[16,48,896]{2,1,0:T(8,128)(2,1)}), bf16[16,48,896]{2,1,0:T(8,128)(2,1)S(1)}, u32[]{:S(2)}, u32[]{:S(2)}) async-start(bf16[16,48,896]{2,1,0:T(8,128)(2,1)} %bitcast.28), calls=%async_computation.4 | async-start | bytes 2752512 | tf_op jit(solution)/shard_map/all_to_all | solution.py:35
  164.3 21.2 %all-to-all-done.4 = bf16[16,48,896]{2,1,0:T(8,128)(2,1)S(1)} async-done(((bf16[16,48,896]{2,1,0:T(8,128)(2,1)}), bf16[16,48,896]{2,1,0:T(8,128)(2,1)S(1)}, u32[]{:S(2)}, u32[]{:S(2)}) %all-to-all-start.4) | async-done | bytes 1376288 | tf_op jit(solution)/shard_map/all_to_all | solution.py:35
  185.5 1.0 fusion.16
  186.5 0.5 copy-done.18
  187.0 1.0 fusion.22
  188.0 1.3 pad_maximum_fusion
  189.2 1.0 fusion.13
  190.2 0.5 copy-done.19
  190.7 1.0 fusion.19
  191.7 1.3 collective-permute-done.1
  193.0 2.0 add_convert_fusion
  195.0 40.1 %all_to_all.74 = bf16[4,96,2048]{2,1,0:T(8,128)(2,1)S(1)} all-to-all(bf16[4,96,2048]{2,1,0:T(8,128)(2,1)S(1)} %bitcast.131), channel_id=1, replica_groups=mesh['zlo'=4,'core'=2,'x'=4,'y'=4,'zhi'=2] {'zlo'}, dimensions={0} | all-to-all | bytes 3145728 | tf_op jit(solution)/shard_map/all_to_all | solution.py:35
  235.1 0.3 convert_reduce_fusion.1
  235.4 0.8 fusion.66
  236.2 41.4 %all-gather.2.cloned.1.call-done = bf16[768,1024]{1,0:T(8,128)(2,1)} async-done(((bf16[96,1024]{1,0:T(8,128)(2,1)}), bf16[768,1024]{1,0:T(8,128)(2,1)}) %all-gather.2.cloned.1.call-update) | async-done | bytes 1572880 | tf_op jit(solution)/shard_map/all_gather | solution.py:173
  277.6 4.8 %fusion.10 = bf16[768,896]{1,0:T(8,128)(2,1)} fusion(bf16[768,1024]{1,0:T(8,128)(2,1)} %all-gather.2.cloned.1.call-done, bf16[1,1024,896]{2,1,0:T(8,128)(2,1)} %param.31), kind=kOutput, calls=%fused_computation.15 | convolution fusion | flops 1409974272 | bytes 4784128 | tf_op jit(solution)/shard_map/dot_general | solution.py:19
  282.4 6.8 %all-to-all-start.6 = ((bf16[16,48,896]{2,1,0:T(8,128)(2,1)}), bf16[16,48,896]{2,1,0:T(8,128)(2,1)S(1)}, u32[]{:S(2)}, u32[]{:S(2)}) async-start(bf16[16,48,896]{2,1,0:T(8,128)(2,1)} %bitcast.141), calls=%async_computation.6 | async-start | bytes 2752512 | tf_op jit(solution)/shard_map/all_to_all | solution.py:35
  289.4 0.8 convert_element_type.337
  290.2 20.4 %all-to-all-done.6 = bf16[16,48,896]{2,1,0:T(8,128)(2,1)S(1)} async-done(((bf16[16,48,896]{2,1,0:T(8,128)(2,1)}), bf16[16,48,896]{2,1,0:T(8,128)(2,1)S(1)}, u32[]{:S(2)}, u32[]{:S(2)}) %all-to-all-start.6) | async-done | bytes 1376288 | tf_op jit(solution)/shard_map/all_to_all | solution.py:35
  310.6 0.4 convolution_bitcast_fusion
  311.0 1.1 fusion.33
  312.1 7.4 %all-to-all-start.7 = ((bf16[16,8,896]{2,1,0:T(8,128)(2,1)}), bf16[16,8,896]{2,1,0:T(8,128)(2,1)S(1)}, u32[]{:S(2)}, u32[]{:S(2)}) async-start(bf16[16,8,896]{2,1,0:T(8,128)(2,1)} %fusion.33), calls=%async_computation.7 | async-start | bytes 458752 | tf_op jit(solution)/shard_map/all_to_all | solution.py:35
  319.5 1.7 fusion.101
  321.2 8.9 %all-to-all-done.7 = bf16[16,8,896]{2,1,0:T(8,128)(2,1)S(1)} async-done(((bf16[16,8,896]{2,1,0:T(8,128)(2,1)}), bf16[16,8,896]{2,1,0:T(8,128)(2,1)S(1)}, u32[]{:S(2)}, u32[]{:S(2)}) %all-to-all-start.7) | async-done | bytes 229408 | tf_op jit(solution)/shard_map/all_to_all | solution.py:35
  330.1 0.7 bitcast_reduce_fusion
  (90 shorter events, 3.6 us)
Async XLA Ops:
  7.2 178.3 %copy-start = (bf16[1,896,1024]{2,1,0:T(8,128)(2,1)S(1)}, bf16[1,896,1024]{2,1,0:T(8,128)(2,1)}, u32[]{:S(2)}) copy-start(bf16[1,896,1024]{2,1,0:T(8,128)(2,1)} %param.29) | copy-start | bytes 5505028
  8.6 9.4 %copy-start.9 = (bf16[256,128]{1,0:T(8,128)(2,1)S(1)}, bf16[256,128]{1,0:T(8,128)(2,1)}, u32[]{:S(2)}) copy-start(bf16[256,128]{1,0:T(8,128)(2,1)} %param.17) | copy-start | bytes 196612
  9.7 8.9 %copy-start.2 = (bf16[256,2,512]{2,1,0:T(2,128)(2,1)S(1)}, bf16[256,2,512]{2,1,0:T(2,128)(2,1)}, u32[]{:S(2)}) copy-start(bf16[256,2,512]{2,1,0:T(2,128)(2,1)} %param.16) | copy-start | bytes 1572868
  11.8 19.4 %copy-start.3 = (bf16[1,512,512]{2,1,0:T(8,128)(2,1)S(1)}, bf16[1,512,512]{2,1,0:T(8,128)(2,1)}, u32[]{:S(2)}) copy-start(bf16[1,512,512]{2,1,0:T(8,128)(2,1)} %param.20) | copy-start | bytes 1572868
  11.8 19.4 %all-to-all-start = ((bf16[8,32,1152]{2,1,0:T(8,128)(2,1)}), bf16[8,32,1152]{2,1,0:T(8,128)(2,1)S(1)}, u32[]{:S(2)}, u32[]{:S(2)}) async-start(bf16[8,32,1152]{2,1,0:T(8,128)(2,1)} %bitcast.146), calls=%async_computation | async-start | bytes 1179648 | tf_op jit(solution)/shard_map/all_to_all | solution.py:35
  20.4 11.5 %copy-start.12 = (bf16[1,64,512]{2,1,0:T(8,128)(2,1)S(1)}, bf16[1,64,512]{2,1,0:T(8,128)(2,1)}, u32[]{:S(2)}) copy-start(bf16[1,64,512]{2,1,0:T(8,128)(2,1)} %param.21) | copy-start | bytes 196612
  32.3 0.8 copy-start.6
  35.8 0.8 copy-start.7
  39.0 10.4 %copy-start.4 = (bf16[256,1,512]{2,1,0:T(2,128)(2,1)S(1)}, bf16[256,1,512]{2,1,0:T(2,128)(2,1)}, u32[]{:S(2)}) copy-start(bf16[256,1,512]{2,1,0:T(2,128)(2,1)} %get-tuple-element.12) | copy-start | bytes 786436
  39.0 10.4 %copy-start.5 = (bf16[256,1,512]{2,1,0:T(2,128)(2,1)S(1)}, bf16[256,1,512]{2,1,0:T(2,128)(2,1)}, u32[]{:S(2)}) copy-start(bf16[256,1,512]{2,1,0:T(2,128)(2,1)} %get-tuple-element.13) | copy-start | bytes 786436
  39.0 10.4 %copy-start.8 = (bf16[256,512]{1,0:T(8,128)(2,1)S(1)}, bf16[256,512]{1,0:T(8,128)(2,1)}, u32[]{:S(2)}) copy-start(bf16[256,512]{1,0:T(8,128)(2,1)} %param.18) | copy-start | bytes 786436
  42.5 7.2 %copy-start.11 = (bf16[256,64]{1,0:T(8,128)(2,1)S(1)}, bf16[256,64]{1,0:T(8,128)(2,1)}, u32[]{:S(2)}) copy-start(bf16[256,64]{1,0:T(8,128)(2,1)} %get-tuple-element.23) | copy-start | bytes 98308
  42.5 7.2 %copy-start.10 = (bf16[256,64]{1,0:T(8,128)(2,1)S(1)}, bf16[256,64]{1,0:T(8,128)(2,1)}, u32[]{:S(2)}) copy-start(bf16[256,64]{1,0:T(8,128)(2,1)} %get-tuple-element.22) | copy-start | bytes 98308
  42.5 7.4 %copy-start.14 = (bf16[256,64]{0,1:T(8,128)(2,1)S(1)}, bf16[256,64]{0,1:T(8,128)(2,1)}, u32[]{:S(2)}) copy-start(bf16[256,64]{0,1:T(8,128)(2,1)} %param.19) | copy-start | bytes 98308
  42.5 13.7 %all-to-all-start.1 = ((bf16[8,32,384]{2,1,0:T(8,128)(2,1)}), bf16[8,32,384]{2,1,0:T(8,128)(2,1)S(1)}, u32[]{:S(2)}, u32[]{:S(2)}) async-start(bf16[8,32,384]{2,1,0:T(8,128)(2,1)} %concatenate.26), calls=%async_computation.1 | async-start | bytes 393216 | tf_op jit(solution)/shard_map/all_to_all | solution.py:35
  64.5 7.2 %copy-start.13 = (bf16[8,7168]{1,0:T(8,128)(2,1)S(1)}, bf16[8,7168]{1,0:T(8,128)(2,1)}, u32[]{:S(2)}) copy-start(bf16[8,7168]{1,0:T(8,128)(2,1)} %param.25) | copy-start | bytes 344068
  64.5 7.3 %copy-start.17 = (s32[8,8]{1,0:T(8,128)S(1)}, s32[8,8]{1,0:T(8,128)}, u32[]{:S(2)}) copy-start(s32[8,8]{1,0:T(8,128)} %param.27) | copy-start | bytes 772
  64.5 7.3 %copy-start.16 = (f32[8,8]{1,0:T(8,128)S(1)}, f32[8,8]{1,0:T(8,128)}, u32[]{:S(2)}) copy-start(f32[8,8]{1,0:T(8,128)} %param.28) | copy-start | bytes 772
  64.5 55.7 %all-to-all-start.2 = ((bf16[16,16,7168]{2,1,0:T(8,128)(2,1)}), bf16[16,16,7168]{2,1,0:T(8,128)(2,1)}, u32[]{:S(2)}, u32[]{:S(2)}) async-start(bf16[16,16,7168]{2,1,0:T(8,128)(2,1)} %bitcast.129), calls=%async_computation.2 | async-start | bytes 7340032 | tf_op jit(solution)/shard_map/all_to_all | solution.py:35
  122.8 10.6 %copy-start.1 = (f32[16,7168]{1,0:T(8,128)}, f32[16,7168]{1,0:T(8,128)S(1)}, u32[]{:S(2)}) copy-start(f32[16,7168]{1,0:T(8,128)S(1)} %convert_reduce_fusion) | copy-start | bytes 1376260
  122.8 10.4 %copy-start.15 = (f32[7168]{0:T(1024)S(1)}, f32[7168]{0:T(1024)}, u32[]{:S(2)}) copy-start(f32[7168]{0:T(1024)} %param.26) | copy-start | bytes 86020
  122.9 10.0 %collective-permute-start = (bf16[2,8,7168]{2,1,0:T(8,128)(2,1)S(1)}, bf16[2,8,7168]{2,1,0:T(8,128)(2,1)S(1)}, u32[]{:S(2)}, u32[]{:S(2)}) collective-permute-start(bf16[2,8,7168]{2,1,0:T(8,128)(2,1)S(1)} %fusion.64), channel_id=1, source_target_pairs={{0,1},{1,0},{2,3},{3,2},{4,5},{5,4},{6,7},{7,6},{8,9},{9,8},{10,11... | collective-permute-start | bytes 688136 | tf_op jit(solution)/shard_map/ppermute | solution.py:147
  134.1 19.2 %all-to-all-start.3 = ((bf16[8,16,896]{2,1,0:T(8,128)(2,1)}), bf16[8,16,896]{2,1,0:T(8,128)(2,1)S(1)}, u32[]{:S(2)}, u32[]{:S(2)}) async-start(bf16[8,16,896]{2,1,0:T(8,128)(2,1)} %copy.143), calls=%async_computation.3 | async-start | bytes 458752 | tf_op jit(solution)/shard_map/all_to_all | solution.py:35
  155.0 30.5 %all-to-all-start.4 = ((bf16[16,48,896]{2,1,0:T(8,128)(2,1)}), bf16[16,48,896]{2,1,0:T(8,128)(2,1)S(1)}, u32[]{:S(2)}, u32[]{:S(2)}) async-start(bf16[16,48,896]{2,1,0:T(8,128)(2,1)} %bitcast.28), calls=%async_computation.4 | async-start | bytes 2752512 | tf_op jit(solution)/shard_map/all_to_all | solution.py:35
  164.3 113.3 %all-gather.2.cloned.1.call-start = ((), (), s32[]{:S(2)}) async-start(), calls=%async_computation.8 | async-start | bytes 1769472 | tf_op jit(solution)/shard_map/all_gather | solution.py:173
  185.5 1.5 copy-start.18
  189.2 3.8 %collective-permute-start.1 = (bf16[384,2048]{1,0:T(8,128)(2,1)}, bf16[384,2048]{1,0:T(8,128)(2,1)}, u32[]{:S(2)}, u32[]{:S(2)}) collective-permute-start(bf16[384,2048]{1,0:T(8,128)(2,1)} %pad_maximum_fusion), channel_id=1, source_target_pairs={{0,32},{32,0},{1,33},{33,1},{2,34},{34,2},{3,35},{35,3},{4,36},{36... | collective-permute-start | bytes 4718600 | tf_op jit(solution)/shard_map/ppermute | solution.py:166
  189.2 1.5 copy-start.19
  282.4 28.1 %all-to-all-start.6 = ((bf16[16,48,896]{2,1,0:T(8,128)(2,1)}), bf16[16,48,896]{2,1,0:T(8,128)(2,1)S(1)}, u32[]{:S(2)}, u32[]{:S(2)}) async-start(bf16[16,48,896]{2,1,0:T(8,128)(2,1)} %bitcast.141), calls=%async_computation.6 | async-start | bytes 2752512 | tf_op jit(solution)/shard_map/all_to_all | solution.py:35
  312.1 18.0 %all-to-all-start.7 = ((bf16[16,8,896]{2,1,0:T(8,128)(2,1)}), bf16[16,8,896]{2,1,0:T(8,128)(2,1)S(1)}, u32[]{:S(2)}, u32[]{:S(2)}) async-start(bf16[16,8,896]{2,1,0:T(8,128)(2,1)} %fusion.33), calls=%async_computation.7 | async-start | bytes 458752 | tf_op jit(solution)/shard_map/all_to_all | solution.py:35
Sparse Core Ops, SparseCore 0:
  236.3 41.2 all-gather.1

commit v2 on v1

v2 whole, which is shorter than its diff:
```python
import jax
import jax.numpy as jnp
from jax import lax
from jax.sharding import Mesh, PartitionSpec as P

ROPE = 64
VD = 128
NORM_EPS = 1e-06
RUNS = 4
CAP = 3
ROWS = 8
CHUNKS = 1
GATHER = "sc"

GROUP = ("zlo", "core")
XY = ("x", "y")
BF = jnp.bfloat16
F32 = jnp.float32


def dot(a, b):
    return jnp.dot(a, b, preferred_element_type=F32)


def dot_t(a, b):
    return lax.dot_general(a, b, (((1,), (1,)), ((), ())), preferred_element_type=F32)


def split3(value):
    one = value.astype(BF)
    rest = value - one.astype(F32)
    two = rest.astype(BF)
    three = (rest - two.astype(F32)).astype(BF)
    return one, two, three


def exchange(value, axes):
    return lax.all_to_all(value, axes, 0, 0, tiled=True)


def block_permutation(prompt_of_sample, prompts):
    samples = prompt_of_sample.shape[0]
    block = samples // (prompts * RUNS)
    own = prompt_of_sample.reshape(-1, block)[:, 0]
    blocks = own.shape[0]
    at = jnp.arange(blocks, dtype=jnp.int32)
    same = (own[:, None] == own[None, :]) & (at[None, :] < at[:, None])
    rank = own * RUNS + jnp.sum(same.astype(jnp.int32), axis=1)
    rank_of_sample = jnp.repeat(rank, block) * block + jnp.arange(samples, dtype=jnp.int32) % block
    return rank_of_sample


SIDE = 4
LINES = 4
CORES = 2
HALVES = 2
ALL = ("zlo", "core", "x", "y", "zhi")


def shift(count, k):
    return [(i, (i + k) % count) for i in range(count)]


def sum_wide(parts):
    total = parts[0].astype(F32)
    for part in parts[1:]:
        total = total + part.astype(F32)
    return total


def plane_shift(k, stage):
    pairs = []
    sizes = (LINES, CORES, SIDE, SIDE, HALVES)

    def number(place):
        flat = 0
        for size, one in zip(sizes, place):
            flat = flat * size + one
        return flat

    for flat in range(LINES * CORES * SIDE * SIDE * HALVES):
        place, rest = [], flat
        for size in reversed(sizes):
            place.insert(0, rest % size)
            rest //= size
        there = list(place)
        axis = 2 if place[1] == stage else 3
        there[axis] = (there[axis] + k) % SIDE
        pairs.append((number(place), number(there)))
    return pairs


def plane_order(my_core):
    me = (lax.axis_index("x"), lax.axis_index("y"))
    count = SIDE * SIDE * HALVES * ROWS
    row = jnp.arange(count, dtype=jnp.int32)
    rest = row % (HALVES * ROWS)
    first = row // (HALVES * ROWS) // SIDE
    second = row // (HALVES * ROWS) % SIDE
    x = (me[0] + jnp.where(my_core == 0, first, second)) % SIDE
    y = (me[1] + jnp.where(my_core == 0, second, first)) % SIDE
    source = (x * SIDE + y) * (HALVES * ROWS) + rest
    return (source[:, None] == row[None, :]).astype(BF)


def body(
    q_latent,
    q_rope,
    self_latent,
    self_rope,
    cache_latent,
    cache_rope,
    prompt_of_sample,
    w_uv,
    w_out,
    residual,
    norm_gain,
    expert_ids,
    gate_weight,
    w_gate,
    w_up,
    w_down,
):
    groups = lax.axis_size(GROUP)
    halves = lax.axis_size("zhi")
    planes = lax.axis_size(XY)
    my_half = lax.axis_index("zhi")
    my_core = lax.axis_index("core")
    samples, heads, lat = q_latent.shape
    experts = planes * halves
    rows_here = residual.shape[0]
    width = residual.shape[1]
    share = width // groups
    scale = (VD + ROPE) ** (-0.5)

    top = expert_ids.shape[1]
    tokens = groups * halves * rows_here
    own_table = jnp.concatenate([expert_ids.astype(BF), *split3(gate_weight)], axis=1)
    other_table = lax.ppermute(own_table, "zhi", [(0, 1), (1, 0)])
    table = jnp.concatenate(
        [
            jnp.where(my_half == 0, own_table, other_table),
            jnp.where(my_half == 0, other_table, own_table),
        ],
        axis=0,
    )

    rank = block_permutation(prompt_of_sample, groups)
    to_rank = (rank[None, :] == jnp.arange(samples, dtype=jnp.int32)[:, None]).astype(BF)
    q_all = jnp.concatenate([q_latent.reshape(samples, heads * lat), q_rope], axis=1)
    q_sorted = dot(to_rank, q_all).astype(BF)
    q_here = exchange(q_sorted, GROUP)
    keys = cache_latent[0]
    rope_keys = cache_rope[0]
    outs = []
    stats = []
    for head in range(heads):
        q_head = q_here[:, head * lat : (head + 1) * lat]
        r_head = q_here[:, heads * lat + head * ROPE : heads * lat + (head + 1) * ROPE]
        score = (dot_t(q_head, keys) + dot(r_head, rope_keys)) * scale
        best = jnp.max(score, axis=-1, keepdims=True)
        weight = jnp.exp(score - best)
        total = jnp.sum(weight, axis=-1, keepdims=True)
        latent = (dot(weight.astype(BF), keys) / total).astype(BF)
        outs.append(dot(latent, w_uv[head]).astype(BF))
        stats.extend(split3(best + jnp.log(total)))
    pad = jnp.zeros((samples, VD - len(stats) - table.shape[1]), BF)
    table = jnp.pad(table, ((0, samples // groups - table.shape[0]), (0, 0)))
    table = jnp.tile(table, (groups, 1))
    back = exchange(jnp.concatenate(outs + stats + [table, pad], axis=1), GROUP)

    table = back.reshape(groups, samples // groups, -1)[:, : halves * rows_here]
    table = table[:, :, heads * VD + len(stats) :].reshape(tokens, -1).astype(F32)
    ids = table[:, :top].astype(jnp.int32)
    gates = table[:, top : 2 * top] + table[:, 2 * top : 3 * top] + table[:, 3 * top : 4 * top]
    wanted = jnp.arange(planes, dtype=jnp.int32) * halves + my_half
    slots = tokens // rows_here * CAP // CHUNKS
    tables = []
    for chunk in range(CHUNKS):
        some_ids = ids.reshape(groups, CHUNKS, -1, top)[:, chunk].reshape(-1, top)
        some_gates = gates.reshape(groups, CHUNKS, -1, top)[:, chunk].reshape(-1, top)
        hit = some_ids[:, :, None] == wanted[None, None, :]
        member = jnp.any(hit, axis=1)
        gate_of = jnp.sum(jnp.where(hit, some_gates[:, :, None], 0.0), axis=1)
        before = jnp.cumsum(member.astype(jnp.int32), axis=0) - member.astype(jnp.int32)
        place = jnp.where(member, before, -1).T
        routed = place[:, None, :] == jnp.arange(slots, dtype=jnp.int32)[None, :, None]
        routed = routed.reshape(planes * slots, -1)
        weights = jnp.where(routed, jnp.repeat(gate_of.T, slots, axis=0), 0.0)
        gate_hi = weights.astype(BF)
        tables.append((routed.astype(BF), gate_hi, (weights - gate_hi.astype(F32)).astype(BF)))

    back = lax.dot_general(to_rank, back, (((0,), (0,)), ((), ())), preferred_element_type=F32)
    values = []
    self_wide = self_latent.astype(F32)
    for head in range(heads):
        self_score = (
            jnp.sum(q_latent[:, head].astype(F32) * self_wide, axis=-1, keepdims=True)
            + jnp.sum(
                q_rope[:, head * ROPE : (head + 1) * ROPE].astype(F32) * self_rope.astype(F32),
                axis=-1,
                keepdims=True,
            )
        ) * scale
        at = heads * VD + 3 * head
        lse = back[:, at : at + 1] + back[:, at + 1 : at + 2] + back[:, at + 2 : at + 3]
        best = jnp.maximum(lse, self_score)
        cache_part = jnp.exp(lse - best)
        self_part = jnp.exp(self_score - best)
        own_value = dot(self_latent, w_uv[head])
        mixed_value = cache_part * back[:, head * VD : (head + 1) * VD] + self_part * own_value
        values.append((mixed_value / (cache_part + self_part)).astype(BF))
    head_value = jnp.concatenate(values, axis=1)

    head_rows = dot(plane_order(my_core), head_value).astype(BF)
    near = [None] * CHUNKS
    block = halves * rows_here // CHUNKS
    for chunk in range(CHUNKS):
        rows = head_rows.reshape(SIDE, SIDE, CHUNKS, block, -1)[:, :, chunk]
        first = [dot(rows[k].reshape(SIDE * block, -1), w_out).astype(BF) for k in range(SIDE)]
        first = sum_wide(first[:1] + [lax.ppermute(first[k], ALL, plane_shift(k, 0)) for k in (2, 1, 3)])
        first = first.astype(BF).reshape(SIDE, block, width)
        near[chunk] = sum_wide(
            [first[0]] + [lax.ppermute(first[k], ALL, plane_shift(k, 1)) for k in (2, 1, 3)]
        )

    moes = []
    projections = []
    for chunk in range(CHUNKS):
        part = near[chunk].reshape(halves // CHUNKS, rows_here, width)
        is_mine = (jnp.arange(halves // CHUNKS) + chunk * (halves // CHUNKS) == my_half)[:, None, None]
        with_residual = part + jnp.where(is_mine, residual.astype(F32)[None], 0.0)
        far = lax.ppermute(with_residual.astype(BF), "zhi", [(0, 1), (1, 0)]).astype(F32)
        projections.append(part + far)
        mixed = with_residual + far
        normed = (
            mixed * lax.rsqrt(jnp.mean(mixed * mixed, axis=-1, keepdims=True) + NORM_EPS) * norm_gain
        ).astype(BF)

        by_block = normed.reshape(block, groups, share).transpose(1, 0, 2)
        token_rows = exchange(by_block, GROUP).reshape(tokens // CHUNKS, share)
        routing, gate_hi, gate_lo = tables[chunk]
        rows_in = exchange(dot(routing, token_rows).astype(BF), XY)

        half_rows = rows_in.shape[0] // 2

        def both(rows):
            return jnp.concatenate([dot(rows, w_gate[0]).astype(BF), dot(rows, w_up[0]).astype(BF)], axis=1)

        other_rows = lax.dynamic_slice_in_dim(rows_in, (1 - my_core) * half_rows, half_rows, 0)
        own_rows = lax.dynamic_slice_in_dim(rows_in, my_core * half_rows, half_rows, 0)
        from_core = lax.ppermute(both(other_rows), "core", [(0, 1), (1, 0)])
        own = both(own_rows)
        lines = lax.axis_size("zlo")
        line_rows = half_rows // lines
        my_line = lax.axis_index("zlo")
        parts = []
        for k in (2, 1, 3, 0):
            at = (my_line + k) % lines * line_rows
            here = lax.dynamic_slice_in_dim(own, at, line_rows, 0).astype(F32)
            here = here + lax.dynamic_slice_in_dim(from_core, at, line_rows, 0).astype(F32)
            parts.append(lax.ppermute(here.astype(BF), "zlo", shift(lines, k)) if k else here)
        sums = sum_wide(parts)
        ffe = sums.shape[1] // 2
        hidden = (jax.nn.silu(sums[:, :ffe]) * sums[:, ffe:]).astype(BF)
        if GATHER == "sc":
            mine = lax.all_gather(hidden, "zlo", axis=0, tiled=True)
        else:
            got = [hidden] + [lax.ppermute(hidden, "zlo", shift(lines, k)) for k in (1, 2, 3)]
            mine = jnp.concatenate(got, axis=0)
        theirs = lax.ppermute(mine, "core", [(0, 1), (1, 0)])
        down = [dot(mine, w_down[0]).astype(BF), dot(theirs, w_down[0]).astype(BF)]
        if GATHER == "sc":
            order = [jnp.where(my_core == 0, down[0], down[1]), jnp.where(my_core == 0, down[1], down[0])]
            expert_out = jnp.concatenate(order, axis=0)
        else:
            expert_out = jnp.zeros((2 * half_rows, share), BF)
            for side in range(2):
                base = (my_core if side == 0 else 1 - my_core) * half_rows
                for k in range(lines):
                    at = base + (my_line - k) % lines * line_rows
                    expert_out = lax.dynamic_update_slice_in_dim(
                        expert_out, down[side][k * line_rows : (k + 1) * line_rows], at, 0
                    )

        returned = exchange(expert_out, XY)
        over_rows = (((0,), (0,)), ((), ()))
        moe = lax.dot_general(gate_hi, returned, over_rows, preferred_element_type=F32)
        moe = moe + lax.dot_general(gate_lo, returned, over_rows, preferred_element_type=F32)
        moes.append(moe.astype(BF).reshape(groups, block, share))
    attn_proj = jnp.concatenate(projections, axis=0)
    attn_proj = lax.dynamic_index_in_dim(attn_proj, my_half, 0, keepdims=False).astype(BF)
    moe = jnp.concatenate(moes, axis=1).reshape(tokens, share)
    moe = exchange(moe, GROUP + ("zhi",))
    moe = jnp.sum(moe.reshape(groups, halves, rows_here, share).astype(F32), axis=1).astype(BF)
    moe_out = moe.transpose(1, 0, 2).reshape(rows_here, width)
    return (attn_proj, moe_out)


def solution(mesh):
    fine = Mesh(mesh.devices.reshape(4, 2, 4, 4, 2), ("zlo", "core", "x", "y", "zhi"))
    g = GROUP
    e = XY + ("zhi",)
    in_specs = (
        P(g, e, None),
        P(g, e),
        P(g, None),
        P(g, None),
        P(g, None, None),
        P(g, None, None),
        P(g),
        P(e, None, None),
        P(e, None),
        P(g + e, None),
        P(),
        P(g + e, None),
        P(g + e, None),
        P(e, g, None),
        P(e, g, None),
        P(e, None, g),
    )
    out_specs = (P(g + e, None), P(g + e, None))
    return jax.shard_map(body, mesh=fine, in_specs=in_specs, out_specs=out_specs, check_vma=False)
```

time: 340 us -> 273 us (0.80)
  blocking collectives: 81.2 us -> 15.9 us
  between operations: 14.4 us -> 1.29 us
  waiting for transfers between devices: 129 us -> 137 us
    ppermute x0 -> x11, waiting for transfers between devices: none -> 62.9 us  [the longest x3 33.9 us: body(): lax.ppermute(here.astype(BF), 'zlo', shift(lines, k))]
    all_gather x1 -> x0, waiting for transfers between devices: 41.4 us -> none  [body(): hidden = lax.all_gather(hidden, ('core', 'zlo'), axis=0, tiled=True)]
    all_to_all x1 -> x0, blocking collectives: 40.1 us -> none  [exchange(): return lax.all_to_all(value, axes, 0, 0, tiled=True)]
    all_gather x1, blocking collectives: 41.1 us -> 15.9 us  [body(): mine = lax.all_gather(hidden, 'zlo', axis=0, tiled=True)]
    ppermute x0 -> x11, starting transfers between devices: none -> 20.6 us  [the longest x3 6.34 us: body(): lax.ppermute(first[k], ALL, plane_shift(k, 0))]
    all_to_all x7 -> x6, starting transfers between devices: 55.7 us -> 35.6 us  [exchange(): return lax.all_to_all(value, axes, 0, 0, tiled=True)]
    all_to_all x7 -> x6, waiting for transfers between devices: 81.9 us -> 66.4 us  [exchange(): return lax.all_to_all(value, axes, 0, 0, tiled=True)]
    dot_general x14 -> x19, matrix products: 24.7 us -> 27 us  [dot(): return jnp.dot(a, b, preferred_element_type=F32)]
  transfers between devices with their start and end apart: 10 -> 19, of which waited for: 10 -> 18; matrix products, arithmetic and copies ran while one was open for 2% -> 5% of each run, Pallas kernels for 0% -> 0%
where the time goes in v2:
time: 273 us; the launch traced here: 271 us
  waiting for transfers between devices  137 us (50%)
  starting transfers between devices  60.4 us (22%)
  matrix products  29.4 us (11%)
  blocking collectives  15.9 us (6%)
  other arithmetic  14.2 us (5%)
  local copies, waits for them, and re-layouts  12.4 us (5%)
    all_to_all x6, waiting for transfers between devices, exchange(): return lax.all_to_all(value, axes, 0, 0, tiled=True)  66.4 us
    all_to_all x6, starting transfers between devices, exchange(): return lax.all_to_all(value, axes, 0, 0, tiled=True)  35.6 us
    ppermute x3, waiting for transfers between devices, body(): lax.ppermute(here.astype(BF), 'zlo', shift(lines, k))  33.9 us
    dot_general x19, matrix products, dot(): return jnp.dot(a, b, preferred_element_type=F32)  27 us
    ppermute x3, waiting for transfers between devices, body(): lax.ppermute(first[k], ALL, plane_shift(k, 0))  18.6 us
    all_gather x1, blocking collectives, body(): mine = lax.all_gather(hidden, 'zlo', axis=0, tiled=True)  15.9 us
    ppermute x1, waiting for transfers between devices, body(): lax.ppermute(with_residual.astype(BF), 'zhi', [(0, 1), (1, 0)]).astype(F32)  7.81 us
    ppermute x3, starting transfers between devices, body(): lax.ppermute(first[k], ALL, plane_shift(k, 0))  6.34 us
  transfers between devices with their start and end apart: 19, of which 18 were waited for; matrix products, arithmetic and copies ran while one was open for 5% of the time, Pallas kernels for 0%

profile of v2, /device:TPU:32, one launch (start us, length us, event | category | flops | bytes accessed | tf_op | source)
XLA Modules:
  0.0 270.7 jit_solution(6736504287901900951)
XLA Ops:
  0.7 0.9 reshape.431
  2.1 1.1 copy.140
  3.2 2.0 convolution_convert_fusion.4
  5.2 6.0 %all-to-all-start = ((bf16[8,32,1152]{2,1,0:T(8,128)(2,1)}), bf16[8,32,1152]{2,1,0:T(8,128)(2,1)S(1)}, u32[]{:S(2)}, u32[]{:S(2)}) async-start(bf16[8,32,1152]{2,1,0:T(8,128)(2,1)} %bitcast), calls=%async_computation | async-start | bytes 1179648 | tf_op jit(solution)/shard_map/all_to_all | solution.py:38
  11.4 4.8 %collective-permute-start = (bf16[8,32]{1,0:T(8,128)(2,1)S(1)}, bf16[8,32]{1,0:T(8,128)(2,1)S(1)}, u32[]{:S(2)}, u32[]{:S(2)}) collective-permute-start(bf16[8,32]{1,0:T(8,128)(2,1)S(1)} %pad_maximum_fusion.2), channel_id=1, source_target_pairs={{0,1},{1,0},{2,3},{3,2},{4,5},{5,4},{6,7},{7,6},{8,9},{9,8},{10,11... | collective-permute-start | bytes 1544 | tf_op jit(solution)/shard_map/ppermute | solution.py:139
  16.9 1.8 fusion.55
  19.3 2.0 collective-permute-done
  21.4 3.2 %all-to-all-done = bf16[8,32,1152]{2,1,0:T(8,128)(2,1)S(1)} async-done(((bf16[8,32,1152]{2,1,0:T(8,128)(2,1)}), bf16[8,32,1152]{2,1,0:T(8,128)(2,1)S(1)}, u32[]{:S(2)}, u32[]{:S(2)}) %all-to-all-start) | async-done | bytes 589856 | tf_op jit(solution)/shard_map/all_to_all | solution.py:38
  25.3 1.2 fusion.167
  26.5 0.8 copy-done.5
  28.1 2.2 fusion.47
  30.7 0.8 copy-done.6
  31.7 1.6 fusion.46
  34.5 0.9 concatenate.34
  35.4 7.6 %all-to-all-start.1 = ((bf16[8,32,384]{2,1,0:T(8,128)(2,1)}), bf16[8,32,384]{2,1,0:T(8,128)(2,1)S(1)}, u32[]{:S(2)}, u32[]{:S(2)}) async-start(bf16[8,32,384]{2,1,0:T(8,128)(2,1)} %concatenate.34), calls=%async_computation.1 | async-start | bytes 393216 | tf_op jit(solution)/shard_map/all_to_all | solution.py:38
  43.3 6.4 %all-to-all-done.1 = bf16[8,32,384]{2,1,0:T(8,128)(2,1)S(1)} async-done(((bf16[8,32,384]{2,1,0:T(8,128)(2,1)}), bf16[8,32,384]{2,1,0:T(8,128)(2,1)S(1)}, u32[]{:S(2)}, u32[]{:S(2)}) %all-to-all-start.1) | async-done | bytes 196640 | tf_op jit(solution)/shard_map/all_to_all | solution.py:38
  50.8 1.1 fusion.44
  52.0 1.1 fusion.45
  53.3 2.9 %convolution_convert_fusion = bf16[64,7168]{1,0:T(8,128)(2,1)S(1)} fusion(bf16[256,7168]{1,0:T(8,128)(2,1)} %param.24, bf16[256,256]{1,0:T(8,128)(2,1)S(1)} %convolution_convert_fusion.6), kind=kOutput, calls=%fused_computation | convolution fusion | flops 235339776 | bytes 4620288 | tf_op jit(solution)/shard_map/dot_general | solution.py:22
  58.0 3.1 %collective-permute-start.1 = (bf16[64,7168]{1,0:T(8,128)(2,1)S(1)}, bf16[64,7168]{1,0:T(8,128)(2,1)S(1)}, u32[]{:S(2)}, u32[]{:S(2)}) collective-permute-start(bf16[64,7168]{1,0:T(8,128)(2,1)S(1)} %convolution_convert_fusion.2), channel_id=1, source_target_pairs={{0,16},{1,17},{2,18},{3,19},{4,20},{5,21},{6,22},{7,23},{8,24},{9,... | collective-permute-start | bytes 2752520 | tf_op jit(solution)/shard_map/ppermute | solution.py:221
  61.7 2.6 collective-permute-start.3
  64.4 8.7 %collective-permute-done.1 = bf16[64,7168]{1,0:T(8,128)(2,1)S(1)} collective-permute-done((bf16[64,7168]{1,0:T(8,128)(2,1)S(1)}, bf16[64,7168]{1,0:T(8,128)(2,1)S(1)}, u32[]{:S(2)}, u32[]{:S(2)}) %collective-permute-start.1) | collective-permute-done | bytes 917536 | tf_op jit(solution)/shard_map/ppermute | solution.py:221
  73.1 9.7 %collective-permute-done.2 = bf16[64,7168]{1,0:T(8,128)(2,1)S(1)} collective-permute-done((bf16[64,7168]{1,0:T(8,128)(2,1)S(1)}, bf16[64,7168]{1,0:T(8,128)(2,1)S(1)}, u32[]{:S(2)}, u32[]{:S(2)}) %collective-permute-start.2) | collective-permute-done | bytes 917536 | tf_op jit(solution)/shard_map/ppermute | solution.py:221
  82.9 1.3 add_convert_fusion
  84.3 3.3 %collective-permute-start.4 = (bf16[16,7168]{1,0:T(8,128)(2,1)S(1)}, bf16[16,7168]{1,0:T(8,128)(2,1)S(1)}, u32[]{:S(2)}, u32[]{:S(2)}) collective-permute-start(bf16[16,7168]{1,0:T(8,128)(2,1)S(1)} %get-tuple-element.19), channel_id=1, source_target_pairs={{0,4},{1,5},{2,6},{3,7},{4,0},{5,1},{6,2},{7,3},{8,12},{9,13},{10,... | collective-permute-start | bytes 688136 | tf_op jit(solution)/shard_map/ppermute | solution.py:224
  87.6 1.1 collective-permute-start.6
  88.6 1.0 collective-permute-start.5
  89.7 2.2 collective-permute-done.4
  91.9 2.8 %collective-permute-done.6 = bf16[16,7168]{1,0:T(8,128)(2,1)S(1)} collective-permute-done((bf16[16,7168]{1,0:T(8,128)(2,1)S(1)}, bf16[16,7168]{1,0:T(8,128)(2,1)S(1)}, u32[]{:S(2)}, u32[]{:S(2)}) %collective-permute-start.6) | collective-permute-done | bytes 229408 | tf_op jit(solution)/shard_map/ppermute | solution.py:224
  94.7 1.2 collective-permute-done.5
  96.0 4.2 %collective-permute-start.7 = (bf16[2,8,7168]{2,1,0:T(8,128)(2,1)S(1)}, bf16[2,8,7168]{2,1,0:T(8,128)(2,1)S(1)}, u32[]{:S(2)}, u32[]{:S(2)}) collective-permute-start(bf16[2,8,7168]{2,1,0:T(8,128)(2,1)S(1)} %get-tuple-element.6), channel_id=1, source_target_pairs={{0,1},{1,0},{2,3},{3,2},{4,5},{5,4},{6,7},{7,6},{8,9},{9,8},{10,11... | collective-permute-start | bytes 688136 | tf_op jit(solution)/shard_map/ppermute | solution.py:233
  101.5 7.8 %collective-permute-done.7 = bf16[2,8,7168]{2,1,0:T(8,128)(2,1)S(1)} collective-permute-done((bf16[2,8,7168]{2,1,0:T(8,128)(2,1)S(1)}, bf16[2,8,7168]{2,1,0:T(8,128)(2,1)S(1)}, u32[]{:S(2)}, u32[]{:S(2)}) %collective-permute-start.7) | collective-permute-done | bytes 229408 | tf_op jit(solution)/shard_map/ppermute | solution.py:233
  110.6 5.3 %all-to-all-start.2 = ((bf16[8,16,896]{2,1,0:T(8,128)(2,1)}), bf16[8,16,896]{2,1,0:T(8,128)(2,1)S(1)}, u32[]{:S(2)}, u32[]{:S(2)}) async-start(bf16[8,16,896]{2,1,0:T(8,128)(2,1)} %copy.123), calls=%async_computation.2 | async-start | bytes 458752 | tf_op jit(solution)/shard_map/all_to_all | solution.py:38
  116.0 7.1 %all-to-all-done.2 = bf16[8,16,896]{2,1,0:T(8,128)(2,1)S(1)} async-done(((bf16[8,16,896]{2,1,0:T(8,128)(2,1)}), bf16[8,16,896]{2,1,0:T(8,128)(2,1)S(1)}, u32[]{:S(2)}, u32[]{:S(2)}) %all-to-all-start.2) | async-done | bytes 229408 | tf_op jit(solution)/shard_map/all_to_all | solution.py:38
  123.1 1.6 convolution_convert_fusion.5
  124.7 5.3 %all-to-all-start.3 = ((bf16[16,48,896]{2,1,0:T(8,128)(2,1)}), bf16[16,48,896]{2,1,0:T(8,128)(2,1)S(1)}, u32[]{:S(2)}, u32[]{:S(2)}) async-start(bf16[16,48,896]{2,1,0:T(8,128)(2,1)} %bitcast.29), calls=%async_computation.3 | async-start | bytes 2752512 | tf_op jit(solution)/shard_map/all_to_all | solution.py:38
  130.0 21.2 %all-to-all-done.3 = bf16[16,48,896]{2,1,0:T(8,128)(2,1)S(1)} async-done(((bf16[16,48,896]{2,1,0:T(8,128)(2,1)}), bf16[16,48,896]{2,1,0:T(8,128)(2,1)S(1)}, u32[]{:S(2)}, u32[]{:S(2)}) %all-to-all-start.3) | async-done | bytes 1376288 | tf_op jit(solution)/shard_map/all_to_all | solution.py:38
  151.2 3.0 %fusion.22 = bf16[384,1024]{1,0:T(8,128)(2,1)S(1)} fusion(bf16[1,896,1024]{2,1,0:T(8,128)(2,1)} %param.30, bf16[768,896]{1,0:T(8,128)(2,1)S(1)} %bitcast.145, s32[]{:T(128)S(6)} %select_n.199), kind=kOutput, calls=%fused_computation.32 | convolution fusion | flops 705036288 | bytes 3309572 | tf_op jit(solution)/shard_map/dot_general | solution.py:22
  154.3 1.0 fusion.16
  155.3 1.2 pad_maximum_fusion
  156.5 2.8 %fusion.19 = bf16[384,1024]{1,0:T(8,128)(2,1)S(1)} fusion(bf16[1,896,1024]{2,1,0:T(8,128)(2,1)} %param.30, bf16[768,896]{1,0:T(8,128)(2,1)} %bitcast.147, s32[]{:T(128)S(6)} %select_n.196), kind=kOutput, calls=%fused_computation.31 | convolution fusion | flops 705036288 | bytes 3309572 | tf_op jit(solution)/shard_map/dot_general | solution.py:22
  159.4 1.0 fusion.13
  160.4 2.5 add_convert_fusion.3
  162.9 2.1 collective-permute-start.9
  165.0 1.1 collective-permute-start.10
  166.1 0.9 collective-permute-start.11
  167.0 15.2 %collective-permute-done.9 = bf16[96,2048]{1,0:T(8,128)(2,1)} collective-permute-done((bf16[96,2048]{1,0:T(8,128)(2,1)}, bf16[96,2048]{1,0:T(8,128)(2,1)}, u32[]{:S(2)}, u32[]{:S(2)}) %collective-permute-start.9) | collective-permute-done | bytes 393248 | tf_op jit(solution)/shard_map/ppermute | solution.py:262
  182.3 16.8 %collective-permute-done.10 = bf16[96,2048]{1,0:T(8,128)(2,1)} collective-permute-done((bf16[96,2048]{1,0:T(8,128)(2,1)}, bf16[96,2048]{1,0:T(8,128)(2,1)}, u32[]{:S(2)}, u32[]{:S(2)}) %collective-permute-start.10) | collective-permute-done | bytes 393248 | tf_op jit(solution)/shard_map/ppermute | solution.py:262
  199.1 1.9 collective-permute-done.11
  200.9 1.6 add_add_fusion
  202.7 15.9 %all_gather.3 = bf16[384,1024]{1,0:T(8,128)(2,1)S(1)} all-gather(bf16[96,1024]{1,0:T(8,128)(2,1)S(1)} %fusion.76), channel_id=1, replica_groups=mesh['zlo'=4,'core'=2,'x'=4,'y'=4,'zhi'=2] {'zlo'}, dimensions={0}, use_global_device_ids=true | all-gather | bytes 983040 | tf_op jit(solution)/shard_map/all_gather | solution.py:267
  218.6 2.3 collective-permute-done.12
  220.9 1.0 fusion.28
  221.9 1.0 broadcast_select_fusion.1
  222.9 1.2 pad_maximum_fusion.1
  224.1 3.8 %all-to-all-start.4 = ((bf16[16,48,896]{2,1,0:T(8,128)(2,1)}), bf16[16,48,896]{2,1,0:T(8,128)(2,1)S(1)}, u32[]{:S(2)}, u32[]{:S(2)}) async-start(bf16[16,48,896]{2,1,0:T(8,128)(2,1)} %bitcast.139), calls=%async_computation.4 | async-start | bytes 2752512 | tf_op jit(solution)/shard_map/all_to_all | solution.py:38
  228.0 0.9 copy.138
  228.8 0.9 copy.137
  229.9 0.8 convert_element_type.448
  230.8 19.5 %all-to-all-done.4 = bf16[16,48,896]{2,1,0:T(8,128)(2,1)S(1)} async-done(((bf16[16,48,896]{2,1,0:T(8,128)(2,1)}), bf16[16,48,896]{2,1,0:T(8,128)(2,1)S(1)}, u32[]{:S(2)}, u32[]{:S(2)}) %all-to-all-start.4) | async-done | bytes 1376288 | tf_op jit(solution)/shard_map/all_to_all | solution.py:38
  250.7 1.1 fusion.39
  251.8 7.7 %all-to-all-start.5 = ((bf16[16,8,896]{2,1,0:T(8,128)(2,1)}), bf16[16,8,896]{2,1,0:T(8,128)(2,1)S(1)}, u32[]{:S(2)}, u32[]{:S(2)}) async-start(bf16[16,8,896]{2,1,0:T(8,128)(2,1)} %fusion.39), calls=%async_computation.5 | async-start | bytes 458752 | tf_op jit(solution)/shard_map/all_to_all | solution.py:38
  259.5 1.7 fusion.112
  261.2 8.9 %all-to-all-done.5 = bf16[16,8,896]{2,1,0:T(8,128)(2,1)S(1)} async-done(((bf16[16,8,896]{2,1,0:T(8,128)(2,1)}), bf16[16,8,896]{2,1,0:T(8,128)(2,1)S(1)}, u32[]{:S(2)}, u32[]{:S(2)}) %all-to-all-start.5) | async-done | bytes 229408 | tf_op jit(solution)/shard_map/all_to_all | solution.py:38
  (140 shorter events, 13.5 us)
Async XLA Ops:
  0.6 220.2 %copy-start = (bf16[1,1024,896]{2,1,0:T(8,128)(2,1)S(1)}, bf16[1,1024,896]{2,1,0:T(8,128)(2,1)}, u32[]{:S(2)}) copy-start(bf16[1,1024,896]{2,1,0:T(8,128)(2,1)} %param.31) | copy-start | bytes 5505028
  0.6 15.5 %copy-start.3 = (bf16[256,2,512]{2,1,0:T(2,128)(2,1)S(1)}, bf16[256,2,512]{2,1,0:T(2,128)(2,1)}, u32[]{:S(2)}) copy-start(bf16[256,2,512]{2,1,0:T(2,128)(2,1)} %param.16) | copy-start | bytes 1572868
  0.7 10.6 %copy-start.25 = (s32[8,8]{1,0:T(8,128)S(1)}, s32[8,8]{1,0:T(8,128)}, u32[]{:S(2)}) copy-start(s32[8,8]{1,0:T(8,128)} %param.27) | copy-start | bytes 772
  0.7 10.6 %copy-start.26 = (f32[8,8]{1,0:T(8,128)S(1)}, f32[8,8]{1,0:T(8,128)}, u32[]{:S(2)}) copy-start(f32[8,8]{1,0:T(8,128)} %param.28) | copy-start | bytes 772
  2.1 3.2 %copy-start.20 = (s32[256]{0:T(256)}, s32[256]{0:T(256)S(1)}, u32[]{:S(2)}) copy-start(s32[256]{0:T(256)S(1)} %fusion.142) | copy-start | bytes 3076
  5.2 19.4 %all-to-all-start = ((bf16[8,32,1152]{2,1,0:T(8,128)(2,1)}), bf16[8,32,1152]{2,1,0:T(8,128)(2,1)S(1)}, u32[]{:S(2)}, u32[]{:S(2)}) async-start(bf16[8,32,1152]{2,1,0:T(8,128)(2,1)} %bitcast), calls=%async_computation | async-start | bytes 1179648 | tf_op jit(solution)/shard_map/all_to_all | solution.py:38
  11.3 7.4 %copy-start.12 = (bf16[256,128]{1,0:T(8,128)(2,1)S(1)}, bf16[256,128]{1,0:T(8,128)(2,1)}, u32[]{:S(2)}) copy-start(bf16[256,128]{1,0:T(8,128)(2,1)} %param.17) | copy-start | bytes 196612
  11.4 10.0 %collective-permute-start = (bf16[8,32]{1,0:T(8,128)(2,1)S(1)}, bf16[8,32]{1,0:T(8,128)(2,1)S(1)}, u32[]{:S(2)}, u32[]{:S(2)}) collective-permute-start(bf16[8,32]{1,0:T(8,128)(2,1)S(1)} %pad_maximum_fusion.2), channel_id=1, source_target_pairs={{0,1},{1,0},{2,3},{3,2},{4,5},{5,4},{6,7},{7,6},{8,9},{9,8},{10,11... | collective-permute-start | bytes 1544 | tf_op jit(solution)/shard_map/ppermute | solution.py:139
  16.1 8.5 %copy-start.4 = (bf16[1,512,512]{2,1,0:T(8,128)(2,1)S(1)}, bf16[1,512,512]{2,1,0:T(8,128)(2,1)}, u32[]{:S(2)}) copy-start(bf16[1,512,512]{2,1,0:T(8,128)(2,1)} %param.20) | copy-start | bytes 1572868
  26.5 0.8 copy-start.5
  26.5 3.8 %copy-start.15 = (bf16[1,64,512]{2,1,0:T(8,128)(2,1)S(1)}, bf16[1,64,512]{2,1,0:T(8,128)(2,1)}, u32[]{:S(2)}) copy-start(bf16[1,64,512]{2,1,0:T(8,128)(2,1)} %param.21) | copy-start | bytes 196612
  30.6 0.8 copy-start.6
  30.6 2.7 %copy-start.24 = (f32[256]{0:T(256)S(1)}, f32[256]{0:T(256)}, u32[]{:S(2)}) copy-start(f32[256]{0:T(256)} %log_add_fusion) | copy-start | bytes 3076
  31.7 2.8 %copy-start.17 = (bf16[256,128]{1,0:T(8,128)(2,1)S(1)}, bf16[256,128]{1,0:T(8,128)(2,1)}, u32[]{:S(2)}) copy-start(bf16[256,128]{1,0:T(8,128)(2,1)} %fusion.47) | copy-start | bytes 196612
  31.7 11.3 %copy-start.14 = (bf16[256,64]{1,0:T(8,128)(2,1)S(1)}, bf16[256,64]{1,0:T(8,128)(2,1)}, u32[]{:S(2)}) copy-start(bf16[256,64]{1,0:T(8,128)(2,1)} %get-tuple-element.34) | copy-start | bytes 98308
  31.7 11.4 %copy-start.13 = (bf16[256,64]{1,0:T(8,128)(2,1)S(1)}, bf16[256,64]{1,0:T(8,128)(2,1)}, u32[]{:S(2)}) copy-start(bf16[256,64]{1,0:T(8,128)(2,1)} %get-tuple-element.35) | copy-start | bytes 98308
  31.7 11.5 %copy-start.18 = (bf16[256,64]{0,1:T(8,128)(2,1)S(1)}, bf16[256,64]{0,1:T(8,128)(2,1)}, u32[]{:S(2)}) copy-start(bf16[256,64]{0,1:T(8,128)(2,1)} %param.19) | copy-start | bytes 98308
  31.7 11.6 %copy-start.22 = (f32[256]{0:T(256)S(1)}, f32[256]{0:T(256)}, u32[]{:S(2)}) copy-start(f32[256]{0:T(256)} %get-tuple-element.2) | copy-start | bytes 3076
  31.7 11.6 %copy-start.23 = (f32[256]{0:T(256)S(1)}, f32[256]{0:T(256)}, u32[]{:S(2)}) copy-start(f32[256]{0:T(256)} %get-tuple-element.3) | copy-start | bytes 3076
  31.7 18.0 %copy-start.21 = (s32[256]{0:T(256)S(1)}, s32[256]{0:T(256)}, u32[]{:S(2)}) copy-start(s32[256]{0:T(256)} %copy-done.20) | copy-start | bytes 3076
  35.4 15.4 %copy-start.11 = (bf16[256,512]{1,0:T(8,128)(2,1)S(1)}, bf16[256,512]{1,0:T(8,128)(2,1)}, u32[]{:S(2)}) copy-start(bf16[256,512]{1,0:T(8,128)(2,1)} %param.18) | copy-start | bytes 786436
  35.4 14.3 %all-to-all-start.1 = ((bf16[8,32,384]{2,1,0:T(8,128)(2,1)}), bf16[8,32,384]{2,1,0:T(8,128)(2,1)S(1)}, u32[]{:S(2)}, u32[]{:S(2)}) async-start(bf16[8,32,384]{2,1,0:T(8,128)(2,1)} %concatenate.34), calls=%async_computation.1 | async-start | bytes 393216 | tf_op jit(solution)/shard_map/all_to_all | solution.py:38
  53.3 3.1 %copy-start.1 = (bf16[256,7168]{1,0:T(8,128)(2,1)S(1)}, bf16[256,7168]{1,0:T(8,128)(2,1)}, u32[]{:S(2)}) copy-start(bf16[256,7168]{1,0:T(8,128)(2,1)} %param.24) | copy-start | bytes 11010052
  58.0 15.1 %collective-permute-start.1 = (bf16[64,7168]{1,0:T(8,128)(2,1)S(1)}, bf16[64,7168]{1,0:T(8,128)(2,1)S(1)}, u32[]{:S(2)}, u32[]{:S(2)}) collective-permute-start(bf16[64,7168]{1,0:T(8,128)(2,1)S(1)} %convolution_convert_fusion.2), channel_id=1, source_target_pairs={{0,16},{1,17},{2,18},{3,19},{4,20},{5,21},{6,22},{7,23},{8,24},{9,... | collective-permute-start | bytes 2752520 | tf_op jit(solution)/shard_map/ppermute | solution.py:221
  61.1 21.7 %collective-permute-start.2 = (bf16[64,7168]{1,0:T(8,128)(2,1)S(1)}, bf16[64,7168]{1,0:T(8,128)(2,1)S(1)}, u32[]{:S(2)}, u32[]{:S(2)}) collective-permute-start(bf16[64,7168]{1,0:T(8,128)(2,1)S(1)} %convolution_convert_fusion.1), channel_id=1, source_target_pairs={{0,8},{1,9},{2,10},{3,11},{4,12},{5,13},{6,14},{7,15},{8,16},{9,17... | collective-permute-start | bytes 2752520 | tf_op jit(solution)/shard_map/ppermute | solution.py:221
  61.7 21.2 %collective-permute-start.3 = (bf16[64,7168]{1,0:T(8,128)(2,1)S(1)}, bf16[64,7168]{1,0:T(8,128)(2,1)S(1)}, u32[]{:S(2)}, u32[]{:S(2)}) collective-permute-start(bf16[64,7168]{1,0:T(8,128)(2,1)S(1)} %convolution_convert_fusion), channel_id=1, source_target_pairs={{0,24},{1,25},{2,26},{3,27},{4,28},{5,29},{6,30},{7,31},{8,0},{9,1... | collective-permute-start | bytes 2752520 | tf_op jit(solution)/shard_map/ppermute | solution.py:221
  64.4 25.2 %copy-start.16 = (bf16[8,7168]{1,0:T(8,128)(2,1)S(1)}, bf16[8,7168]{1,0:T(8,128)(2,1)}, u32[]{:S(2)}) copy-start(bf16[8,7168]{1,0:T(8,128)(2,1)} %param.25) | copy-start | bytes 344068
  84.3 7.6 %collective-permute-start.4 = (bf16[16,7168]{1,0:T(8,128)(2,1)S(1)}, bf16[16,7168]{1,0:T(8,128)(2,1)S(1)}, u32[]{:S(2)}, u32[]{:S(2)}) collective-permute-start(bf16[16,7168]{1,0:T(8,128)(2,1)S(1)} %get-tuple-element.19), channel_id=1, source_target_pairs={{0,4},{1,5},{2,6},{3,7},{4,0},{5,1},{6,2},{7,3},{8,12},{9,13},{10,... | collective-permute-start | bytes 688136 | tf_op jit(solution)/shard_map/ppermute | solution.py:224
  87.6 7.1 %collective-permute-start.6 = (bf16[16,7168]{1,0:T(8,128)(2,1)S(1)}, bf16[16,7168]{1,0:T(8,128)(2,1)S(1)}, u32[]{:S(2)}, u32[]{:S(2)}) collective-permute-start(bf16[16,7168]{1,0:T(8,128)(2,1)S(1)} %get-tuple-element.20), channel_id=1, source_target_pairs={{0,6},{1,7},{2,0},{3,1},{4,2},{5,3},{6,4},{7,5},{8,14},{9,15},{10,... | collective-permute-start | bytes 688136 | tf_op jit(solution)/shard_map/ppermute | solution.py:224
  88.6 7.2 %collective-permute-start.5 = (bf16[16,7168]{1,0:T(8,128)(2,1)S(1)}, bf16[16,7168]{1,0:T(8,128)(2,1)S(1)}, u32[]{:S(2)}, u32[]{:S(2)}) collective-permute-start(bf16[16,7168]{1,0:T(8,128)(2,1)S(1)} %get-tuple-element.21), channel_id=1, source_target_pairs={{0,2},{1,3},{2,4},{3,5},{4,6},{5,7},{6,0},{7,1},{8,10},{9,11},{10,... | collective-permute-start | bytes 688136 | tf_op jit(solution)/shard_map/ppermute | solution.py:224
  89.7 19.9 %copy-start.19 = (f32[7168]{0:T(1024)S(1)}, f32[7168]{0:T(1024)}, u32[]{:S(2)}) copy-start(f32[7168]{0:T(1024)} %param.26) | copy-start | bytes 86020
  96.0 14.6 %copy-start.2 = (f32[2,8,7168]{2,1,0:T(8,128)}, f32[2,8,7168]{2,1,0:T(8,128)S(1)}, u32[]{:S(2)}) copy-start(f32[2,8,7168]{2,1,0:T(8,128)S(1)} %get-tuple-element.7) | copy-start | bytes 1376260
  96.0 13.3 %collective-permute-start.7 = (bf16[2,8,7168]{2,1,0:T(8,128)(2,1)S(1)}, bf16[2,8,7168]{2,1,0:T(8,128)(2,1)S(1)}, u32[]{:S(2)}, u32[]{:S(2)}) collective-permute-start(bf16[2,8,7168]{2,1,0:T(8,128)(2,1)S(1)} %get-tuple-element.6), channel_id=1, source_target_pairs={{0,1},{1,0},{2,3},{3,2},{4,5},{5,4},{6,7},{7,6},{8,9},{9,8},{10,11... | collective-permute-start | bytes 688136 | tf_op jit(solution)/shard_map/ppermute | solution.py:233
  109.4 6.5 %copy-start.7 = (bf16[2,8,7168]{2,1,0:T(8,128)(2,1)}, bf16[2,8,7168]{2,1,0:T(8,128)(2,1)S(1)}, u32[]{:S(2)}) copy-start(bf16[2,8,7168]{2,1,0:T(8,128)(2,1)S(1)} %collective-permute-done.7) | copy-start | bytes 688132
  110.6 12.5 %all-to-all-start.2 = ((bf16[8,16,896]{2,1,0:T(8,128)(2,1)}), bf16[8,16,896]{2,1,0:T(8,128)(2,1)S(1)}, u32[]{:S(2)}, u32[]{:S(2)}) async-start(bf16[8,16,896]{2,1,0:T(8,128)(2,1)} %copy.123), calls=%async_computation.2 | async-start | bytes 458752 | tf_op jit(solution)/shard_map/all_to_all | solution.py:38
  124.7 26.5 %all-to-all-start.3 = ((bf16[16,48,896]{2,1,0:T(8,128)(2,1)}), bf16[16,48,896]{2,1,0:T(8,128)(2,1)S(1)}, u32[]{:S(2)}, u32[]{:S(2)}) async-start(bf16[16,48,896]{2,1,0:T(8,128)(2,1)} %bitcast.29), calls=%async_computation.3 | async-start | bytes 2752512 | tf_op jit(solution)/shard_map/all_to_all | solution.py:38
  151.2 3.0 %copy-start.9 = (bf16[16,48,896]{2,1,0:T(8,128)(2,1)}, bf16[16,48,896]{2,1,0:T(8,128)(2,1)S(1)}, u32[]{:S(2)}) copy-start(bf16[16,48,896]{2,1,0:T(8,128)(2,1)S(1)} %all-to-all-done.3) | copy-start | bytes 4128772
  151.2 3.0 %copy-start.27 = (bf16[1,896,1024]{2,1,0:T(8,128)(2,1)S(1)}, bf16[1,896,1024]{2,1,0:T(8,128)(2,1)}, u32[]{:S(2)}) copy-start(bf16[1,896,1024]{2,1,0:T(8,128)(2,1)} %param.29) | copy-start | bytes 5505028
  156.5 3.9 %collective-permute-start.8 = (bf16[384,2048]{1,0:T(8,128)(2,1)}, bf16[384,2048]{1,0:T(8,128)(2,1)}, u32[]{:S(2)}, u32[]{:S(2)}) collective-permute-start(bf16[384,2048]{1,0:T(8,128)(2,1)} %pad_maximum_fusion), channel_id=1, source_target_pairs={{0,32},{32,0},{1,33},{33,1},{2,34},{34,2},{3,35},{35,3},{4,36},{36... | collective-permute-start | bytes 4718600 | tf_op jit(solution)/shard_map/ppermute | solution.py:252
  156.5 2.8 %copy-start.10 = (bf16[16,48,896]{2,1,0:T(8,128)(2,1)S(1)}, bf16[16,48,896]{2,1,0:T(8,128)(2,1)}, u32[]{:S(2)}) copy-start(bf16[16,48,896]{2,1,0:T(8,128)(2,1)} %copy-done.9) | copy-start | bytes 4128772
  156.5 2.9 %copy-start.28 = (bf16[1,896,1024]{2,1,0:T(8,128)(2,1)S(1)}, bf16[1,896,1024]{2,1,0:T(8,128)(2,1)}, u32[]{:S(2)}) copy-start(bf16[1,896,1024]{2,1,0:T(8,128)(2,1)} %param.29) | copy-start | bytes 5505028
  162.9 19.4 %collective-permute-start.9 = (bf16[96,2048]{1,0:T(8,128)(2,1)}, bf16[96,2048]{1,0:T(8,128)(2,1)}, u32[]{:S(2)}, u32[]{:S(2)}) collective-permute-start(bf16[96,2048]{1,0:T(8,128)(2,1)} %get-tuple-element.14), channel_id=1, source_target_pairs={{0,128},{64,192},{128,0},{192,64},{1,129},{65,193},{129,1},{193,65... | collective-permute-start | bytes 1179656 | tf_op jit(solution)/shard_map/ppermute | solution.py:262
  165.0 34.1 %collective-permute-start.10 = (bf16[96,2048]{1,0:T(8,128)(2,1)}, bf16[96,2048]{1,0:T(8,128)(2,1)}, u32[]{:S(2)}, u32[]{:S(2)}) collective-permute-start(bf16[96,2048]{1,0:T(8,128)(2,1)} %get-tuple-element.15), channel_id=1, source_target_pairs={{0,64},{64,128},{128,192},{192,0},{1,65},{65,129},{129,193},{193,1... | collective-permute-start | bytes 1179656 | tf_op jit(solution)/shard_map/ppermute | solution.py:262
  166.1 34.8 %collective-permute-start.11 = (bf16[96,2048]{1,0:T(8,128)(2,1)}, bf16[96,2048]{1,0:T(8,128)(2,1)}, u32[]{:S(2)}, u32[]{:S(2)}) collective-permute-start(bf16[96,2048]{1,0:T(8,128)(2,1)} %get-tuple-element.16), channel_id=1, source_target_pairs={{0,192},{64,0},{128,64},{192,128},{1,193},{65,1},{129,65},{193,129... | collective-permute-start | bytes 1179656 | tf_op jit(solution)/shard_map/ppermute | solution.py:262
  218.6 2.3 collective-permute-start.12
  224.1 5.8 %copy-start.8 = (bf16[2,8,7168]{2,1,0:T(8,128)(2,1)S(1)}, bf16[2,8,7168]{2,1,0:T(8,128)(2,1)}, u32[]{:S(2)}) copy-start(bf16[2,8,7168]{2,1,0:T(8,128)(2,1)} %copy-done.7) | copy-start | bytes 688132
  224.1 26.2 %all-to-all-start.4 = ((bf16[16,48,896]{2,1,0:T(8,128)(2,1)}), bf16[16,48,896]{2,1,0:T(8,128)(2,1)S(1)}, u32[]{:S(2)}, u32[]{:S(2)}) async-start(bf16[16,48,896]{2,1,0:T(8,128)(2,1)} %bitcast.139), calls=%async_computation.4 | async-start | bytes 2752512 | tf_op jit(solution)/shard_map/all_to_all | solution.py:38
  251.8 18.3 %all-to-all-start.5 = ((bf16[16,8,896]{2,1,0:T(8,128)(2,1)}), bf16[16,8,896]{2,1,0:T(8,128)(2,1)S(1)}, u32[]{:S(2)}, u32[]{:S(2)}) async-start(bf16[16,8,896]{2,1,0:T(8,128)(2,1)} %fusion.39), calls=%async_computation.5 | async-start | bytes 458752 | tf_op jit(solution)/shard_map/all_to_all | solution.py:38

commit v3 on v1

v3 whole, which is shorter than its diff:
```python
import functools

import jax
import jax.numpy as jnp
from jax import lax
from jax.experimental import pallas as pl
from jax.experimental.pallas import tpu as pltpu
from jax.sharding import Mesh, PartitionSpec as P

ROPE = 64
VD = 128
NORM_EPS = 1e-06
SCALE = (VD + ROPE) ** (-0.5)
RUNS = 4
CAP = 3
ROWS = 8
LINE_ORDER = (2, 1, 3)

SIDE = 4
LINES = 4
CORES = 2
HALVES = 2
GROUPS = LINES * CORES
PLANES = SIDE * SIDE
GROUP = ("zlo", "core")
XY = ("x", "y")
ALL = ("zlo", "core", "x", "y", "zhi")
SIZES = (LINES, CORES, SIDE, SIDE, HALVES)
BF = jnp.bfloat16
F32 = jnp.float32


def dot(a, b):
    return jnp.dot(a, b, preferred_element_type=F32)


def dot_t(a, b):
    return lax.dot_general(a, b, (((1,), (1,)), ((), ())), preferred_element_type=F32)


def dot_rows(a, b):
    return lax.dot_general(a, b, (((0,), (0,)), ((), ())), preferred_element_type=F32)


def split(value, count):
    pieces = []
    for _ in range(count):
        piece = lax.reduce_precision(value, 8, 7)
        pieces.append(piece.astype(BF))
        value = value - piece
    return pieces


def split_in_kernel(value):
    one = value.astype(BF)
    rest = value - one.astype(F32)
    two = rest.astype(BF)
    return one, two, (rest - two.astype(F32)).astype(BF)


def exchange(value, axes):
    return lax.all_to_all(value, axes, 0, 0, tiled=True)


def flips(count, k):
    return [(i, i ^ k) for i in range(count)]


def sum_wide(parts):
    total = parts[0].astype(F32)
    for part in parts[1:]:
        total = total + part.astype(F32)
    return total


def shift(k):
    return [(i, (i + k) % LINES) for i in range(LINES)]


def along_line(parts, sign=1):
    got = {k: lax.ppermute(parts[k], "zlo", shift(sign * k)) for k in LINE_ORDER}
    return [parts[0]] + [got[k] for k in range(1, LINES)]


def plane_shift(k, stage):
    pairs = []

    def number(place):
        flat = 0
        for size, one in zip(SIZES, place):
            flat = flat * size + one
        return flat

    for flat in range(LINES * CORES * PLANES * HALVES):
        place, rest = [], flat
        for size in reversed(SIZES):
            place.insert(0, rest % size)
            rest //= size
        there = list(place)
        axis = 2 if place[1] == stage else 3
        there[axis] = (there[axis] + k) % SIDE
        pairs.append((number(place), number(there)))
    return pairs


def one_hot(source, count):
    return (source[:, None] == jnp.arange(count, dtype=jnp.int32)[None, :]).astype(BF)


def plane_order(my_core):
    me = (lax.axis_index("x"), lax.axis_index("y"))
    row = jnp.arange(PLANES * HALVES * ROWS, dtype=jnp.int32)
    rest = row % (HALVES * ROWS)
    first = row // (HALVES * ROWS) // SIDE
    second = row // (HALVES * ROWS) % SIDE
    x = (me[0] + jnp.where(my_core == 0, first, second)) % SIDE
    y = (me[1] + jnp.where(my_core == 0, second, first)) % SIDE
    return one_hot((x * SIDE + y) * (HALVES * ROWS) + rest, row.shape[0])


def sorted_place(prompt_of_sample, my_line, my_core):
    samples = prompt_of_sample.shape[0]
    block = samples // (GROUPS * RUNS)
    own = prompt_of_sample.reshape(-1, block)[:, 0]
    at = jnp.arange(own.shape[0], dtype=jnp.int32)
    same = (own[:, None] == own[None, :]) & (at[None, :] < at[:, None])
    line = (own // CORES + LINES - my_line) % LINES
    seen = line * CORES + (own % CORES ^ my_core)
    rank = seen * RUNS + jnp.sum(same.astype(jnp.int32), axis=1)
    return jnp.repeat(rank, block) * block + jnp.arange(samples, dtype=jnp.int32) % block


def sort_kernel(q_latent_ref, q_rope_ref, place_ref, *out_refs):
    samples, heads, lat = q_latent_ref.shape
    order = place_ref[...] == lax.broadcasted_iota(jnp.int32, (samples, samples), 0)
    order = jnp.where(order, 1.0, 0.0).astype(BF)
    each = samples // LINES
    parts = [q_latent_ref[:, head, :] for head in range(heads)] + [q_rope_ref[...]]
    at = 0
    for part in parts:
        wide = dot(order, part).astype(BF)
        for k, out_ref in enumerate(out_refs):
            out_ref[:, at : at + part.shape[1]] = wide[k * each : (k + 1) * each]
        at += part.shape[1]


def attend_kernel(heads, *refs):
    q_refs, out_refs = refs[:LINES], refs[-LINES:]
    key_refs = refs[LINES : LINES + CORES]
    rope_refs = refs[LINES + CORES : LINES + 2 * CORES]
    w_uv_ref, table_ref = refs[LINES + 2 * CORES : LINES + 2 * CORES + 2]
    lat = key_refs[0].shape[1]
    each = q_refs[0].shape[0] // CORES
    rows = each * LINES
    column = lax.broadcasted_iota(jnp.int32, (rows, VD), 1)
    for core in range(CORES):
        mine = slice(core * each, (core + 1) * each)
        q = jnp.concatenate([ref[mine, :] for ref in q_refs], axis=0)
        keys = key_refs[core][...]
        rope_keys = rope_refs[core][...]
        none = jnp.zeros_like(rope_keys)
        extra = jnp.concatenate([table_ref[mine, :]] * LINES, axis=0).astype(F32)
        for head in range(heads):
            pair = [rope_keys if head == one else none for one in range(heads)]
            score = dot_t(q[:, head * lat : (head + 1) * lat], keys)
            score = (score + dot(q[:, heads * lat :], jnp.concatenate(pair, axis=0))) * SCALE
            best = jnp.max(score, axis=-1, keepdims=True)
            weight = jnp.exp(score - best)
            total = jnp.sum(weight, axis=-1, keepdims=True)
            latent = (dot(weight.astype(BF), keys) / total).astype(BF)
            value = dot(latent, w_uv_ref[head]).astype(BF)
            for k, out_ref in enumerate(out_refs):
                out_ref[mine, head * VD : (head + 1) * VD] = value[k * each : (k + 1) * each]
            for place, piece in enumerate(split_in_kernel(best + jnp.log(total))):
                extra = jnp.where(column == 3 * head + place, piece.astype(F32), extra)
        extra = extra.astype(BF)
        for k, out_ref in enumerate(out_refs):
            out_ref[mine, heads * VD :] = extra[k * each : (k + 1) * each]


def merge_kernel(heads, *refs):
    back_refs = refs[:LINES]
    place_ref, order_ref, self_score_ref, self_latent_ref, w_uv_ref, out_ref = refs[LINES:]
    back = jnp.concatenate([ref[...] for ref in back_refs], axis=0)
    samples = back.shape[0]
    to_place = place_ref[...] == lax.broadcasted_iota(jnp.int32, (samples, samples), 0)
    back = dot_rows(jnp.where(to_place, 1.0, 0.0).astype(BF), back)
    values = []
    for head in range(heads):
        at = heads * VD + 3 * head
        lse = back[:, at : at + 1] + back[:, at + 1 : at + 2] + back[:, at + 2 : at + 3]
        self_score = self_score_ref[:, head : head + 1]
        best = jnp.maximum(lse, self_score)
        cache_part = jnp.exp(lse - best)
        self_part = jnp.exp(self_score - best)
        own_value = dot(self_latent_ref[...], w_uv_ref[head])
        mixed = cache_part * back[:, head * VD : (head + 1) * VD] + self_part * own_value
        values.append((mixed / (cache_part + self_part)).astype(BF))
    out_ref[...] = dot(order_ref[...], jnp.concatenate(values, axis=1)).astype(BF)


def up_kernel(line_ref, rows_ref, *refs):
    w_refs, out_refs = refs[: 2 * CORES], refs[2 * CORES :]
    each = rows_ref.shape[0] // LINES
    share = rows_ref.shape[1] // CORES
    line = line_ref[0]
    rows = []
    for k in range(LINES):
        at = pl.multiple_of(lax.rem(line + k, LINES) * each, each)
        rows.append(rows_ref[pl.ds(at, each), :])
    rows = jnp.concatenate(rows, axis=0)
    for half in range(2):
        total = dot(rows[:, :share], w_refs[half][...]) + dot(rows[:, share:], w_refs[2 + half][...])
        total = total.astype(BF)
        width = total.shape[1]
        for k, out_ref in enumerate(out_refs):
            out_ref[:, half * width : (half + 1) * width] = total[k * each : (k + 1) * each]


def down_kernel(line_ref, *refs):
    hidden_refs, w_refs, out_ref = refs[:LINES], refs[LINES : LINES + CORES], refs[-1]
    each = hidden_refs[0].shape[0]
    line = line_ref[0]
    hidden = jnp.concatenate([ref[...] for ref in hidden_refs], axis=0)
    for core in range(CORES):
        total = dot(hidden, w_refs[core][...]).astype(BF)
        width = total.shape[1]
        for k in range(LINES):
            at = pl.multiple_of(lax.rem(line + LINES - k, LINES) * each, each)
            out_ref[pl.ds(at, each), core * width : (core + 1) * width] = total[k * each : (k + 1) * each]


def on_chip(kernel, shapes, *args):
    vmem = pl.BlockSpec(memory_space=pltpu.VMEM)
    smem = pl.BlockSpec(memory_space=pltpu.SMEM)
    return pl.pallas_call(
        kernel,
        out_shape=[jax.ShapeDtypeStruct(shape, BF) for shape in shapes],
        in_specs=[smem if one.shape == (1,) else vmem for one in args],
        out_specs=[vmem] * len(shapes),
        compiler_params=pltpu.CompilerParams(vmem_limit_bytes=48 * 1024 * 1024),
    )(*args)


def routing_tables(ids, gates, my_half, order):
    tokens = ids.shape[0]
    slots = tokens // ROWS * CAP
    wanted = jnp.arange(PLANES, dtype=jnp.int32) * HALVES + my_half
    hit = ids[:, :, None] == wanted[None, None, :]
    member = jnp.any(hit, axis=1)
    gate_of = jnp.sum(jnp.where(hit, gates[:, :, None], 0.0), axis=1)
    before = jnp.cumsum(member.astype(jnp.int32), axis=0) - member.astype(jnp.int32)
    place = jnp.where(member, before, -1).T
    routed = place[:, None, :] == jnp.arange(slots, dtype=jnp.int32)[None, :, None]
    routed = routed.reshape(PLANES * slots, tokens)
    weights = jnp.where(routed, jnp.repeat(gate_of.T, slots, axis=0), 0.0)
    routing = jnp.take(routed.astype(BF).reshape(PLANES * slots, LINES, -1), order, axis=1)
    return (routing.reshape(PLANES * slots, tokens), *split(weights, 2))


def body(
    q_latent,
    q_rope,
    self_latent,
    self_rope,
    cache_latent,
    cache_rope,
    prompt_of_sample,
    w_uv,
    w_out,
    residual,
    norm_gain,
    expert_ids,
    gate_weight,
    w_gate,
    w_up,
    w_down,
):
    my_half = lax.axis_index("zhi")
    my_core = lax.axis_index("core")
    my_line = lax.axis_index("zlo")
    line = my_line.astype(jnp.int32).reshape(1)
    lines = jnp.arange(LINES, dtype=jnp.int32)
    samples, heads, lat = q_latent.shape
    width = residual.shape[1]
    share = width // GROUPS
    top = expert_ids.shape[1]
    tokens = LINES * HALVES * ROWS
    each = samples // LINES

    def sibling(value):
        return lax.ppermute(value, "core", flips(CORES, 1))

    place = sorted_place(prompt_of_sample, my_line, my_core)[None, :]
    q_sorted = on_chip(
        sort_kernel, [(each, heads * lat + heads * ROPE)] * LINES, q_latent, q_rope, place
    )
    q_here = along_line(q_sorted)
    keys = [cache_latent[0], sibling(cache_latent[0])]
    rope_keys = [cache_rope[0], sibling(cache_rope[0])]

    own_table = jnp.concatenate([expert_ids.astype(BF), *split(gate_weight, 3)], axis=1)
    other_table = lax.ppermute(own_table, "zhi", flips(HALVES, 1))
    table = jnp.concatenate(
        [
            jnp.where(my_half == 0, own_table, other_table),
            jnp.where(my_half == 0, other_table, own_table),
        ],
        axis=0,
    )
    stats = 3 * heads
    table_pad = jnp.pad(
        table, ((0, each - table.shape[0]), (stats, VD - stats - table.shape[1]))
    )
    back = on_chip(
        functools.partial(attend_kernel, heads),
        [(each, (heads + 1) * VD)] * LINES,
        *q_here,
        *keys,
        *rope_keys,
        w_uv,
        table_pad,
    )
    back = along_line(back, -1)
    self_wide = self_latent.astype(F32)
    self_pos = self_rope.astype(F32)
    self_score = [
        jnp.sum(q_latent[:, head].astype(F32) * self_wide, axis=-1)
        + jnp.sum(q_rope[:, head * ROPE : (head + 1) * ROPE].astype(F32) * self_pos, axis=-1)
        for head in range(heads)
    ]
    self_score = jnp.stack(self_score, axis=1) * SCALE
    (head_rows,) = on_chip(
        functools.partial(merge_kernel, heads),
        [(samples, heads * VD)],
        *back,
        place,
        plane_order(my_core),
        self_score,
        self_latent,
        w_uv,
    )

    rows = head_rows.reshape(SIDE, samples // SIDE, -1)
    first = [dot(rows[k], w_out).astype(BF) for k in range(SIDE)]
    first = sum_wide([first[0]] + [lax.ppermute(first[k], ALL, plane_shift(k, 0)) for k in (2, 1, 3)])
    first = first.astype(BF).reshape(SIDE, HALVES * ROWS, width)
    near = sum_wide([first[0]] + [lax.ppermute(first[k], ALL, plane_shift(k, 1)) for k in (2, 1, 3)])

    near = near.reshape(HALVES, ROWS, width)
    is_mine = (jnp.arange(HALVES) == my_half)[:, None, None]
    with_residual = near + jnp.where(is_mine, residual.astype(F32)[None], 0.0)
    far = lax.ppermute(with_residual.astype(BF), "zhi", flips(HALVES, 1)).astype(F32)
    attn_proj = lax.dynamic_index_in_dim(near + far, my_half, 0, keepdims=False).astype(BF)
    mixed = with_residual + far
    normed = (
        mixed * lax.rsqrt(jnp.mean(mixed * mixed, axis=-1, keepdims=True) + NORM_EPS) * norm_gain
    ).astype(BF)

    by_chip = normed.reshape(HALVES * ROWS, LINES, CORES, share)
    by_chip = jnp.where(my_core == 0, by_chip, by_chip[:, :, ::-1]).reshape(-1, LINES, CORES * share)
    by_chip = jnp.take(by_chip.transpose(1, 0, 2), (my_line + LINES - lines) % LINES, axis=0)
    token_rows = jnp.concatenate(along_line([by_chip[k] for k in range(LINES)], -1), axis=0)

    table = jnp.stack([one[: HALVES * ROWS, heads * VD + stats :] for one in back])
    table = jnp.take(table, (lines + LINES - my_line) % LINES, axis=0)
    table = table.reshape(tokens, -1).astype(F32)
    gates = table[:, top : 2 * top] + table[:, 2 * top : 3 * top] + table[:, 3 * top : 4 * top]
    routing, gate_hi, gate_lo = routing_tables(
        table[:, :top].astype(jnp.int32), gates, my_half, (lines + my_line) % LINES
    )
    rows_in = exchange(dot(routing, token_rows).astype(BF), XY)

    line_rows = rows_in.shape[0] // LINES
    parts = on_chip(
        up_kernel,
        [(line_rows, 2 * w_gate.shape[2])] * LINES,
        line,
        rows_in,
        w_gate[0],
        w_up[0],
        sibling(w_gate[0]),
        sibling(w_up[0]),
    )
    sums = sum_wide(along_line(parts))
    ffe = sums.shape[1] // 2
    hidden = (jax.nn.silu(sums[:, :ffe]) * sums[:, ffe:]).astype(BF)
    (expert_out,) = on_chip(
        down_kernel,
        [(rows_in.shape[0], CORES * share)],
        line,
        *along_line([hidden] * LINES),
        w_down[0],
        sibling(w_down[0]),
    )

    returned = exchange(expert_out, XY)
    moe = dot_rows(gate_hi, returned) + dot_rows(gate_lo, returned)
    moe = exchange(moe.astype(BF), ("zlo", "zhi"))
    moe = jnp.sum(moe.reshape(LINES, HALVES, ROWS, CORES, share).astype(F32), axis=1).astype(BF)
    moe = jnp.where(my_core == 0, moe, moe[:, :, ::-1])
    moe_out = moe.transpose(1, 0, 2, 3).reshape(ROWS, width)
    return (attn_proj, moe_out)


def solution(mesh):
    fine = Mesh(mesh.devices.reshape(SIZES), ALL)
    g = GROUP
    e = XY + ("zhi",)
    in_specs = (
        P(g, e, None),
        P(g, e),
        P(g, None),
        P(g, None),
        P(g, None, None),
        P(g, None, None),
        P(g),
        P(e, None, None),
        P(e, None),
        P(g + e, None),
        P(),
        P(g + e, None),
        P(g + e, None),
        P(e, g, None),
        P(e, g, None),
        P(e, None, g),
    )
    out_specs = (P(g + e, None), P(g + e, None))
    return jax.shard_map(body, mesh=fine, in_specs=in_specs, out_specs=out_specs, check_vma=False)
```

time: 340 us -> 243 us (0.71)
  blocking collectives: 81.2 us -> 0 us
  Pallas kernels: 0 us -> 17.2 us
  waiting for transfers between devices: 129 us -> 115 us
  between operations: 14.4 us -> 1.21 us
  matrix products: 27.1 us -> 14.4 us
    ppermute x2 -> x28, waiting for transfers between devices: 5.8 us -> 74.5 us  [the longest x15 41.3 us: along_line(): lax.ppermute(parts[k], 'zlo', shift(sign * k))]
    all_gather x1 -> x0, waiting for transfers between devices: 41.4 us -> none  [body(): hidden = lax.all_gather(hidden, ('core', 'zlo'), axis=0, tiled=True)]
    all_to_all x7 -> x3, waiting for transfers between devices: 81.9 us -> 40.6 us  [exchange(): return lax.all_to_all(value, axes, 0, 0, tiled=True)]
    all_gather x1 -> x0, blocking collectives: 41.1 us -> none  [body(): table = lax.all_gather(table, GROUP + ('zhi',), axis=0, tiled=True)]
    all_to_all x1 -> x0, blocking collectives: 40.1 us -> none  [exchange(): return lax.all_to_all(value, axes, 0, 0, tiled=True)]
    ppermute x2 -> x28, starting transfers between devices: 4.82 us -> 44.5 us  [the longest x15 25 us: along_line(): lax.ppermute(parts[k], 'zlo', shift(sign * k))]
    all_to_all x7 -> x3, starting transfers between devices: 55.7 us -> 19.5 us  [exchange(): return lax.all_to_all(value, axes, 0, 0, tiled=True)]
    pallas_call x0 -> x5, Pallas kernels: none -> 17.2 us  [on_chip(): pl.pallas_call(kernel, out_shape=[jax.ShapeDtypeStruct(shape, BF) for sha...]
  transfers between devices with their start and end apart: 10 -> 31, of which waited for: 10 -> 20; matrix products, arithmetic and copies ran while one was open for 2% -> 15% of each run, Pallas kernels for 0% -> 5%
where the time goes in v3:
time: 243 us; the launch traced here: 242 us
  waiting for transfers between devices  115 us (47%)
  starting transfers between devices  63.9 us (26%)
  Pallas kernels  17.2 us (7%)
  local copies, waits for them, and re-layouts  16.2 us (7%)
  matrix products  14.4 us (6%)
  other arithmetic  13.8 us (6%)
    ppermute x15, waiting for transfers between devices, along_line(): lax.ppermute(parts[k], 'zlo', shift(sign * k))  41.3 us
    all_to_all x3, waiting for transfers between devices, exchange(): return lax.all_to_all(value, axes, 0, 0, tiled=True)  40.6 us
    ppermute x15, starting transfers between devices, along_line(): lax.ppermute(parts[k], 'zlo', shift(sign * k))  25 us
    all_to_all x3, starting transfers between devices, exchange(): return lax.all_to_all(value, axes, 0, 0, tiled=True)  19.5 us
    ppermute x3, waiting for transfers between devices, body(): lax.ppermute(first[k], ALL, plane_shift(k, 0))  17.8 us
    pallas_call x5, Pallas kernels, on_chip(): pl.pallas_call(kernel, out_shape=[jax.ShapeDtypeStruct(shape, BF) for sha...  17.2 us
    dot_general x5, matrix products, dot(): return jnp.dot(a, b, preferred_element_type=F32)  12.9 us
    ppermute x1, waiting for transfers between devices, body(): lax.ppermute(with_residual.astype(BF), 'zhi', flips(HALVES, 1)).astype(F32)  9.88 us
  transfers between devices with their start and end apart: 31, of which 20 were waited for; matrix products, arithmetic and copies ran while one was open for 15% of the time, Pallas kernels for 5%

profile of v3, /device:TPU:32, one launch (start us, length us, event | category | flops | bytes accessed | tf_op | source)
XLA Modules:
  0.0 241.8 jit_solution(16171516628368982738)
XLA Ops:
  0.6 0.7 convert_element_type.150
  1.3 0.7 reduce-precision_convert_fusion.3
  2.0 0.7 pad_maximum_fusion.1
  2.7 6.3 %collective-permute-start.5 = (bf16[8,32]{1,0:T(8,128)(2,1)}, bf16[8,32]{1,0:T(8,128)(2,1)}, u32[]{:S(2)}, u32[]{:S(2)}) collective-permute-start(bf16[8,32]{1,0:T(8,128)(2,1)} %pad_maximum_fusion.1), channel_id=1, source_target_pairs={{0,1},{1,0},{2,3},{3,2},{4,5},{5,4},{6,7},{7,6},{8,9},{9,8},{10,11... | collective-permute-start | bytes 1544 | tf_op jit(solution)/shard_map/ppermute | solution.py:303
  9.5 0.8 reshape.410
  10.8 1.0 copy-done
  11.8 0.8 copy-done.5
  12.7 2.1 shard_map.167
  15.4 1.0 collective-permute-start
  16.4 2.4 collective-permute-start.1
  20.5 1.0 fusion.76
  21.6 3.2 %fusion.75 = (bf16[256,1,512]{2,1,0:T(2,128)(2,1)}, bf16[256,1,512]{2,1,0:T(2,128)(2,1)}) fusion(bf16[256,2,512]{2,1,0:T(2,128)(2,1)} %q_latent_ref.1), kind=kLoop, calls=%fused_computation.196 | loop fusion | bytes 1048576 | tf_op jit(solution)/shard_map/slice | solution.py:328
  26.8 1.4 fusion.8
  30.1 0.7 convert_element_type.176
  31.0 0.7 broadcast_select_fusion.3
  32.3 3.9 %collective-permute-done.2.refs_3_ = bf16[64,1152]{1,0:T(8,128)(2,1)S(1)} collective-permute-done((bf16[64,1152]{1,0:T(8,128)(2,1)}, bf16[64,1152]{1,0:T(8,128)(2,1)S(1)}, u32[]{:S(2)}, u32[]{:S(2)}) %collective-permute-start.2) | collective-permute-done | bytes 147488 | tf_op jit(solution)/shard_map/ppermute | solution.py:81
  36.3 3.7 %shard_map.168 = (bf16[64,384]{1,0:T(8,128)(2,1)S(1)}, bf16[64,384]{1,0:T(8,128)(2,1)S(1)}, bf16[64,384]{1,0:T(8,128)(2,1)S(1)}, bf16[64,384]{1,0:T(8,128)(2,1)S(1)}) custom-call(bf16[64,1152]{1,0:T(8,128)(2,1)S(1)} %get-tuple-element.14.refs_0_, bf16[64,1152]{1,0:T(8,128)(2,1)} %collective-permute-done.refs_1_, ...), custom_call_target="tpu_custom_call" | custom-call | tf_op jit(solution)/shard_map/pallas_call | solution.py:236
  40.4 2.2 collective-permute-start.7
  42.6 2.8 %collective-permute-start.8 = (bf16[64,384]{1,0:T(8,128)(2,1)S(1)}, bf16[64,384]{1,0:T(8,128)(2,1)S(1)}, u32[]{:S(2)}, u32[]{:S(2)}) collective-permute-start(bf16[64,384]{1,0:T(8,128)(2,1)S(1)} %get-tuple-element.21), channel_id=1, source_target_pairs={{0,64},{64,128},{128,192},{192,0},{1,65},{65,129},{129,193},{193,1... | collective-permute-start | bytes 147464 | tf_op jit(solution)/shard_map/ppermute | solution.py:81
  45.9 1.3 collective-permute-done.8.refs_3_
  47.1 0.9 shard_map.169
  48.1 3.9 %convolution_convert_fusion = bf16[64,7168]{1,0:T(8,128)(2,1)} fusion(bf16[256,7168]{1,0:T(8,128)(2,1)} %param.24, bf16[256,256]{1,0:T(8,128)(2,1)S(1)} %shard_map.169), kind=kOutput, calls=%fused_computation.3 | convolution fusion | flops 235339776 | bytes 4620288 | tf_op jit(solution)/shard_map/dot_general | solution.py:34
  52.0 1.7 convolution_convert_fusion.1
  53.7 1.8 convolution_convert_fusion.2
  55.4 3.0 %collective-permute-start.9 = (bf16[64,7168]{1,0:T(8,128)(2,1)}, bf16[64,7168]{1,0:T(8,128)(2,1)}, u32[]{:S(2)}, u32[]{:S(2)}) collective-permute-start(bf16[64,7168]{1,0:T(8,128)(2,1)} %convolution_convert_fusion.2), channel_id=1, source_target_pairs={{0,16},{1,17},{2,18},{3,19},{4,20},{5,21},{6,22},{7,23},{8,24},{9,... | collective-permute-start | bytes 2752520 | tf_op jit(solution)/shard_map/ppermute | solution.py:346
  59.1 2.6 %collective-permute-start.11 = (bf16[64,7168]{1,0:T(8,128)(2,1)}, bf16[64,7168]{1,0:T(8,128)(2,1)}, u32[]{:S(2)}, u32[]{:S(2)}) collective-permute-start(bf16[64,7168]{1,0:T(8,128)(2,1)} %convolution_convert_fusion), channel_id=1, source_target_pairs={{0,24},{1,25},{2,26},{3,27},{4,28},{5,29},{6,30},{7,31},{8,0},{9,1... | collective-permute-start | bytes 2752520 | tf_op jit(solution)/shard_map/ppermute | solution.py:346
  61.9 0.7 gather_fusion
  62.8 7.9 %collective-permute-done.9 = bf16[64,7168]{1,0:T(8,128)(2,1)} collective-permute-done((bf16[64,7168]{1,0:T(8,128)(2,1)}, bf16[64,7168]{1,0:T(8,128)(2,1)}, u32[]{:S(2)}, u32[]{:S(2)}) %collective-permute-start.9) | collective-permute-done | bytes 917536 | tf_op jit(solution)/shard_map/ppermute | solution.py:346
  70.8 9.7 %collective-permute-done.10 = bf16[64,7168]{1,0:T(8,128)(2,1)} collective-permute-done((bf16[64,7168]{1,0:T(8,128)(2,1)}, bf16[64,7168]{1,0:T(8,128)(2,1)}, u32[]{:S(2)}, u32[]{:S(2)}) %collective-permute-start.10) | collective-permute-done | bytes 917536 | tf_op jit(solution)/shard_map/ppermute | solution.py:346
  80.6 4.0 %fusion.4 = bf16[64,7168]{1,0:T(8,128)(2,1)S(1)} fusion(bf16[256,7168]{1,0:T(8,128)(2,1)} %param.24, bf16[64,7168]{1,0:T(8,128)(2,1)} %collective-permute-done.11, bf16[64,7168]{1,0:T(8,128)(2,1)} %collective-permute-done.10, bf16[64,7168]{1,0:T(8,128)(2,1)} %collective-permute-done.9, bf16[256,256]{1,0:T(8,128)(2,1)S(1)} %shard_map.169), kind=kOutput, calls=%fused_computation.11 | convolution fusion | flops 239009792 | bytes 7372800 | tf_op jit(solution)/shard_map/dot_general | solution.py:34
  84.6 0.9 fusion.74
  85.4 3.2 %collective-permute-start.12 = (bf16[16,7168]{1,0:T(8,128)(2,1)}, bf16[16,7168]{1,0:T(8,128)(2,1)S(1)}, u32[]{:S(2)}, u32[]{:S(2)}) collective-permute-start(bf16[16,7168]{1,0:T(8,128)(2,1)} %get-tuple-element.32), channel_id=1, source_target_pairs={{0,4},{1,5},{2,6},{3,7},{4,0},{5,1},{6,2},{7,3},{8,12},{9,13},{10,... | collective-permute-start | bytes 688136 | tf_op jit(solution)/shard_map/ppermute | solution.py:348
  88.6 1.1 collective-permute-start.14
  89.7 1.0 collective-permute-start.13
  91.0 2.1 collective-permute-done.12
  93.2 2.8 %collective-permute-done.14 = bf16[16,7168]{1,0:T(8,128)(2,1)S(1)} collective-permute-done((bf16[16,7168]{1,0:T(8,128)(2,1)}, bf16[16,7168]{1,0:T(8,128)(2,1)S(1)}, u32[]{:S(2)}, u32[]{:S(2)}) %collective-permute-start.14) | collective-permute-done | bytes 229408 | tf_op jit(solution)/shard_map/ppermute | solution.py:348
  96.0 0.7 copy-done.16
  97.3 2.0 fusion.11
  100.3 0.7 gather_fusion.1
  101.0 9.9 %collective-permute-done.15 = bf16[2,8,7168]{2,1,0:T(8,128)(2,1)S(1)} collective-permute-done((bf16[2,8,7168]{2,1,0:T(8,128)(2,1)}, bf16[2,8,7168]{2,1,0:T(8,128)(2,1)S(1)}, u32[]{:S(2)}, u32[]{:S(2)}) %collective-permute-start.15) | collective-permute-done | bytes 229408 | tf_op jit(solution)/shard_map/ppermute | solution.py:353
  111.7 1.3 rev.6
  113.4 0.7 gather_fusion.2
  114.2 4.1 %collective-permute-start.18 = (bf16[16,1792]{1,0:T(8,128)(2,1)S(1)}, bf16[16,1792]{1,0:T(8,128)(2,1)S(1)}, u32[]{:S(2)}, u32[]{:S(2)}) collective-permute-start(bf16[16,1792]{1,0:T(8,128)(2,1)S(1)} %get-tuple-element.38), channel_id=1, source_target_pairs={{0,64},{64,128},{128,192},{192,0},{1,65},{65,129},{129,193},{193,1... | collective-permute-start | bytes 172040 | tf_op jit(solution)/shard_map/ppermute | solution.py:81
  118.2 1.2 collective-permute-start.17
  120.1 3.3 %collective-permute-done.17 = bf16[16,1792]{1,0:T(8,128)(2,1)S(1)} collective-permute-done((bf16[16,1792]{1,0:T(8,128)(2,1)S(1)}, bf16[16,1792]{1,0:T(8,128)(2,1)S(1)}, u32[]{:S(2)}, u32[]{:S(2)}) %collective-permute-start.17) | collective-permute-done | bytes 57376 | tf_op jit(solution)/shard_map/ppermute | solution.py:81
  123.9 1.6 convolution_convert_fusion.4
  125.6 5.6 %all-to-all-start = ((bf16[16,24,1792]{2,1,0:T(8,128)(2,1)}), bf16[16,24,1792]{2,1,0:T(8,128)(2,1)S(1)}, u32[]{:S(2)}, u32[]{:S(2)}) async-start(bf16[16,24,1792]{2,1,0:T(8,128)(2,1)} %bitcast.97), calls=%async_computation | async-start | bytes 2752512 | tf_op jit(solution)/shard_map/all_to_all | solution.py:62
  131.3 14.8 %all-to-all-done = bf16[16,24,1792]{2,1,0:T(8,128)(2,1)S(1)} async-done(((bf16[16,24,1792]{2,1,0:T(8,128)(2,1)}), bf16[16,24,1792]{2,1,0:T(8,128)(2,1)S(1)}, u32[]{:S(2)}, u32[]{:S(2)}) %all-to-all-start) | async-done | bytes 1376288 | tf_op jit(solution)/shard_map/all_to_all | solution.py:62
  146.1 6.0 %shard_map.170 = (bf16[96,2048]{1,0:T(8,128)(2,1)S(1)}, bf16[96,2048]{1,0:T(8,128)(2,1)S(1)}, bf16[96,2048]{1,0:T(8,128)(2,1)S(1)}, bf16[96,2048]{1,0:T(8,128)(2,1)S(1)}) custom-call(s32[1]{0:T(128)} %bitcast.17.line_ref, bf16[384,1792]{1,0:T(8,128)(2,1)S(1)} %bitcast.88, bf16[896,1024]{1,0:T(8,128)(2,1)S(1)} %bitcast.90, bf16[896,1024]{1,0:T(8,128)(2,1)} %bitcast.99, ...), custom_call_target="tpu_custom_call" | custom-call | tf_op jit(solution)/shard_map/pallas_call | solution.py:236
  152.1 0.8 collective-permute-start.21
  152.9 2.7 %collective-permute-start.22 = (bf16[96,2048]{1,0:T(8,128)(2,1)S(1)}, bf16[96,2048]{1,0:T(8,128)(2,1)S(1)}, u32[]{:S(2)}, u32[]{:S(2)}) collective-permute-start(bf16[96,2048]{1,0:T(8,128)(2,1)S(1)} %get-tuple-element.24), channel_id=1, source_target_pairs={{0,128},{64,192},{128,0},{192,64},{1,129},{65,193},{129,1},{193,65... | collective-permute-start | bytes 1179656 | tf_op jit(solution)/shard_map/ppermute | solution.py:81
  155.6 1.9 collective-permute-start.23
  157.5 15.0 %collective-permute-done.21 = bf16[96,2048]{1,0:T(8,128)(2,1)S(1)} collective-permute-done((bf16[96,2048]{1,0:T(8,128)(2,1)S(1)}, bf16[96,2048]{1,0:T(8,128)(2,1)S(1)}, u32[]{:S(2)}, u32[]{:S(2)}) %collective-permute-start.21) | collective-permute-done | bytes 393248 | tf_op jit(solution)/shard_map/ppermute | solution.py:81
  172.5 6.3 %collective-permute-done.22 = bf16[96,2048]{1,0:T(8,128)(2,1)S(1)} collective-permute-done((bf16[96,2048]{1,0:T(8,128)(2,1)S(1)}, bf16[96,2048]{1,0:T(8,128)(2,1)S(1)}, u32[]{:S(2)}, u32[]{:S(2)}) %collective-permute-start.22) | collective-permute-done | bytes 393248 | tf_op jit(solution)/shard_map/ppermute | solution.py:81
  178.9 1.3 collective-permute-done.23
  180.6 2.2 collective-permute-start.25
  182.7 2.8 %collective-permute-start.24 = (bf16[96,1024]{1,0:T(8,128)(2,1)S(1)}, bf16[96,1024]{1,0:T(8,128)(2,1)S(1)}, u32[]{:S(2)}, u32[]{:S(2)}) collective-permute-start(bf16[96,1024]{1,0:T(8,128)(2,1)S(1)} %fusion.12.refs_0_), channel_id=1, source_target_pairs={{0,64},{64,128},{128,192},{192,0},{1,65},{65,129},{129,193},{193,1... | collective-permute-start | bytes 589832 | tf_op jit(solution)/shard_map/ppermute | solution.py:81
  185.6 9.0 %collective-permute-done.26.refs_3_ = bf16[96,1024]{1,0:T(8,128)(2,1)S(1)} collective-permute-done((bf16[96,1024]{1,0:T(8,128)(2,1)S(1)}, bf16[96,1024]{1,0:T(8,128)(2,1)S(1)}, u32[]{:S(2)}, u32[]{:S(2)}) %collective-permute-start.26) | collective-permute-done | bytes 196640 | tf_op jit(solution)/shard_map/ppermute | solution.py:81
  194.6 4.4 %shard_map.171 = bf16[384,1792]{1,0:T(8,128)(2,1)} custom-call(s32[1]{0:T(128)} %bitcast.17.line_ref, bf16[96,1024]{1,0:T(8,128)(2,1)S(1)} %fusion.12.refs_0_, bf16[96,1024]{1,0:T(8,128)(2,1)S(1)} %collective-permute-done.24.refs_1_, bf16[96,1024]{1,0:T(8,128)(2,1)S(1)} %collective-permute-done.25.refs_2_, ...), custom_call_target="tpu_custom_call" | custom-call | tf_op jit(solution)/shard_map/pallas_call | solution.py:236
  199.0 3.8 %all-to-all-start.1 = ((bf16[16,24,1792]{2,1,0:T(8,128)(2,1)}), bf16[16,24,1792]{2,1,0:T(8,128)(2,1)S(1)}, u32[]{:S(2)}, u32[]{:S(2)}) async-start(bf16[16,24,1792]{2,1,0:T(8,128)(2,1)} %bitcast.32), calls=%async_computation.1 | async-start | bytes 2752512 | tf_op jit(solution)/shard_map/all_to_all | solution.py:62
  203.1 18.1 %all-to-all-done.1 = bf16[16,24,1792]{2,1,0:T(8,128)(2,1)S(1)} async-done(((bf16[16,24,1792]{2,1,0:T(8,128)(2,1)}), bf16[16,24,1792]{2,1,0:T(8,128)(2,1)S(1)}, u32[]{:S(2)}, u32[]{:S(2)}) %all-to-all-start.1) | async-done | bytes 1376288 | tf_op jit(solution)/shard_map/all_to_all | solution.py:62
  221.6 1.1 fusion.7
  222.6 10.1 %all-to-all-start.2 = ((bf16[8,8,1792]{2,1,0:T(8,128)(2,1)}), bf16[8,8,1792]{2,1,0:T(8,128)(2,1)S(1)}, u32[]{:S(2)}, u32[]{:S(2)}) async-start(bf16[8,8,1792]{2,1,0:T(8,128)(2,1)} %fusion.7), calls=%async_computation.2 | async-start | bytes 458752 | tf_op jit(solution)/shard_map/all_to_all | solution.py:62
  233.4 7.7 %all-to-all-done.2 = bf16[8,8,1792]{2,1,0:T(8,128)(2,1)S(1)} async-done(((bf16[8,8,1792]{2,1,0:T(8,128)(2,1)}), bf16[8,8,1792]{2,1,0:T(8,128)(2,1)S(1)}, u32[]{:S(2)}, u32[]{:S(2)}) %all-to-all-start.2) | async-done | bytes 229408 | tf_op jit(solution)/shard_map/all_to_all | solution.py:62
  (142 shorter events, 16.8 us)
Async XLA Ops:
  0.6 26.2 %copy-start.18 = (bf16[256,64]{0,1:T(8,128)(2,1)S(1)}, bf16[256,64]{0,1:T(8,128)(2,1)}, u32[]{:S(2)}) copy-start(bf16[256,64]{0,1:T(8,128)(2,1)} %param.19) | copy-start | bytes 98308
  2.7 28.2 %collective-permute-start.5 = (bf16[8,32]{1,0:T(8,128)(2,1)}, bf16[8,32]{1,0:T(8,128)(2,1)}, u32[]{:S(2)}, u32[]{:S(2)}) collective-permute-start(bf16[8,32]{1,0:T(8,128)(2,1)} %pad_maximum_fusion.1), channel_id=1, source_target_pairs={{0,1},{1,0},{2,3},{3,2},{4,5},{5,4},{6,7},{7,6},{8,9},{9,8},{10,11... | collective-permute-start | bytes 1544 | tf_op jit(solution)/shard_map/ppermute | solution.py:303
  9.0 22.8 %collective-permute-start.4 = (bf16[64,512]{1,0:T(8,128)(2,1)}, bf16[64,512]{1,0:T(8,128)(2,1)S(1)}, u32[]{:S(2)}, u32[]{:S(2)}) collective-permute-start(bf16[64,512]{1,0:T(8,128)(2,1)} %bitcast.95), channel_id=1, source_target_pairs={{0,32},{32,0},{1,33},{33,1},{2,34},{34,2},{3,35},{35,3},{4,36},{36... | collective-permute-start | bytes 196616 | tf_op jit(solution)/shard_map/ppermute | solution.py:292
  9.0 27.3 %collective-permute-start.3 = (bf16[512,512]{1,0:T(8,128)(2,1)}, bf16[512,512]{1,0:T(8,128)(2,1)}, u32[]{:S(2)}, u32[]{:S(2)}) collective-permute-start(bf16[512,512]{1,0:T(8,128)(2,1)} %bitcast.93), channel_id=1, source_target_pairs={{0,32},{32,0},{1,33},{33,1},{2,34},{34,2},{3,35},{35,3},{4,36},{36... | collective-permute-start | bytes 1572872 | tf_op jit(solution)/shard_map/ppermute | solution.py:292
  10.8 1.0 copy-start
  11.8 0.8 copy-start.5
  12.7 14.2 %copy-start.3 = (bf16[256,512]{1,0:T(8,128)(2,1)S(1)}, bf16[256,512]{1,0:T(8,128)(2,1)}, u32[]{:S(2)}) copy-start(bf16[256,512]{1,0:T(8,128)(2,1)} %refs_7_.1) | copy-start | bytes 786436
  14.8 0.7 copy-start.8
  15.4 16.4 %collective-permute-start = (bf16[64,1152]{1,0:T(8,128)(2,1)}, bf16[64,1152]{1,0:T(8,128)(2,1)}, u32[]{:S(2)}, u32[]{:S(2)}) collective-permute-start(bf16[64,1152]{1,0:T(8,128)(2,1)} %get-tuple-element.15), channel_id=1, source_target_pairs={{0,64},{64,128},{128,192},{192,0},{1,65},{65,129},{129,193},{193,1... | collective-permute-start | bytes 442376 | tf_op jit(solution)/shard_map/ppermute | solution.py:81
  16.4 15.9 %collective-permute-start.1 = (bf16[64,1152]{1,0:T(8,128)(2,1)}, bf16[64,1152]{1,0:T(8,128)(2,1)}, u32[]{:S(2)}, u32[]{:S(2)}) collective-permute-start(bf16[64,1152]{1,0:T(8,128)(2,1)} %get-tuple-element.16), channel_id=1, source_target_pairs={{0,128},{64,192},{128,0},{192,64},{1,129},{65,193},{129,1},{193,65... | collective-permute-start | bytes 442376 | tf_op jit(solution)/shard_map/ppermute | solution.py:81
  21.5 8.6 %copy-start.17 = (bf16[8,7168]{1,0:T(8,128)(2,1)S(1)}, bf16[8,7168]{1,0:T(8,128)(2,1)}, u32[]{:S(2)}) copy-start(bf16[8,7168]{1,0:T(8,128)(2,1)} %param.25) | copy-start | bytes 344068
  21.5 10.2 %copy-start.1 = (bf16[1,896,1024]{2,1,0:T(8,128)(2,1)S(1)}, bf16[1,896,1024]{2,1,0:T(8,128)(2,1)}, u32[]{:S(2)}) copy-start(bf16[1,896,1024]{2,1,0:T(8,128)(2,1)} %param.29) | copy-start | bytes 5505028
  21.5 14.7 %copy-start.4 = (bf16[2,512,128]{2,1,0:T(8,128)(2,1)S(1)}, bf16[2,512,128]{2,1,0:T(8,128)(2,1)}, u32[]{:S(2)}) copy-start(bf16[2,512,128]{2,1,0:T(8,128)(2,1)} %refs_8_.3) | copy-start | bytes 786436
  21.6 14.7 %copy-start.6 = (bf16[1,512,512]{2,1,0:T(8,128)(2,1)S(1)}, bf16[1,512,512]{2,1,0:T(8,128)(2,1)}, u32[]{:S(2)}) copy-start(bf16[1,512,512]{2,1,0:T(8,128)(2,1)} %param.20) | copy-start | bytes 1572868
  21.6 14.7 %copy-start.7 = (bf16[1,64,512]{2,1,0:T(8,128)(2,1)S(1)}, bf16[1,64,512]{2,1,0:T(8,128)(2,1)}, u32[]{:S(2)}) copy-start(bf16[1,64,512]{2,1,0:T(8,128)(2,1)} %param.21) | copy-start | bytes 196612
  30.9 5.4 %collective-permute-start.2 = (bf16[64,1152]{1,0:T(8,128)(2,1)}, bf16[64,1152]{1,0:T(8,128)(2,1)S(1)}, u32[]{:S(2)}, u32[]{:S(2)}) collective-permute-start(bf16[64,1152]{1,0:T(8,128)(2,1)} %copy-done.8), channel_id=1, source_target_pairs={{0,192},{64,0},{128,64},{192,128},{1,193},{65,1},{129,65},{193,129... | collective-permute-start | bytes 442376 | tf_op jit(solution)/shard_map/ppermute | solution.py:81
  31.8 99.5 %collective-permute-start.19 = (bf16[896,1024]{1,0:T(8,128)(2,1)S(1)}, bf16[896,1024]{1,0:T(8,128)(2,1)}, u32[]{:S(2)}, u32[]{:S(2)}) collective-permute-start(bf16[896,1024]{1,0:T(8,128)(2,1)S(1)} %bitcast.89), channel_id=1, source_target_pairs={{0,32},{32,0},{1,33},{33,1},{2,34},{34,2},{3,35},{35,3},{4,36},{36... | collective-permute-start | bytes 5505032 | tf_op jit(solution)/shard_map/ppermute | solution.py:292
  31.9 99.4 %collective-permute-start.20 = (bf16[896,1024]{1,0:T(8,128)(2,1)}, bf16[896,1024]{1,0:T(8,128)(2,1)}, u32[]{:S(2)}, u32[]{:S(2)}) collective-permute-start(bf16[896,1024]{1,0:T(8,128)(2,1)} %bitcast.98), channel_id=1, source_target_pairs={{0,32},{32,0},{1,33},{33,1},{2,34},{34,2},{3,35},{35,3},{4,36},{36... | collective-permute-start | bytes 5505032 | tf_op jit(solution)/shard_map/ppermute | solution.py:292
  40.0 5.5 %collective-permute-start.6 = (bf16[64,384]{1,0:T(8,128)(2,1)S(1)}, bf16[64,384]{1,0:T(8,128)(2,1)S(1)}, u32[]{:S(2)}, u32[]{:S(2)}) collective-permute-start(bf16[64,384]{1,0:T(8,128)(2,1)S(1)} %get-tuple-element.19), channel_id=1, source_target_pairs={{0,192},{64,0},{128,64},{192,128},{1,193},{65,1},{129,65},{193,129... | collective-permute-start | bytes 147464 | tf_op jit(solution)/shard_map/ppermute | solution.py:81
  40.4 5.5 %collective-permute-start.7 = (bf16[64,384]{1,0:T(8,128)(2,1)S(1)}, bf16[64,384]{1,0:T(8,128)(2,1)S(1)}, u32[]{:S(2)}, u32[]{:S(2)}) collective-permute-start(bf16[64,384]{1,0:T(8,128)(2,1)S(1)} %get-tuple-element.20), channel_id=1, source_target_pairs={{0,128},{64,192},{128,0},{192,64},{1,129},{65,193},{129,1},{193,65... | collective-permute-start | bytes 147464 | tf_op jit(solution)/shard_map/ppermute | solution.py:81
  42.6 4.6 %collective-permute-start.8 = (bf16[64,384]{1,0:T(8,128)(2,1)S(1)}, bf16[64,384]{1,0:T(8,128)(2,1)S(1)}, u32[]{:S(2)}, u32[]{:S(2)}) collective-permute-start(bf16[64,384]{1,0:T(8,128)(2,1)S(1)} %get-tuple-element.21), channel_id=1, source_target_pairs={{0,64},{64,128},{128,192},{192,0},{1,65},{65,129},{129,193},{193,1... | collective-permute-start | bytes 147464 | tf_op jit(solution)/shard_map/ppermute | solution.py:81
  48.1 3.9 %copy-start.9 = (bf16[256,7168]{1,0:T(8,128)(2,1)S(1)}, bf16[256,7168]{1,0:T(8,128)(2,1)}, u32[]{:S(2)}) copy-start(bf16[256,7168]{1,0:T(8,128)(2,1)} %param.24) | copy-start | bytes 11010052
  53.7 9.1 %copy-start.23 = (pred[64]{0:T(512)(128)(4,1)S(1)}, pred[64]{0:T(512)(128)(4,1)}, u32[]{:S(2)}) copy-start(pred[64]{0:T(512)(128)(4,1)} %broadcast_in_dim.103) | copy-start | bytes 196
  55.4 15.3 %collective-permute-start.9 = (bf16[64,7168]{1,0:T(8,128)(2,1)}, bf16[64,7168]{1,0:T(8,128)(2,1)}, u32[]{:S(2)}, u32[]{:S(2)}) collective-permute-start(bf16[64,7168]{1,0:T(8,128)(2,1)} %convolution_convert_fusion.2), channel_id=1, source_target_pairs={{0,16},{1,17},{2,18},{3,19},{4,20},{5,21},{6,22},{7,23},{8,24},{9,... | collective-permute-start | bytes 2752520 | tf_op jit(solution)/shard_map/ppermute | solution.py:346
  58.5 22.0 %collective-permute-start.10 = (bf16[64,7168]{1,0:T(8,128)(2,1)}, bf16[64,7168]{1,0:T(8,128)(2,1)}, u32[]{:S(2)}, u32[]{:S(2)}) collective-permute-start(bf16[64,7168]{1,0:T(8,128)(2,1)} %convolution_convert_fusion.1), channel_id=1, source_target_pairs={{0,8},{1,9},{2,10},{3,11},{4,12},{5,13},{6,14},{7,15},{8,16},{9,17... | collective-permute-start | bytes 2752520 | tf_op jit(solution)/shard_map/ppermute | solution.py:346
  59.1 21.6 %collective-permute-start.11 = (bf16[64,7168]{1,0:T(8,128)(2,1)}, bf16[64,7168]{1,0:T(8,128)(2,1)}, u32[]{:S(2)}, u32[]{:S(2)}) collective-permute-start(bf16[64,7168]{1,0:T(8,128)(2,1)} %convolution_convert_fusion), channel_id=1, source_target_pairs={{0,24},{1,25},{2,26},{3,27},{4,28},{5,29},{6,30},{7,31},{8,0},{9,1... | collective-permute-start | bytes 2752520 | tf_op jit(solution)/shard_map/ppermute | solution.py:346
  62.8 27.9 %copy-start.21 = (s32[16]{0:T(128)S(1)}, s32[16]{0:T(128)}, u32[]{:S(2)}) copy-start(s32[16]{0:T(128)} %multiply_add_fusion) | copy-start | bytes 196
  62.8 34.5 %copy-start.12 = (f32[8,7168]{1,0:T(8,128)S(1)}, f32[8,7168]{1,0:T(8,128)}, u32[]{:S(2)}) copy-start(f32[8,7168]{1,0:T(8,128)} %convert_element_type.176) | copy-start | bytes 688132
  62.8 34.4 %copy-start.20 = (pred[2]{0:T(512)(128)(4,1)S(1)}, pred[2]{0:T(512)(128)(4,1)}, u32[]{:S(2)}) copy-start(pred[2]{0:T(512)(128)(4,1)} %iota_compare_fusion.6) | copy-start | bytes 10
  85.4 7.7 %collective-permute-start.12 = (bf16[16,7168]{1,0:T(8,128)(2,1)}, bf16[16,7168]{1,0:T(8,128)(2,1)S(1)}, u32[]{:S(2)}, u32[]{:S(2)}) collective-permute-start(bf16[16,7168]{1,0:T(8,128)(2,1)} %get-tuple-element.32), channel_id=1, source_target_pairs={{0,4},{1,5},{2,6},{3,7},{4,0},{5,1},{6,2},{7,3},{8,12},{9,13},{10,... | collective-permute-start | bytes 688136 | tf_op jit(solution)/shard_map/ppermute | solution.py:348
  88.6 7.3 %collective-permute-start.14 = (bf16[16,7168]{1,0:T(8,128)(2,1)}, bf16[16,7168]{1,0:T(8,128)(2,1)S(1)}, u32[]{:S(2)}, u32[]{:S(2)}) collective-permute-start(bf16[16,7168]{1,0:T(8,128)(2,1)} %get-tuple-element.33), channel_id=1, source_target_pairs={{0,6},{1,7},{2,0},{3,1},{4,2},{5,3},{6,4},{7,5},{8,14},{9,15},{10,... | collective-permute-start | bytes 688136 | tf_op jit(solution)/shard_map/ppermute | solution.py:348
  89.7 7.5 %collective-permute-start.13 = (bf16[16,7168]{1,0:T(8,128)(2,1)}, bf16[16,7168]{1,0:T(8,128)(2,1)}, u32[]{:S(2)}, u32[]{:S(2)}) collective-permute-start(bf16[16,7168]{1,0:T(8,128)(2,1)} %get-tuple-element.34), channel_id=1, source_target_pairs={{0,2},{1,3},{2,4},{3,5},{4,6},{5,7},{6,0},{7,1},{8,10},{9,11},{10,... | collective-permute-start | bytes 688136 | tf_op jit(solution)/shard_map/ppermute | solution.py:348
  93.2 2.8 %copy-start.15 = (bf16[16,7168]{1,0:T(8,128)(2,1)}, bf16[16,7168]{1,0:T(8,128)(2,1)S(1)}, u32[]{:S(2)}) copy-start(bf16[16,7168]{1,0:T(8,128)(2,1)S(1)} %collective-permute-done.12) | copy-start | bytes 688132
  96.0 0.7 copy-start.16
  99.3 12.1 %copy-start.10 = (f32[2,8,7168]{2,1,0:T(8,128)}, f32[2,8,7168]{2,1,0:T(8,128)S(1)}, u32[]{:S(2)}) copy-start(f32[2,8,7168]{2,1,0:T(8,128)S(1)} %get-tuple-element.31) | copy-start | bytes 1376260
  99.3 11.9 %copy-start.19 = (f32[7168]{0:T(1024)S(1)}, f32[7168]{0:T(1024)}, u32[]{:S(2)}) copy-start(f32[7168]{0:T(1024)} %param.26) | copy-start | bytes 86020
  99.3 11.6 %collective-permute-start.15 = (bf16[2,8,7168]{2,1,0:T(8,128)(2,1)}, bf16[2,8,7168]{2,1,0:T(8,128)(2,1)S(1)}, u32[]{:S(2)}, u32[]{:S(2)}) collective-permute-start(bf16[2,8,7168]{2,1,0:T(8,128)(2,1)} %get-tuple-element.30), channel_id=1, source_target_pairs={{0,1},{1,0},{2,3},{3,2},{4,5},{5,4},{6,7},{7,6},{8,9},{9,8},{10,11... | collective-permute-start | bytes 688136 | tf_op jit(solution)/shard_map/ppermute | solution.py:353
  110.9 2.3 copy-start.13
  111.1 2.9 %copy-start.24 = (pred[4]{0:T(512)(128)(4,1)S(1)}, pred[4]{0:T(512)(128)(4,1)}, u32[]{:S(2)}) copy-start(pred[4]{0:T(512)(128)(4,1)} %compare_and_fusion) | copy-start | bytes 16
  111.5 8.3 %copy-start.22 = (pred[64]{0:T(512)(128)(4,1)S(1)}, pred[64]{0:T(512)(128)(4,1)}, u32[]{:S(2)}) copy-start(pred[64]{0:T(512)(128)(4,1)} %broadcast_in_dim.112) | copy-start | bytes 196
  114.2 5.9 %collective-permute-start.18 = (bf16[16,1792]{1,0:T(8,128)(2,1)S(1)}, bf16[16,1792]{1,0:T(8,128)(2,1)S(1)}, u32[]{:S(2)}, u32[]{:S(2)}) collective-permute-start(bf16[16,1792]{1,0:T(8,128)(2,1)S(1)} %get-tuple-element.38), channel_id=1, source_target_pairs={{0,64},{64,128},{128,192},{192,0},{1,65},{65,129},{129,193},{193,1... | collective-permute-start | bytes 172040 | tf_op jit(solution)/shard_map/ppermute | solution.py:81
  118.2 5.1 %collective-permute-start.17 = (bf16[16,1792]{1,0:T(8,128)(2,1)S(1)}, bf16[16,1792]{1,0:T(8,128)(2,1)S(1)}, u32[]{:S(2)}, u32[]{:S(2)}) collective-permute-start(bf16[16,1792]{1,0:T(8,128)(2,1)S(1)} %get-tuple-element.39), channel_id=1, source_target_pairs={{0,128},{64,192},{128,0},{192,64},{1,129},{65,193},{129,1},{193,65... | collective-permute-start | bytes 172040 | tf_op jit(solution)/shard_map/ppermute | solution.py:81
  119.5 4.4 %collective-permute-start.16 = (bf16[16,1792]{1,0:T(8,128)(2,1)S(1)}, bf16[16,1792]{1,0:T(8,128)(2,1)S(1)}, u32[]{:S(2)}, u32[]{:S(2)}) collective-permute-start(bf16[16,1792]{1,0:T(8,128)(2,1)S(1)} %get-tuple-element.40), channel_id=1, source_target_pairs={{0,192},{64,0},{128,64},{192,128},{1,193},{65,1},{129,65},{193,129... | collective-permute-start | bytes 172040 | tf_op jit(solution)/shard_map/ppermute | solution.py:81
  125.6 20.5 %all-to-all-start = ((bf16[16,24,1792]{2,1,0:T(8,128)(2,1)}), bf16[16,24,1792]{2,1,0:T(8,128)(2,1)S(1)}, u32[]{:S(2)}, u32[]{:S(2)}) async-start(bf16[16,24,1792]{2,1,0:T(8,128)(2,1)} %bitcast.97), calls=%async_computation | async-start | bytes 2752512 | tf_op jit(solution)/shard_map/all_to_all | solution.py:62
  131.1 54.4 %collective-permute-start.27 = (bf16[1024,896]{1,0:T(8,128)(2,1)}, bf16[1024,896]{1,0:T(8,128)(2,1)}, u32[]{:S(2)}, u32[]{:S(2)}) collective-permute-start(bf16[1024,896]{1,0:T(8,128)(2,1)} %bitcast.91), channel_id=1, source_target_pairs={{0,32},{32,0},{1,33},{33,1},{2,34},{34,2},{3,35},{35,3},{4,36},{36... | collective-permute-start | bytes 5505032 | tf_op jit(solution)/shard_map/ppermute | solution.py:292
  152.1 42.5 %copy-start.2 = (bf16[1,1024,896]{2,1,0:T(8,128)(2,1)S(1)}, bf16[1,1024,896]{2,1,0:T(8,128)(2,1)}, u32[]{:S(2)}) copy-start(bf16[1,1024,896]{2,1,0:T(8,128)(2,1)} %param.31) | copy-start | bytes 5505028
  152.1 20.4 %collective-permute-start.21 = (bf16[96,2048]{1,0:T(8,128)(2,1)S(1)}, bf16[96,2048]{1,0:T(8,128)(2,1)S(1)}, u32[]{:S(2)}, u32[]{:S(2)}) collective-permute-start(bf16[96,2048]{1,0:T(8,128)(2,1)S(1)} %get-tuple-element.23), channel_id=1, source_target_pairs={{0,64},{64,128},{128,192},{192,0},{1,65},{65,129},{129,193},{193,1... | collective-permute-start | bytes 1179656 | tf_op jit(solution)/shard_map/ppermute | solution.py:81
  152.9 26.0 %collective-permute-start.22 = (bf16[96,2048]{1,0:T(8,128)(2,1)S(1)}, bf16[96,2048]{1,0:T(8,128)(2,1)S(1)}, u32[]{:S(2)}, u32[]{:S(2)}) collective-permute-start(bf16[96,2048]{1,0:T(8,128)(2,1)S(1)} %get-tuple-element.24), channel_id=1, source_target_pairs={{0,128},{64,192},{128,0},{192,64},{1,129},{65,193},{129,1},{193,65... | collective-permute-start | bytes 1179656 | tf_op jit(solution)/shard_map/ppermute | solution.py:81
  155.6 24.6 %collective-permute-start.23 = (bf16[96,2048]{1,0:T(8,128)(2,1)S(1)}, bf16[96,2048]{1,0:T(8,128)(2,1)S(1)}, u32[]{:S(2)}, u32[]{:S(2)}) collective-permute-start(bf16[96,2048]{1,0:T(8,128)(2,1)S(1)} %get-tuple-element.25), channel_id=1, source_target_pairs={{0,192},{64,0},{128,64},{192,128},{1,193},{65,1},{129,65},{193,129... | collective-permute-start | bytes 1179656 | tf_op jit(solution)/shard_map/ppermute | solution.py:81
  180.5 14.1 %collective-permute-start.26 = (bf16[96,1024]{1,0:T(8,128)(2,1)S(1)}, bf16[96,1024]{1,0:T(8,128)(2,1)S(1)}, u32[]{:S(2)}, u32[]{:S(2)}) collective-permute-start(bf16[96,1024]{1,0:T(8,128)(2,1)S(1)} %fusion.12.refs_0_), channel_id=1, source_target_pairs={{0,192},{64,0},{128,64},{192,128},{1,193},{65,1},{129,65},{193,129... | collective-permute-start | bytes 589832 | tf_op jit(solution)/shard_map/ppermute | solution.py:81
  180.6 14.0 %collective-permute-start.25 = (bf16[96,1024]{1,0:T(8,128)(2,1)S(1)}, bf16[96,1024]{1,0:T(8,128)(2,1)S(1)}, u32[]{:S(2)}, u32[]{:S(2)}) collective-permute-start(bf16[96,1024]{1,0:T(8,128)(2,1)S(1)} %fusion.12.refs_0_), channel_id=1, source_target_pairs={{0,128},{64,192},{128,0},{192,64},{1,129},{65,193},{129,1},{193,65... | collective-permute-start | bytes 589832 | tf_op jit(solution)/shard_map/ppermute | solution.py:81
  182.7 11.9 %collective-permute-start.24 = (bf16[96,1024]{1,0:T(8,128)(2,1)S(1)}, bf16[96,1024]{1,0:T(8,128)(2,1)S(1)}, u32[]{:S(2)}, u32[]{:S(2)}) collective-permute-start(bf16[96,1024]{1,0:T(8,128)(2,1)S(1)} %fusion.12.refs_0_), channel_id=1, source_target_pairs={{0,64},{64,128},{128,192},{192,0},{1,65},{65,129},{129,193},{193,1... | collective-permute-start | bytes 589832 | tf_op jit(solution)/shard_map/ppermute | solution.py:81
  199.0 4.0 %copy-start.14 = (bf16[2,8,7168]{2,1,0:T(8,128)(2,1)S(1)}, bf16[2,8,7168]{2,1,0:T(8,128)(2,1)}, u32[]{:S(2)}) copy-start(bf16[2,8,7168]{2,1,0:T(8,128)(2,1)} %copy-done.13) | copy-start | bytes 688132
  199.0 22.1 %all-to-all-start.1 = ((bf16[16,24,1792]{2,1,0:T(8,128)(2,1)}), bf16[16,24,1792]{2,1,0:T(8,128)(2,1)S(1)}, u32[]{:S(2)}, u32[]{:S(2)}) async-start(bf16[16,24,1792]{2,1,0:T(8,128)(2,1)} %bitcast.32), calls=%async_computation.1 | async-start | bytes 2752512 | tf_op jit(solution)/shard_map/all_to_all | solution.py:62
  221.2 11.5 %copy-start.11 = (f32[2,8,7168]{2,1,0:T(8,128)S(1)}, f32[2,8,7168]{2,1,0:T(8,128)}, u32[]{:S(2)}) copy-start(f32[2,8,7168]{2,1,0:T(8,128)} %copy-done.10) | copy-start | bytes 1376260
  222.6 18.4 %all-to-all-start.2 = ((bf16[8,8,1792]{2,1,0:T(8,128)(2,1)}), bf16[8,8,1792]{2,1,0:T(8,128)(2,1)S(1)}, u32[]{:S(2)}, u32[]{:S(2)}) async-start(bf16[8,8,1792]{2,1,0:T(8,128)(2,1)} %fusion.7), calls=%async_computation.2 | async-start | bytes 458752 | tf_op jit(solution)/shard_map/all_to_all | solution.py:62

commit v4 on v3

--- a/solution.py
+++ b/solution.py
@@ -15,6 +15,7 @@
 CAP = 3
 ROWS = 8
 LINE_ORDER = (2, 1, 3)
+UP_STEPS = 4
 
 SIDE = 4
 LINES = 4
@@ -180,7 +181,8 @@
 
 def merge_kernel(heads, *refs):
     back_refs = refs[:LINES]
-    place_ref, order_ref, self_score_ref, self_latent_ref, w_uv_ref, out_ref = refs[LINES:]
+    place_ref, order_ref, self_score_ref, self_latent_ref, w_uv_ref, w_out_ref = refs[LINES:-SIDE]
+    out_refs = refs[-SIDE:]
     back = jnp.concatenate([ref[...] for ref in back_refs], axis=0)
     samples = back.shape[0]
     to_place = place_ref[...] == lax.broadcasted_iota(jnp.int32, (samples, samples), 0)
@@ -196,49 +198,121 @@
         own_value = dot(self_latent_ref[...], w_uv_ref[head])
         mixed = cache_part * back[:, head * VD : (head + 1) * VD] + self_part * own_value
         values.append((mixed / (cache_part + self_part)).astype(BF))
-    out_ref[...] = dot(order_ref[...], jnp.concatenate(values, axis=1)).astype(BF)
+    rows = dot(order_ref[...], jnp.concatenate(values, axis=1)).astype(BF)
+    width = w_out_ref.shape[1] // LINES
+    for part in range(LINES):
+        columns = slice(part * width, (part + 1) * width)
+        total = dot(rows, w_out_ref[:, columns]).astype(BF)
+        for k, out_ref in enumerate(out_refs):
+            each = out_ref.shape[0]
+            out_ref[:, columns] = total[k * each : (k + 1) * each]
+
+
+def own_rows(half, rows):
+    return jnp.where(half == 0, rows[:ROWS], rows[ROWS:])
+
+
+def with_own(half, rows, residual):
+    first = jnp.where(half == 0, residual, 0.0)
+    return rows + jnp.concatenate([first, residual - first], axis=0)
+
+
+def near_kernel(half_ref, *refs):
+    part_refs, residual_ref, near_ref, out_ref = refs[:SIDE], refs[SIDE], refs[-2], refs[-1]
+    near = sum_wide([ref[...] for ref in part_refs])
+    near_ref[...] = near
+    out_ref[...] = with_own(half_ref[0], near, residual_ref[...].astype(F32)).astype(BF)
+
+
+def norm_kernel(half_ref, line_ref, core_ref, near_ref, far_ref, residual_ref, gain_ref, *refs):
+    attn_ref, out_refs, scratch = refs[0], refs[1:-1], refs[-1]
+    half, line, core = half_ref[0], line_ref[0], core_ref[0]
+    total = near_ref[...] + far_ref[...].astype(F32)
+    attn_ref[...] = own_rows(half, total).astype(BF)
+    mixed = with_own(half, total, residual_ref[...].astype(F32))
+    scale = lax.rsqrt(jnp.mean(mixed * mixed, axis=-1, keepdims=True) + NORM_EPS)
+    scratch[...] = (mixed * scale * gain_ref[...]).astype(BF)
+    share = scratch.shape[1] // GROUPS
+    for k, out_ref in enumerate(out_refs):
+        chip = lax.rem(line + LINES - k, LINES) * CORES
+        for side in range(CORES):
+            at = pl.multiple_of((chip + (core + side) % CORES) * share, share)
+            out_ref[:, side * share : (side + 1) * share] = scratch[:, pl.ds(at, share)]
 
 
 def up_kernel(line_ref, rows_ref, *refs):
-    w_refs, out_refs = refs[: 2 * CORES], refs[2 * CORES :]
+    w_refs, out_refs, rows_scratch = refs[: 2 * CORES], refs[2 * CORES : -1], refs[-1]
     each = rows_ref.shape[0] // LINES
     share = rows_ref.shape[1] // CORES
-    line = line_ref[0]
-    rows = []
-    for k in range(LINES):
-        at = pl.multiple_of(lax.rem(line + k, LINES) * each, each)
-        rows.append(rows_ref[pl.ds(at, each), :])
-    rows = jnp.concatenate(rows, axis=0)
+    step = pl.program_id(0)
+
+    @pl.when(step == 0)
+    def _():
+        line = line_ref[0]
+        for k in range(LINES):
+            at = pl.multiple_of(lax.rem(line + k, LINES) * each, each)
+            rows_scratch[k * each : (k + 1) * each, :] = rows_ref[pl.ds(at, each), :]
+
+    rows = rows_scratch[...]
     for half in range(2):
         total = dot(rows[:, :share], w_refs[half][...]) + dot(rows[:, share:], w_refs[2 + half][...])
         total = total.astype(BF)
         width = total.shape[1]
+        at = pl.multiple_of((half * pl.num_programs(0) + step) * width, width)
         for k, out_ref in enumerate(out_refs):
-            out_ref[:, half * width : (half + 1) * width] = total[k * each : (k + 1) * each]
+            out_ref[:, pl.ds(at, width)] = total[k * each : (k + 1) * each]
 
 
 def down_kernel(line_ref, *refs):
-    hidden_refs, w_refs, out_ref = refs[:LINES], refs[LINES : LINES + CORES], refs[-1]
+    hidden_refs, w_refs, out_ref, total_ref = refs[:LINES], refs[LINES : LINES + CORES], refs[-2], refs[-1]
     each = hidden_refs[0].shape[0]
-    line = line_ref[0]
-    hidden = jnp.concatenate([ref[...] for ref in hidden_refs], axis=0)
+    step = pl.program_id(0)
+    depth = w_refs[0].shape[0]
+    width = w_refs[0].shape[1]
+    at = pl.multiple_of(step * depth, depth)
+    hidden = jnp.concatenate([ref[:, pl.ds(at, depth)] for ref in hidden_refs], axis=0)
     for core in range(CORES):
-        total = dot(hidden, w_refs[core][...]).astype(BF)
-        width = total.shape[1]
-        for k in range(LINES):
-            at = pl.multiple_of(lax.rem(line + LINES - k, LINES) * each, each)
-            out_ref[pl.ds(at, each), core * width : (core + 1) * width] = total[k * each : (k + 1) * each]
-
-
-def on_chip(kernel, shapes, *args):
+        columns = slice(core * width, (core + 1) * width)
+        total = dot(hidden, w_refs[core][...])
+
+        @pl.when(step == 0)
+        def _():
+            total_ref[:, columns] = total
+
+        @pl.when(step == pl.num_programs(0) - 1)
+        def _():
+            line = line_ref[0]
+            whole = (total_ref[:, columns] + total).astype(BF)
+            for k in range(LINES):
+                at = pl.multiple_of(lax.rem(line + LINES - k, LINES) * each, each)
+                out_ref[pl.ds(at, each), columns] = whole[k * each : (k + 1) * each]
+
+
+def whole(shape):
+    return pl.BlockSpec(shape, lambda step: (0, 0))
+
+
+def column_block(one, count):
+    return pl.BlockSpec((one.shape[0], one.shape[1] // count), lambda step: (0, step))
+
+
+def row_block(one, count):
+    return pl.BlockSpec((one.shape[0] // count, one.shape[1]), lambda step: (step, 0))
+
+
+def on_chip(kernel, shapes, *args, dtypes=None, **more):
     vmem = pl.BlockSpec(memory_space=pltpu.VMEM)
     smem = pl.BlockSpec(memory_space=pltpu.SMEM)
+    more.setdefault("in_specs", [smem if one.shape == (1,) else vmem for one in args])
+    more.setdefault("out_specs", [vmem] * len(shapes))
     return pl.pallas_call(
         kernel,
-        out_shape=[jax.ShapeDtypeStruct(shape, BF) for shape in shapes],
-        in_specs=[smem if one.shape == (1,) else vmem for one in args],
-        out_specs=[vmem] * len(shapes),
+        out_shape=[
+            jax.ShapeDtypeStruct(shape, dtype)
+            for shape, dtype in zip(shapes, dtypes or [BF] * len(shapes))
+        ],
         compiler_params=pltpu.CompilerParams(vmem_limit_bytes=48 * 1024 * 1024),
+        **more,
     )(*args)
 
 
@@ -299,15 +373,7 @@
     keys = [cache_latent[0], sibling(cache_latent[0])]
     rope_keys = [cache_rope[0], sibling(cache_rope[0])]
 
-    own_table = jnp.concatenate([expert_ids.astype(BF), *split(gate_weight, 3)], axis=1)
-    other_table = lax.ppermute(own_table, "zhi", flips(HALVES, 1))
-    table = jnp.concatenate(
-        [
-            jnp.where(my_half == 0, own_table, other_table),
-            jnp.where(my_half == 0, other_table, own_table),
-        ],
-        axis=0,
-    )
+    table = jnp.concatenate([expert_ids.astype(BF), *split(gate_weight, 3)], axis=1)
     stats = 3 * heads
     table_pad = jnp.pad(
         table, ((0, each - table.shape[0]), (stats, VD - stats - table.shape[1]))
@@ -330,39 +396,49 @@
         for head in range(heads)
     ]
     self_score = jnp.stack(self_score, axis=1) * SCALE
-    (head_rows,) = on_chip(
+    first = on_chip(
         functools.partial(merge_kernel, heads),
-        [(samples, heads * VD)],
+        [(samples // SIDE, width)] * SIDE,
         *back,
         place,
         plane_order(my_core),
         self_score,
         self_latent,
         w_uv,
-    )
-
-    rows = head_rows.reshape(SIDE, samples // SIDE, -1)
-    first = [dot(rows[k], w_out).astype(BF) for k in range(SIDE)]
+        w_out,
+    )
     first = sum_wide([first[0]] + [lax.ppermute(first[k], ALL, plane_shift(k, 0)) for k in (2, 1, 3)])
     first = first.astype(BF).reshape(SIDE, HALVES * ROWS, width)
-    near = sum_wide([first[0]] + [lax.ppermute(first[k], ALL, plane_shift(k, 1)) for k in (2, 1, 3)])
-
-    near = near.reshape(HALVES, ROWS, width)
-    is_mine = (jnp.arange(HALVES) == my_half)[:, None, None]
-    with_residual = near + jnp.where(is_mine, residual.astype(F32)[None], 0.0)
-    far = lax.ppermute(with_residual.astype(BF), "zhi", flips(HALVES, 1)).astype(F32)
-    attn_proj = lax.dynamic_index_in_dim(near + far, my_half, 0, keepdims=False).astype(BF)
-    mixed = with_residual + far
-    normed = (
-        mixed * lax.rsqrt(jnp.mean(mixed * mixed, axis=-1, keepdims=True) + NORM_EPS) * norm_gain
-    ).astype(BF)
-
-    by_chip = normed.reshape(HALVES * ROWS, LINES, CORES, share)
-    by_chip = jnp.where(my_core == 0, by_chip, by_chip[:, :, ::-1]).reshape(-1, LINES, CORES * share)
-    by_chip = jnp.take(by_chip.transpose(1, 0, 2), (my_line + LINES - lines) % LINES, axis=0)
-    token_rows = jnp.concatenate(along_line([by_chip[k] for k in range(LINES)], -1), axis=0)
-
-    table = jnp.stack([one[: HALVES * ROWS, heads * VD + stats :] for one in back])
+    second = [first[0]] + [lax.ppermute(first[k], ALL, plane_shift(k, 1)) for k in (1, 2, 3)]
+    half = my_half.astype(jnp.int32).reshape(1)
+    near, outgoing = on_chip(
+        near_kernel,
+        [(HALVES * ROWS, width)] * 2,
+        half,
+        *second,
+        residual,
+        dtypes=[F32, BF],
+    )
+    far = lax.ppermute(outgoing, "zhi", flips(HALVES, 1))
+    attn_proj, *by_chip = on_chip(
+        norm_kernel,
+        [(ROWS, width)] + [(HALVES * ROWS, CORES * share)] * LINES,
+        half,
+        line,
+        my_core.astype(jnp.int32).reshape(1),
+        near,
+        far,
+        residual,
+        norm_gain.reshape(1, -1),
+        scratch_shapes=[pltpu.VMEM((HALVES * ROWS, width), BF)],
+    )
+
+    token_rows = jnp.concatenate(along_line(by_chip, -1), axis=0)
+
+    table = jnp.stack([one[:ROWS, heads * VD + stats : heads * VD + stats + 4 * top] for one in back])
+    other = lax.ppermute(table, "zhi", flips(HALVES, 1))
+    pair = [jnp.where(my_half == 0, table, other), jnp.where(my_half == 0, other, table)]
+    table = jnp.concatenate(pair, axis=1)
     table = jnp.take(table, (lines + LINES - my_line) % LINES, axis=0)
     table = table.reshape(tokens, -1).astype(F32)
     gates = table[:, top : 2 * top] + table[:, 2 * top : 3 * top] + table[:, 3 * top : 4 * top]
@@ -372,26 +448,35 @@
     rows_in = exchange(dot(routing, token_rows).astype(BF), XY)
 
     line_rows = rows_in.shape[0] // LINES
+    ups = [w_gate[0], w_up[0], sibling(w_gate[0]), sibling(w_up[0])]
+    scalar = pl.BlockSpec(memory_space=pltpu.SMEM)
+    out_shape = (line_rows, 2 * w_gate.shape[2])
     parts = on_chip(
         up_kernel,
-        [(line_rows, 2 * w_gate.shape[2])] * LINES,
+        [out_shape] * LINES,
         line,
         rows_in,
-        w_gate[0],
-        w_up[0],
-        sibling(w_gate[0]),
-        sibling(w_up[0]),
+        *ups,
+        grid=(UP_STEPS,),
+        in_specs=[scalar, whole(rows_in.shape)] + [column_block(one, UP_STEPS) for one in ups],
+        out_specs=[whole(out_shape)] * LINES,
+        scratch_shapes=[pltpu.VMEM(rows_in.shape, BF)],
     )
     sums = sum_wide(along_line(parts))
     ffe = sums.shape[1] // 2
     hidden = (jax.nn.silu(sums[:, :ffe]) * sums[:, ffe:]).astype(BF)
+    downs = [w_down[0], sibling(w_down[0])]
+    out_shape = (rows_in.shape[0], CORES * share)
     (expert_out,) = on_chip(
         down_kernel,
-        [(rows_in.shape[0], CORES * share)],
+        [out_shape],
         line,
         *along_line([hidden] * LINES),
-        w_down[0],
-        sibling(w_down[0]),
+        *downs,
+        grid=(2,),
+        in_specs=[scalar] + [whole(hidden.shape)] * LINES + [row_block(one, 2) for one in downs],
+        out_specs=[whole(out_shape)],
+        scratch_shapes=[pltpu.VMEM(out_shape, F32)],
     )
 
     returned = exchange(expert_out, XY)

time: 243 us -> 234 us (0.963)
  blocking collectives: 0 us -> 13.3 us
  starting transfers between devices: 63.9 us -> 51.8 us
  matrix products: 14.4 us -> 2.43 us
  Pallas kernels: 17.2 us -> 24.1 us
  other arithmetic: 13.8 us -> 7.79 us
  waiting for transfers between devices: 115 us -> 120 us
  local copies, waits for them, and re-layouts: 16.2 us -> 12.8 us
    ppermute x15, waiting for transfers between devices: 41.3 us -> 56.2 us  [along_line(): lax.ppermute(parts[k], 'zlo', shift(sign * k))]
    all_to_all x0 -> x1, blocking collectives: none -> 13.3 us  [exchange(): return lax.all_to_all(value, axes, 0, 0, tiled=True)]
    dot_general x5 -> x1, matrix products: 12.9 us -> 1.67 us  [dot(): return jnp.dot(a, b, preferred_element_type=F32)]
    all_to_all x3 -> x2, starting transfers between devices: 19.5 us -> 10.6 us  [exchange(): return lax.all_to_all(value, axes, 0, 0, tiled=True)]
    pallas_call x5 -> x7, Pallas kernels: 17.2 us -> 24.1 us  [on_chip(): pl.pallas_call(kernel, out_shape=[jax.ShapeDtypeStruct(shape, dtype) for...]
    ppermute x15, starting transfers between devices: 25 us -> 18.3 us  [along_line(): lax.ppermute(parts[k], 'zlo', shift(sign * k))]
    ppermute x2, starting transfers between devices: 6.83 us -> 11.7 us  [the longest x1 5.92 us: body(): other = lax.ppermute(table, 'zhi', flips(HALVES, 1))]
    all_to_all x3 -> x2, waiting for transfers between devices: 40.6 us -> 36.7 us  [exchange(): return lax.all_to_all(value, axes, 0, 0, tiled=True)]
  transfers between devices with their start and end apart: 31 -> 30, of which waited for: 20 -> 20; matrix products, arithmetic and copies ran while one was open for 15% -> 8% of each run, Pallas kernels for 5% -> 7%
where the time goes in v4:
time: 234 us; the launch traced here: 233 us
  waiting for transfers between devices  120 us (51%)
  starting transfers between devices  51.8 us (22%)
  Pallas kernels  24.1 us (10%)
  blocking collectives  13.3 us (6%)
  local copies, waits for them, and re-layouts  12.8 us (5%)
  other arithmetic  7.79 us (3%)
  matrix products  2.43 us (1%)
    ppermute x15, waiting for transfers between devices, along_line(): lax.ppermute(parts[k], 'zlo', shift(sign * k))  56.2 us
    all_to_all x2, waiting for transfers between devices, exchange(): return lax.all_to_all(value, axes, 0, 0, tiled=True)  36.7 us
    pallas_call x7, Pallas kernels, on_chip(): pl.pallas_call(kernel, out_shape=[jax.ShapeDtypeStruct(shape, dtype) for...  24.1 us
    ppermute x15, starting transfers between devices, along_line(): lax.ppermute(parts[k], 'zlo', shift(sign * k))  18.3 us
    ppermute x3, waiting for transfers between devices, body(): lax.ppermute(first[k], ALL, plane_shift(k, 0))  14.8 us
    all_to_all x1, blocking collectives, exchange(): return lax.all_to_all(value, axes, 0, 0, tiled=True)  13.3 us
    all_to_all x2, starting transfers between devices, exchange(): return lax.all_to_all(value, axes, 0, 0, tiled=True)  10.6 us
    ppermute x1, waiting for transfers between devices, body(): far = lax.ppermute(outgoing, 'zhi', flips(HALVES, 1))  6.85 us
  transfers between devices with their start and end apart: 30, of which 20 were waited for; matrix products, arithmetic and copies ran while one was open for 8% of the time, Pallas kernels for 7%

profile of v4, /device:TPU:32, one launch (start us, length us, event | category | flops | bytes accessed | tf_op | source)
XLA Modules:
  0.0 232.8 jit_solution(9235018205400408295)
XLA Ops:
  0.7 0.8 reshape.335
  2.0 1.0 copy-done
  3.0 0.8 copy-done.5
  3.9 2.1 shard_map.167
  6.0 1.9 collective-permute-start
  7.9 2.3 collective-permute-start.1
  10.2 1.1 collective-permute-start.2
  11.8 3.3 %fusion.65 = (bf16[256,1,512]{2,1,0:T(2,128)(2,1)}, bf16[256,1,512]{2,1,0:T(2,128)(2,1)}) fusion(bf16[256,2,512]{2,1,0:T(2,128)(2,1)} %q_latent_ref.1), kind=kLoop, calls=%fused_computation.159 | loop fusion | bytes 1048576 | tf_op jit(solution)/shard_map/slice | solution.py:394
  15.6 1.4 fusion.3
  17.0 0.8 fusion.23
  17.9 0.8 copy.62
  18.8 0.9 broadcast_multiply_fusion.refs_6_
  20.3 0.5 collective-permute-done.1.refs_2_
  20.8 2.1 collective-permute-done.2.refs_3_
  22.9 0.8 copy-done.9
  23.8 3.7 %shard_map.168 = (bf16[64,384]{1,0:T(8,128)(2,1)S(1)}, bf16[64,384]{1,0:T(8,128)(2,1)S(1)}, bf16[64,384]{1,0:T(8,128)(2,1)S(1)}, bf16[64,384]{1,0:T(8,128)(2,1)S(1)}) custom-call(bf16[64,1152]{1,0:T(8,128)(2,1)S(1)} %get-tuple-element.25.refs_0_, bf16[64,1152]{1,0:T(8,128)(2,1)S(1)} %collective-permute-done.refs_1_, ...), custom_call_target="tpu_custom_call" | custom-call | tf_op jit(solution)/shard_map/pallas_call | solution.py:308
  27.6 1.4 collective-permute-start.6
  29.0 1.9 collective-permute-start.5
  31.0 0.8 collective-permute-done.7.refs_3_
  31.8 1.1 collective-permute-done.6.refs_2_
  32.8 1.5 collective-permute-done.5.refs_1_
  34.3 5.6 %shard_map.169 = (bf16[64,7168]{1,0:T(8,128)(2,1)S(1)}, bf16[64,7168]{1,0:T(8,128)(2,1)}, bf16[64,7168]{1,0:T(8,128)(2,1)}, bf16[64,7168]{1,0:T(8,128)(2,1)}) custom-call(bf16[64,384]{1,0:T(8,128)(2,1)S(1)} %get-tuple-element.29.refs_0_, bf16[64,384]{1,0:T(8,128)(2,1)S(1)} %collective-permute-done.5.refs_1_, ...), custom_call_target="tpu_custom_call" | custom-call | tf_op jit(solution)/shard_map/pallas_call | solution.py:308
  40.0 2.8 %collective-permute-start.10 = (bf16[64,7168]{1,0:T(8,128)(2,1)}, bf16[64,7168]{1,0:T(8,128)(2,1)}, u32[]{:S(2)}, u32[]{:S(2)}) collective-permute-start(bf16[64,7168]{1,0:T(8,128)(2,1)} %get-tuple-element.36), channel_id=1, source_target_pairs={{0,24},{1,25},{2,26},{3,27},{4,28},{5,29},{6,30},{7,31},{8,0},{9,1... | collective-permute-start | bytes 2752520 | tf_op jit(solution)/shard_map/ppermute | solution.py:410
  42.7 0.8 collective-permute-start.8
  43.5 0.9 collective-permute-start.9
  44.6 5.9 %collective-permute-start.15 = (bf16[4,8,32]{2,1,0:T(8,128)(2,1)S(1)}, bf16[4,8,32]{2,1,0:T(8,128)(2,1)S(1)}, u32[]{:S(2)}, u32[]{:S(2)}) collective-permute-start(bf16[4,8,32]{2,1,0:T(8,128)(2,1)S(1)} %pad_maximum_fusion.1), channel_id=1, source_target_pairs={{0,1},{1,0},{2,3},{3,2},{4,5},{5,4},{6,7},{7,6},{8,9},{9,8},{10,11... | collective-permute-start | bytes 6152 | tf_op jit(solution)/shard_map/ppermute | solution.py:439
  50.6 0.7 broadcast_in_dim.65
  51.4 0.7 broadcast_in_dim.74
  52.3 0.6 gather_fusion
  53.0 10.8 %collective-permute-done.10 = bf16[64,7168]{1,0:T(8,128)(2,1)} collective-permute-done((bf16[64,7168]{1,0:T(8,128)(2,1)}, bf16[64,7168]{1,0:T(8,128)(2,1)}, u32[]{:S(2)}, u32[]{:S(2)}) %collective-permute-start.10) | collective-permute-done | bytes 917536 | tf_op jit(solution)/shard_map/ppermute | solution.py:410
  63.8 3.9 %collective-permute-done.9 = bf16[64,7168]{1,0:T(8,128)(2,1)} collective-permute-done((bf16[64,7168]{1,0:T(8,128)(2,1)}, bf16[64,7168]{1,0:T(8,128)(2,1)}, u32[]{:S(2)}, u32[]{:S(2)}) %collective-permute-start.9) | collective-permute-done | bytes 917536 | tf_op jit(solution)/shard_map/ppermute | solution.py:410
  67.8 2.2 add_convert_fusion
  70.0 0.7 fusion.64
  70.7 1.6 collective-permute-start.11
  72.3 2.9 %collective-permute-start.12 = (bf16[16,7168]{1,0:T(8,128)(2,1)S(1)}, bf16[16,7168]{1,0:T(8,128)(2,1)S(1)}, u32[]{:S(2)}, u32[]{:S(2)}) collective-permute-start(bf16[16,7168]{1,0:T(8,128)(2,1)S(1)} %get-tuple-element.53), channel_id=1, source_target_pairs={{0,4},{1,5},{2,6},{3,7},{4,0},{5,1},{6,2},{7,3},{8,12},{9,13},{10,... | collective-permute-start | bytes 688136 | tf_op jit(solution)/shard_map/ppermute | solution.py:412
  75.2 1.3 collective-permute-start.13
  76.9 1.2 collective-permute-done.11.refs_1_
  78.2 3.7 %collective-permute-done.12.refs_2_ = bf16[16,7168]{1,0:T(8,128)(2,1)S(1)} collective-permute-done((bf16[16,7168]{1,0:T(8,128)(2,1)S(1)}, bf16[16,7168]{1,0:T(8,128)(2,1)S(1)}, u32[]{:S(2)}, u32[]{:S(2)}) %collective-permute-start.12) | collective-permute-done | bytes 229408 | tf_op jit(solution)/shard_map/ppermute | solution.py:412
  81.9 0.8 shard_map.170
  82.7 5.8 %collective-permute-start.14 = (bf16[16,7168]{1,0:T(8,128)(2,1)}, bf16[16,7168]{1,0:T(8,128)(2,1)S(1)}, u32[]{:S(2)}, u32[]{:S(2)}) collective-permute-start(bf16[16,7168]{1,0:T(8,128)(2,1)} %get-tuple-element.38), channel_id=1, source_target_pairs={{0,1},{1,0},{2,3},{3,2},{4,5},{5,4},{6,7},{7,6},{8,9},{9,8},{10,11... | collective-permute-start | bytes 688136 | tf_op jit(solution)/shard_map/ppermute | solution.py:422
  89.0 0.6 gather_fusion.1
  89.6 6.8 %collective-permute-done.14.far_ref = bf16[16,7168]{1,0:T(8,128)(2,1)S(1)} collective-permute-done((bf16[16,7168]{1,0:T(8,128)(2,1)}, bf16[16,7168]{1,0:T(8,128)(2,1)S(1)}, u32[]{:S(2)}, u32[]{:S(2)}) %collective-permute-start.14) | collective-permute-done | bytes 229408 | tf_op jit(solution)/shard_map/ppermute | solution.py:422
  96.4 0.8 shard_map.171
  97.2 1.7 collective-permute-start.17
  99.5 1.9 collective-permute-done.16
  101.4 1.0 collective-permute-done.17
  102.4 1.1 collective-permute-done.18
  103.5 1.7 convolution_convert_fusion
  105.2 4.5 %all-to-all-start = ((bf16[16,24,1792]{2,1,0:T(8,128)(2,1)}), bf16[16,24,1792]{2,1,0:T(8,128)(2,1)S(1)}, u32[]{:S(2)}, u32[]{:S(2)}) async-start(bf16[16,24,1792]{2,1,0:T(8,128)(2,1)} %bitcast.79), calls=%async_computation | async-start | bytes 2752512 | tf_op jit(solution)/shard_map/all_to_all | solution.py:63
  110.0 18.6 %all-to-all-done = bf16[16,24,1792]{2,1,0:T(8,128)(2,1)S(1)} async-done(((bf16[16,24,1792]{2,1,0:T(8,128)(2,1)}), bf16[16,24,1792]{2,1,0:T(8,128)(2,1)S(1)}, u32[]{:S(2)}, u32[]{:S(2)}) %all-to-all-start) | async-done | bytes 1376288 | tf_op jit(solution)/shard_map/all_to_all | solution.py:63
  128.6 6.0 %shard_map.172 = (bf16[96,2048]{1,0:T(8,128)(2,1)S(1)}, bf16[96,2048]{1,0:T(8,128)(2,1)S(1)}, bf16[96,2048]{1,0:T(8,128)(2,1)S(1)}, bf16[96,2048]{1,0:T(8,128)(2,1)S(1)}) custom-call(s32[1]{0:T(128)} %bitcast.1.line_ref, bf16[384,1792]{1,0:T(8,128)(2,1)S(1)} %bitcast.69, bf16[896,1024]{1,0:T(8,128)(2,1)S(1)} %bitcast.71, bf16[896,1024]{1,0:T(8,128)(2,1)} %bitcast.81, ...), custom_call_target="tpu_custom_call" | custom-call | tf_op jit(solution)/shard_map/pallas_call | solution.py:308
  134.6 1.0 collective-permute-start.21
  135.5 4.4 %collective-permute-start.22 = (bf16[96,2048]{1,0:T(8,128)(2,1)S(1)}, bf16[96,2048]{1,0:T(8,128)(2,1)S(1)}, u32[]{:S(2)}, u32[]{:S(2)}) collective-permute-start(bf16[96,2048]{1,0:T(8,128)(2,1)S(1)} %get-tuple-element.46), channel_id=1, source_target_pairs={{0,128},{64,192},{128,0},{192,64},{1,129},{65,193},{129,1},{193,65... | collective-permute-start | bytes 1179656 | tf_op jit(solution)/shard_map/ppermute | solution.py:82
  139.9 21.2 %collective-permute-done.21 = bf16[96,2048]{1,0:T(8,128)(2,1)S(1)} collective-permute-done((bf16[96,2048]{1,0:T(8,128)(2,1)S(1)}, bf16[96,2048]{1,0:T(8,128)(2,1)S(1)}, u32[]{:S(2)}, u32[]{:S(2)}) %collective-permute-start.21) | collective-permute-done | bytes 393248 | tf_op jit(solution)/shard_map/ppermute | solution.py:82
  161.1 4.2 %collective-permute-done.22 = bf16[96,2048]{1,0:T(8,128)(2,1)S(1)} collective-permute-done((bf16[96,2048]{1,0:T(8,128)(2,1)S(1)}, bf16[96,2048]{1,0:T(8,128)(2,1)S(1)}, u32[]{:S(2)}, u32[]{:S(2)}) %collective-permute-start.22) | collective-permute-done | bytes 393248 | tf_op jit(solution)/shard_map/ppermute | solution.py:82
  165.3 8.4 %collective-permute-done.23 = bf16[96,2048]{1,0:T(8,128)(2,1)S(1)} collective-permute-done((bf16[96,2048]{1,0:T(8,128)(2,1)S(1)}, bf16[96,2048]{1,0:T(8,128)(2,1)S(1)}, u32[]{:S(2)}, u32[]{:S(2)}) %collective-permute-start.23) | collective-permute-done | bytes 393248 | tf_op jit(solution)/shard_map/ppermute | solution.py:82
  174.3 1.9 collective-permute-start.26
  176.2 10.2 %collective-permute-done.24.refs_1_ = bf16[96,1024]{1,0:T(8,128)(2,1)S(1)} collective-permute-done((bf16[96,1024]{1,0:T(8,128)(2,1)S(1)}, bf16[96,1024]{1,0:T(8,128)(2,1)S(1)}, u32[]{:S(2)}, u32[]{:S(2)}) %collective-permute-start.24) | collective-permute-done | bytes 196640 | tf_op jit(solution)/shard_map/ppermute | solution.py:82
  186.4 2.1 collective-permute-done.25.refs_2_
  188.5 5.0 %shard_map.173 = bf16[384,1792]{1,0:T(8,128)(2,1)} custom-call(s32[1]{0:T(128)} %bitcast.1.line_ref, bf16[96,1024]{1,0:T(8,128)(2,1)S(1)} %fusion.5.refs_0_, bf16[96,1024]{1,0:T(8,128)(2,1)S(1)} %collective-permute-done.24.refs_1_, bf16[96,1024]{1,0:T(8,128)(2,1)S(1)} %collective-permute-done.25.refs_2_, ...), custom_call_target="tpu_custom_call" | custom-call | tf_op jit(solution)/shard_map/pallas_call | solution.py:308
  193.5 6.2 %all-to-all-start.1 = ((bf16[16,24,1792]{2,1,0:T(8,128)(2,1)}), bf16[16,24,1792]{2,1,0:T(8,128)(2,1)S(1)}, u32[]{:S(2)}, u32[]{:S(2)}) async-start(bf16[16,24,1792]{2,1,0:T(8,128)(2,1)} %bitcast.27), calls=%async_computation.1 | async-start | bytes 2752512 | tf_op jit(solution)/shard_map/all_to_all | solution.py:63
  199.8 18.2 %all-to-all-done.1 = bf16[16,24,1792]{2,1,0:T(8,128)(2,1)S(1)} async-done(((bf16[16,24,1792]{2,1,0:T(8,128)(2,1)}), bf16[16,24,1792]{2,1,0:T(8,128)(2,1)S(1)}, u32[]{:S(2)}, u32[]{:S(2)}) %all-to-all-start.1) | async-done | bytes 1376288 | tf_op jit(solution)/shard_map/all_to_all | solution.py:63
  218.8 13.3 %all_to_all.29 = bf16[8,8,1792]{2,1,0:T(8,128)(2,1)S(1)} all-to-all(bf16[8,8,1792]{2,1,0:T(8,128)(2,1)S(1)} %fusion.2), channel_id=1, replica_groups=mesh['zlo'=4,'core'=2,'x'=4,'y'=4,'zhi'=2] {'zlo','zhi'}, dimensions={0} | all-to-all | bytes 458752 | tf_op jit(solution)/shard_map/all_to_all | solution.py:63
  232.1 0.7 reverse_select_fusion
  (98 shorter events, 6.1 us)
Async XLA Ops:
  0.6 14.5 %copy-start.6 = (bf16[256,128]{1,0:T(8,128)(2,1)S(1)}, bf16[256,128]{1,0:T(8,128)(2,1)}, u32[]{:S(2)}) copy-start(bf16[256,128]{1,0:T(8,128)(2,1)} %q_rope_ref.1) | copy-start | bytes 196612
  0.6 14.6 %copy-start.12 = (f32[8,8]{1,0:T(8,128)S(1)}, f32[8,8]{1,0:T(8,128)}, u32[]{:S(2)}) copy-start(f32[8,8]{1,0:T(8,128)} %param.28) | copy-start | bytes 772
  0.7 14.6 %copy-start.11 = (s32[8,8]{1,0:T(8,128)S(1)}, s32[8,8]{1,0:T(8,128)}, u32[]{:S(2)}) copy-start(s32[8,8]{1,0:T(8,128)} %param.27) | copy-start | bytes 772
  2.0 1.0 copy-start
  3.0 0.8 copy-start.5
  3.9 11.8 %copy-start.3 = (bf16[256,512]{1,0:T(8,128)(2,1)S(1)}, bf16[256,512]{1,0:T(8,128)(2,1)}, u32[]{:S(2)}) copy-start(bf16[256,512]{1,0:T(8,128)(2,1)} %refs_7_.1) | copy-start | bytes 786436
  6.0 14.3 %collective-permute-start = (bf16[64,1152]{1,0:T(8,128)(2,1)}, bf16[64,1152]{1,0:T(8,128)(2,1)S(1)}, u32[]{:S(2)}, u32[]{:S(2)}) collective-permute-start(bf16[64,1152]{1,0:T(8,128)(2,1)} %get-tuple-element.26), channel_id=1, source_target_pairs={{0,64},{64,128},{128,192},{192,0},{1,65},{65,129},{129,193},{193,1... | collective-permute-start | bytes 442376 | tf_op jit(solution)/shard_map/ppermute | solution.py:82
  7.9 12.9 %collective-permute-start.1 = (bf16[64,1152]{1,0:T(8,128)(2,1)}, bf16[64,1152]{1,0:T(8,128)(2,1)}, u32[]{:S(2)}, u32[]{:S(2)}) collective-permute-start(bf16[64,1152]{1,0:T(8,128)(2,1)} %get-tuple-element.27), channel_id=1, source_target_pairs={{0,128},{64,192},{128,0},{192,64},{1,129},{65,193},{129,1},{193,65... | collective-permute-start | bytes 442376 | tf_op jit(solution)/shard_map/ppermute | solution.py:82
  10.2 12.7 %collective-permute-start.2 = (bf16[64,1152]{1,0:T(8,128)(2,1)}, bf16[64,1152]{1,0:T(8,128)(2,1)}, u32[]{:S(2)}, u32[]{:S(2)}) collective-permute-start(bf16[64,1152]{1,0:T(8,128)(2,1)} %get-tuple-element.28), channel_id=1, source_target_pairs={{0,192},{64,0},{128,64},{192,128},{1,193},{65,1},{129,65},{193,129... | collective-permute-start | bytes 442376 | tf_op jit(solution)/shard_map/ppermute | solution.py:82
  11.3 11.6 %collective-permute-start.3 = (bf16[512,512]{1,0:T(8,128)(2,1)}, bf16[512,512]{1,0:T(8,128)(2,1)}, u32[]{:S(2)}, u32[]{:S(2)}) collective-permute-start(bf16[512,512]{1,0:T(8,128)(2,1)} %bitcast.74), channel_id=1, source_target_pairs={{0,32},{32,0},{1,33},{33,1},{2,34},{34,2},{3,35},{35,3},{4,36},{36... | collective-permute-start | bytes 1572872 | tf_op jit(solution)/shard_map/ppermute | solution.py:366
  11.3 9.0 %collective-permute-start.4 = (bf16[64,512]{1,0:T(8,128)(2,1)}, bf16[64,512]{1,0:T(8,128)(2,1)}, u32[]{:S(2)}, u32[]{:S(2)}) collective-permute-start(bf16[64,512]{1,0:T(8,128)(2,1)} %bitcast.76), channel_id=1, source_target_pairs={{0,32},{32,0},{1,33},{33,1},{2,34},{34,2},{3,35},{35,3},{4,36},{36... | collective-permute-start | bytes 196616 | tf_op jit(solution)/shard_map/ppermute | solution.py:366
  11.8 8.4 %copy-start.1 = (bf16[1,896,1024]{2,1,0:T(8,128)(2,1)S(1)}, bf16[1,896,1024]{2,1,0:T(8,128)(2,1)}, u32[]{:S(2)}) copy-start(bf16[1,896,1024]{2,1,0:T(8,128)(2,1)} %param.29) | copy-start | bytes 5505028
  11.8 11.1 %copy-start.4 = (bf16[2,512,128]{2,1,0:T(8,128)(2,1)S(1)}, bf16[2,512,128]{2,1,0:T(8,128)(2,1)}, u32[]{:S(2)}) copy-start(bf16[2,512,128]{2,1,0:T(8,128)(2,1)} %refs_8_.3) | copy-start | bytes 786436
  11.8 11.1 %copy-start.7 = (bf16[1,512,512]{2,1,0:T(8,128)(2,1)S(1)}, bf16[1,512,512]{2,1,0:T(8,128)(2,1)}, u32[]{:S(2)}) copy-start(bf16[1,512,512]{2,1,0:T(8,128)(2,1)} %param.20) | copy-start | bytes 1572868
  20.2 89.7 %collective-permute-start.19 = (bf16[896,1024]{1,0:T(8,128)(2,1)S(1)}, bf16[896,1024]{1,0:T(8,128)(2,1)}, u32[]{:S(2)}, u32[]{:S(2)}) collective-permute-start(bf16[896,1024]{1,0:T(8,128)(2,1)S(1)} %bitcast.70), channel_id=1, source_target_pairs={{0,32},{32,0},{1,33},{33,1},{2,34},{34,2},{3,35},{35,3},{4,36},{36... | collective-permute-start | bytes 5505032 | tf_op jit(solution)/shard_map/ppermute | solution.py:366
  22.9 0.8 copy-start.9
  27.5 4.3 %collective-permute-start.7 = (bf16[64,384]{1,0:T(8,128)(2,1)S(1)}, bf16[64,384]{1,0:T(8,128)(2,1)S(1)}, u32[]{:S(2)}, u32[]{:S(2)}) collective-permute-start(bf16[64,384]{1,0:T(8,128)(2,1)S(1)} %get-tuple-element.32), channel_id=1, source_target_pairs={{0,64},{64,128},{128,192},{192,0},{1,65},{65,129},{129,193},{193,1... | collective-permute-start | bytes 147464 | tf_op jit(solution)/shard_map/ppermute | solution.py:82
  27.6 5.3 %collective-permute-start.6 = (bf16[64,384]{1,0:T(8,128)(2,1)S(1)}, bf16[64,384]{1,0:T(8,128)(2,1)S(1)}, u32[]{:S(2)}, u32[]{:S(2)}) collective-permute-start(bf16[64,384]{1,0:T(8,128)(2,1)S(1)} %get-tuple-element.31), channel_id=1, source_target_pairs={{0,128},{64,192},{128,0},{192,64},{1,129},{65,193},{129,1},{193,65... | collective-permute-start | bytes 147464 | tf_op jit(solution)/shard_map/ppermute | solution.py:82
  29.0 5.4 %collective-permute-start.5 = (bf16[64,384]{1,0:T(8,128)(2,1)S(1)}, bf16[64,384]{1,0:T(8,128)(2,1)S(1)}, u32[]{:S(2)}, u32[]{:S(2)}) collective-permute-start(bf16[64,384]{1,0:T(8,128)(2,1)S(1)} %get-tuple-element.30), channel_id=1, source_target_pairs={{0,192},{64,0},{128,64},{192,128},{1,193},{65,1},{129,65},{193,129... | collective-permute-start | bytes 147464 | tf_op jit(solution)/shard_map/ppermute | solution.py:82
  40.0 23.9 %collective-permute-start.10 = (bf16[64,7168]{1,0:T(8,128)(2,1)}, bf16[64,7168]{1,0:T(8,128)(2,1)}, u32[]{:S(2)}, u32[]{:S(2)}) collective-permute-start(bf16[64,7168]{1,0:T(8,128)(2,1)} %get-tuple-element.36), channel_id=1, source_target_pairs={{0,24},{1,25},{2,26},{3,27},{4,28},{5,29},{6,30},{7,31},{8,0},{9,1... | collective-permute-start | bytes 2752520 | tf_op jit(solution)/shard_map/ppermute | solution.py:410
  42.7 21.1 %collective-permute-start.8 = (bf16[64,7168]{1,0:T(8,128)(2,1)}, bf16[64,7168]{1,0:T(8,128)(2,1)}, u32[]{:S(2)}, u32[]{:S(2)}) collective-permute-start(bf16[64,7168]{1,0:T(8,128)(2,1)} %get-tuple-element.34), channel_id=1, source_target_pairs={{0,16},{1,17},{2,18},{3,19},{4,20},{5,21},{6,22},{7,23},{8,24},{9,... | collective-permute-start | bytes 2752520 | tf_op jit(solution)/shard_map/ppermute | solution.py:410
  43.5 24.2 %collective-permute-start.9 = (bf16[64,7168]{1,0:T(8,128)(2,1)}, bf16[64,7168]{1,0:T(8,128)(2,1)}, u32[]{:S(2)}, u32[]{:S(2)}) collective-permute-start(bf16[64,7168]{1,0:T(8,128)(2,1)} %get-tuple-element.35), channel_id=1, source_target_pairs={{0,8},{1,9},{2,10},{3,11},{4,12},{5,13},{6,14},{7,15},{8,16},{9,17... | collective-permute-start | bytes 2752520 | tf_op jit(solution)/shard_map/ppermute | solution.py:410
  44.6 7.6 %collective-permute-start.15 = (bf16[4,8,32]{2,1,0:T(8,128)(2,1)S(1)}, bf16[4,8,32]{2,1,0:T(8,128)(2,1)S(1)}, u32[]{:S(2)}, u32[]{:S(2)}) collective-permute-start(bf16[4,8,32]{2,1,0:T(8,128)(2,1)S(1)} %pad_maximum_fusion.1), channel_id=1, source_target_pairs={{0,1},{1,0},{2,3},{3,2},{4,5},{5,4},{6,7},{7,6},{8,9},{9,8},{10,11... | collective-permute-start | bytes 6152 | tf_op jit(solution)/shard_map/ppermute | solution.py:439
  52.3 57.7 %collective-permute-start.20 = (bf16[896,1024]{1,0:T(8,128)(2,1)}, bf16[896,1024]{1,0:T(8,128)(2,1)}, u32[]{:S(2)}, u32[]{:S(2)}) collective-permute-start(bf16[896,1024]{1,0:T(8,128)(2,1)} %bitcast.80), channel_id=1, source_target_pairs={{0,32},{32,0},{1,33},{33,1},{2,34},{34,2},{3,35},{35,3},{4,36},{36... | collective-permute-start | bytes 5505032 | tf_op jit(solution)/shard_map/ppermute | solution.py:366
  70.0 11.9 %copy-start.8 = (bf16[8,7168]{1,0:T(8,128)(2,1)S(1)}, bf16[8,7168]{1,0:T(8,128)(2,1)}, u32[]{:S(2)}) copy-start(bf16[8,7168]{1,0:T(8,128)(2,1)} %residual_ref.1) | copy-start | bytes 344068
  70.7 25.7 %copy-start.10 = (f32[7168]{0:T(1024)S(1)}, f32[7168]{0:T(1024)}, u32[]{:S(2)}) copy-start(f32[7168]{0:T(1024)} %param.26) | copy-start | bytes 86020
  70.7 7.4 %collective-permute-start.11 = (bf16[16,7168]{1,0:T(8,128)(2,1)}, bf16[16,7168]{1,0:T(8,128)(2,1)S(1)}, u32[]{:S(2)}, u32[]{:S(2)}) collective-permute-start(bf16[16,7168]{1,0:T(8,128)(2,1)} %get-tuple-element.54), channel_id=1, source_target_pairs={{0,2},{1,3},{2,4},{3,5},{4,6},{5,7},{6,0},{7,1},{8,10},{9,11},{10,... | collective-permute-start | bytes 688136 | tf_op jit(solution)/shard_map/ppermute | solution.py:412
  72.3 9.6 %collective-permute-start.12 = (bf16[16,7168]{1,0:T(8,128)(2,1)S(1)}, bf16[16,7168]{1,0:T(8,128)(2,1)S(1)}, u32[]{:S(2)}, u32[]{:S(2)}) collective-permute-start(bf16[16,7168]{1,0:T(8,128)(2,1)S(1)} %get-tuple-element.53), channel_id=1, source_target_pairs={{0,4},{1,5},{2,6},{3,7},{4,0},{5,1},{6,2},{7,3},{8,12},{9,13},{10,... | collective-permute-start | bytes 688136 | tf_op jit(solution)/shard_map/ppermute | solution.py:412
  75.2 6.7 %collective-permute-start.13 = (bf16[16,7168]{1,0:T(8,128)(2,1)S(1)}, bf16[16,7168]{1,0:T(8,128)(2,1)S(1)}, u32[]{:S(2)}, u32[]{:S(2)}) collective-permute-start(bf16[16,7168]{1,0:T(8,128)(2,1)S(1)} %get-tuple-element.52), channel_id=1, source_target_pairs={{0,6},{1,7},{2,0},{3,1},{4,2},{5,3},{6,4},{7,5},{8,14},{9,15},{10,... | collective-permute-start | bytes 688136 | tf_op jit(solution)/shard_map/ppermute | solution.py:412
  82.7 13.7 %collective-permute-start.14 = (bf16[16,7168]{1,0:T(8,128)(2,1)}, bf16[16,7168]{1,0:T(8,128)(2,1)S(1)}, u32[]{:S(2)}, u32[]{:S(2)}) collective-permute-start(bf16[16,7168]{1,0:T(8,128)(2,1)} %get-tuple-element.38), channel_id=1, source_target_pairs={{0,1},{1,0},{2,3},{3,2},{4,5},{5,4},{6,7},{7,6},{8,9},{9,8},{10,11... | collective-permute-start | bytes 688136 | tf_op jit(solution)/shard_map/ppermute | solution.py:422
  97.2 4.2 %collective-permute-start.16 = (bf16[16,1792]{1,0:T(8,128)(2,1)S(1)}, bf16[16,1792]{1,0:T(8,128)(2,1)S(1)}, u32[]{:S(2)}, u32[]{:S(2)}) collective-permute-start(bf16[16,1792]{1,0:T(8,128)(2,1)S(1)} %get-tuple-element.41), channel_id=1, source_target_pairs={{0,192},{64,0},{128,64},{192,128},{1,193},{65,1},{129,65},{193,129... | collective-permute-start | bytes 172040 | tf_op jit(solution)/shard_map/ppermute | solution.py:82
  97.2 5.2 %collective-permute-start.17 = (bf16[16,1792]{1,0:T(8,128)(2,1)S(1)}, bf16[16,1792]{1,0:T(8,128)(2,1)S(1)}, u32[]{:S(2)}, u32[]{:S(2)}) collective-permute-start(bf16[16,1792]{1,0:T(8,128)(2,1)S(1)} %get-tuple-element.42), channel_id=1, source_target_pairs={{0,128},{64,192},{128,0},{192,64},{1,129},{65,193},{129,1},{193,65... | collective-permute-start | bytes 172040 | tf_op jit(solution)/shard_map/ppermute | solution.py:82
  99.0 4.5 %collective-permute-start.18 = (bf16[16,1792]{1,0:T(8,128)(2,1)S(1)}, bf16[16,1792]{1,0:T(8,128)(2,1)S(1)}, u32[]{:S(2)}, u32[]{:S(2)}) collective-permute-start(bf16[16,1792]{1,0:T(8,128)(2,1)S(1)} %get-tuple-element.43), channel_id=1, source_target_pairs={{0,64},{64,128},{128,192},{192,0},{1,65},{65,129},{129,193},{193,1... | collective-permute-start | bytes 172040 | tf_op jit(solution)/shard_map/ppermute | solution.py:82
  105.2 23.4 %all-to-all-start = ((bf16[16,24,1792]{2,1,0:T(8,128)(2,1)}), bf16[16,24,1792]{2,1,0:T(8,128)(2,1)S(1)}, u32[]{:S(2)}, u32[]{:S(2)}) async-start(bf16[16,24,1792]{2,1,0:T(8,128)(2,1)} %bitcast.79), calls=%async_computation | async-start | bytes 2752512 | tf_op jit(solution)/shard_map/all_to_all | solution.py:63
  109.7 66.6 %collective-permute-start.27 = (bf16[1024,896]{1,0:T(8,128)(2,1)}, bf16[1024,896]{1,0:T(8,128)(2,1)}, u32[]{:S(2)}, u32[]{:S(2)}) collective-permute-start(bf16[1024,896]{1,0:T(8,128)(2,1)} %bitcast.72), channel_id=1, source_target_pairs={{0,32},{32,0},{1,33},{33,1},{2,34},{34,2},{3,35},{35,3},{4,36},{36... | collective-permute-start | bytes 5505032 | tf_op jit(solution)/shard_map/ppermute | solution.py:366
  134.5 54.0 %copy-start.2 = (bf16[1,1024,896]{2,1,0:T(8,128)(2,1)S(1)}, bf16[1,1024,896]{2,1,0:T(8,128)(2,1)}, u32[]{:S(2)}) copy-start(bf16[1,1024,896]{2,1,0:T(8,128)(2,1)} %param.31) | copy-start | bytes 5505028
  134.6 26.5 %collective-permute-start.21 = (bf16[96,2048]{1,0:T(8,128)(2,1)S(1)}, bf16[96,2048]{1,0:T(8,128)(2,1)S(1)}, u32[]{:S(2)}, u32[]{:S(2)}) collective-permute-start(bf16[96,2048]{1,0:T(8,128)(2,1)S(1)} %get-tuple-element.45), channel_id=1, source_target_pairs={{0,64},{64,128},{128,192},{192,0},{1,65},{65,129},{129,193},{193,1... | collective-permute-start | bytes 1179656 | tf_op jit(solution)/shard_map/ppermute | solution.py:82
  135.5 29.8 %collective-permute-start.22 = (bf16[96,2048]{1,0:T(8,128)(2,1)S(1)}, bf16[96,2048]{1,0:T(8,128)(2,1)S(1)}, u32[]{:S(2)}, u32[]{:S(2)}) collective-permute-start(bf16[96,2048]{1,0:T(8,128)(2,1)S(1)} %get-tuple-element.46), channel_id=1, source_target_pairs={{0,128},{64,192},{128,0},{192,64},{1,129},{65,193},{129,1},{193,65... | collective-permute-start | bytes 1179656 | tf_op jit(solution)/shard_map/ppermute | solution.py:82
  139.9 33.8 %collective-permute-start.23 = (bf16[96,2048]{1,0:T(8,128)(2,1)S(1)}, bf16[96,2048]{1,0:T(8,128)(2,1)S(1)}, u32[]{:S(2)}, u32[]{:S(2)}) collective-permute-start(bf16[96,2048]{1,0:T(8,128)(2,1)S(1)} %get-tuple-element.47), channel_id=1, source_target_pairs={{0,192},{64,0},{128,64},{192,128},{1,193},{65,1},{129,65},{193,129... | collective-permute-start | bytes 1179656 | tf_op jit(solution)/shard_map/ppermute | solution.py:82
  174.1 12.3 %collective-permute-start.24 = (bf16[96,1024]{1,0:T(8,128)(2,1)S(1)}, bf16[96,1024]{1,0:T(8,128)(2,1)S(1)}, u32[]{:S(2)}, u32[]{:S(2)}) collective-permute-start(bf16[96,1024]{1,0:T(8,128)(2,1)S(1)} %fusion.5.refs_0_), channel_id=1, source_target_pairs={{0,64},{64,128},{128,192},{192,0},{1,65},{65,129},{129,193},{193,1... | collective-permute-start | bytes 589832 | tf_op jit(solution)/shard_map/ppermute | solution.py:82
  174.2 14.3 %collective-permute-start.25 = (bf16[96,1024]{1,0:T(8,128)(2,1)S(1)}, bf16[96,1024]{1,0:T(8,128)(2,1)S(1)}, u32[]{:S(2)}, u32[]{:S(2)}) collective-permute-start(bf16[96,1024]{1,0:T(8,128)(2,1)S(1)} %fusion.5.refs_0_), channel_id=1, source_target_pairs={{0,128},{64,192},{128,0},{192,64},{1,129},{65,193},{129,1},{193,65... | collective-permute-start | bytes 589832 | tf_op jit(solution)/shard_map/ppermute | solution.py:82
  174.3 14.2 %collective-permute-start.26 = (bf16[96,1024]{1,0:T(8,128)(2,1)S(1)}, bf16[96,1024]{1,0:T(8,128)(2,1)S(1)}, u32[]{:S(2)}, u32[]{:S(2)}) collective-permute-start(bf16[96,1024]{1,0:T(8,128)(2,1)S(1)} %fusion.5.refs_0_), channel_id=1, source_target_pairs={{0,192},{64,0},{128,64},{192,128},{1,193},{65,1},{129,65},{193,129... | collective-permute-start | bytes 589832 | tf_op jit(solution)/shard_map/ppermute | solution.py:82
  193.5 24.5 %all-to-all-start.1 = ((bf16[16,24,1792]{2,1,0:T(8,128)(2,1)}), bf16[16,24,1792]{2,1,0:T(8,128)(2,1)S(1)}, u32[]{:S(2)}, u32[]{:S(2)}) async-start(bf16[16,24,1792]{2,1,0:T(8,128)(2,1)} %bitcast.27), calls=%async_computation.1 | async-start | bytes 2752512 | tf_op jit(solution)/shard_map/all_to_all | solution.py:63

commit v5 on v4

--- a/solution.py
+++ b/solution.py
@@ -16,6 +16,7 @@
 ROWS = 8
 LINE_ORDER = (2, 1, 3)
 UP_STEPS = 4
+FLIP_ORDER = (0, 2, 1, 3)
 
 SIDE = 4
 LINES = 4
@@ -241,7 +242,7 @@
 
 
 def up_kernel(line_ref, rows_ref, *refs):
-    w_refs, out_refs, rows_scratch = refs[: 2 * CORES], refs[2 * CORES : -1], refs[-1]
+    w_refs, out_refs, scratches = refs[: 2 * CORES], refs[2 * CORES : -2], refs[-2:]
     each = rows_ref.shape[0] // LINES
     share = rows_ref.shape[1] // CORES
     step = pl.program_id(0)
@@ -249,43 +250,50 @@
     @pl.when(step == 0)
     def _():
         line = line_ref[0]
-        for k in range(LINES):
-            at = pl.multiple_of(lax.rem(line + k, LINES) * each, each)
-            rows_scratch[k * each : (k + 1) * each, :] = rows_ref[pl.ds(at, each), :]
-
-    rows = rows_scratch[...]
-    for half in range(2):
+        for place, k in enumerate(FLIP_ORDER):
+            for scratch, at in zip(scratches, (lax.rem(line + place, LINES), lax.bitwise_xor(line, k))):
+                at = pl.multiple_of(at * each, each)
+                scratch[place * each : (place + 1) * each, :] = rows_ref[pl.ds(at, each), :]
+
+    for half, scratch in enumerate(scratches):
+        rows = scratch[...]
         total = dot(rows[:, :share], w_refs[half][...]) + dot(rows[:, share:], w_refs[2 + half][...])
         total = total.astype(BF)
         width = total.shape[1]
-        at = pl.multiple_of((half * pl.num_programs(0) + step) * width, width)
-        for k, out_ref in enumerate(out_refs):
-            out_ref[:, pl.ds(at, width)] = total[k * each : (k + 1) * each]
+        at = pl.multiple_of(step * width, width)
+        row = 0
+        for out_ref in out_refs[:LINES] if half == 0 else out_refs[LINES:]:
+            out_ref[:, pl.ds(at, width)] = total[row : row + out_ref.shape[0]]
+            row += out_ref.shape[0]
 
 
 def down_kernel(line_ref, *refs):
-    hidden_refs, w_refs, out_ref, total_ref = refs[:LINES], refs[LINES : LINES + CORES], refs[-2], refs[-1]
+    hidden_refs, w_refs, out_ref, total_ref = refs[: LINES + 2], refs[LINES + 2 : -2], refs[-2], refs[-1]
     each = hidden_refs[0].shape[0]
+    width = w_refs[0].shape[1]
+    line = line_ref[0]
     step = pl.program_id(0)
-    depth = w_refs[0].shape[0]
-    width = w_refs[0].shape[1]
-    at = pl.multiple_of(step * depth, depth)
-    hidden = jnp.concatenate([ref[:, pl.ds(at, depth)] for ref in hidden_refs], axis=0)
-    for core in range(CORES):
-        columns = slice(core * width, (core + 1) * width)
-        total = dot(hidden, w_refs[core][...])
-
-        @pl.when(step == 0)
-        def _():
-            total_ref[:, columns] = total
-
-        @pl.when(step == pl.num_programs(0) - 1)
-        def _():
-            line = line_ref[0]
-            whole = (total_ref[:, columns] + total).astype(BF)
-            for k in range(LINES):
-                at = pl.multiple_of(lax.rem(line + LINES - k, LINES) * each, each)
-                out_ref[pl.ds(at, each), columns] = whole[k * each : (k + 1) * each]
+
+    def product(rows):
+        return [dot(rows, ref[...]) for ref in w_refs]
+
+    @pl.when(step == 0)
+    def _():
+        totals = product(jnp.concatenate([ref[...] for ref in hidden_refs[:LINES]], axis=0))
+        for k in range(LINES):
+            at = pl.multiple_of(lax.rem(line + LINES - k, LINES) * each, each)
+            for core, total in enumerate(totals):
+                total_ref[pl.ds(at, each), core * width : (core + 1) * width] = total[k * each : (k + 1) * each]
+
+    @pl.when(step == 1)
+    def _():
+        totals = product(jnp.concatenate([ref[...] for ref in hidden_refs[LINES:]], axis=0))
+        for place, k in enumerate(FLIP_ORDER):
+            at = pl.multiple_of(lax.bitwise_xor(line, k) * each, each)
+            for core, total in enumerate(totals):
+                columns = slice(core * width, (core + 1) * width)
+                whole = total_ref[pl.ds(at, each), columns] + total[place * each : (place + 1) * each]
+                out_ref[pl.ds(at, each), columns] = whole.astype(BF)
 
 
 def whole(shape):
@@ -450,31 +458,38 @@
     line_rows = rows_in.shape[0] // LINES
     ups = [w_gate[0], w_up[0], sibling(w_gate[0]), sibling(w_up[0])]
     scalar = pl.BlockSpec(memory_space=pltpu.SMEM)
-    out_shape = (line_rows, 2 * w_gate.shape[2])
-    parts = on_chip(
+    ffe = w_gate.shape[2]
+    out_shapes = [(line_rows, ffe)] * LINES + [(2 * line_rows, ffe)] * 2
+    *gate_parts, up_kept, up_sent = on_chip(
         up_kernel,
-        [out_shape] * LINES,
+        out_shapes,
         line,
         rows_in,
         *ups,
         grid=(UP_STEPS,),
         in_specs=[scalar, whole(rows_in.shape)] + [column_block(one, UP_STEPS) for one in ups],
-        out_specs=[whole(out_shape)] * LINES,
-        scratch_shapes=[pltpu.VMEM(rows_in.shape, BF)],
-    )
-    sums = sum_wide(along_line(parts))
-    ffe = sums.shape[1] // 2
-    hidden = (jax.nn.silu(sums[:, :ffe]) * sums[:, ffe:]).astype(BF)
+        out_specs=[whole(shape) for shape in out_shapes],
+        scratch_shapes=[pltpu.VMEM(rows_in.shape, BF)] * 2,
+    )
+    up_sums = sum_wide([up_kept, lax.ppermute(up_sent, "zlo", flips(LINES, 1))])
+    gate = sum_wide(along_line(gate_parts))
+    up_far = lax.ppermute(up_sums[line_rows:].astype(BF), "zlo", flips(LINES, 2))
+    up = up_sums[:line_rows] + up_far.astype(F32)
+    hidden = (jax.nn.silu(gate) * up).astype(BF)
+    direct, relayed = hidden[:, : ffe // 2], hidden[:, ffe // 2 :]
+    relayed = jnp.concatenate([relayed, lax.ppermute(relayed, "zlo", flips(LINES, 2))], axis=0)
+    gathered = along_line([direct] * LINES)
+    gathered += [relayed, lax.ppermute(relayed, "zlo", flips(LINES, 1))]
     downs = [w_down[0], sibling(w_down[0])]
     out_shape = (rows_in.shape[0], CORES * share)
     (expert_out,) = on_chip(
         down_kernel,
         [out_shape],
         line,
-        *along_line([hidden] * LINES),
+        *gathered,
         *downs,
         grid=(2,),
-        in_specs=[scalar] + [whole(hidden.shape)] * LINES + [row_block(one, 2) for one in downs],
+        in_specs=[scalar] + [whole(one.shape) for one in gathered] + [row_block(one, 2) for one in downs],
         out_specs=[whole(out_shape)],
         scratch_shapes=[pltpu.VMEM(out_shape, F32)],
     )

time: 234 us -> 227 us (0.970)
  waiting for transfers between devices: 120 us -> 91.2 us
  starting transfers between devices: 51.8 us -> 71.2 us
  blocking collectives: 13.3 us -> 16.3 us
    ppermute x15, waiting for transfers between devices: 56.2 us -> 18.4 us  [along_line(): lax.ppermute(parts[k], 'zlo', shift(sign * k))]
    ppermute x0 -> x4, starting transfers between devices: none -> 13.8 us  [the longest x1 6.9 us: body(): lax.ppermute(up_sums[line_rows:].astype(BF), 'zlo', flips(LINES, 2))]
    ppermute x0 -> x4, waiting for transfers between devices: none -> 12 us  [the longest x1 6.7 us: body(): up_sums = sum_wide([up_kept, lax.ppermute(up_sent, 'zlo', flips(LINES, 1))])]
    all_to_all x1, blocking collectives: 13.3 us -> 16.3 us  [exchange(): return lax.all_to_all(value, axes, 0, 0, tiled=True)]
    all_to_all x2, starting transfers between devices: 10.6 us -> 13.3 us  [exchange(): return lax.all_to_all(value, axes, 0, 0, tiled=True)]
  transfers between devices with their start and end apart: 30 -> 34, of which waited for: 20 -> 21; matrix products, arithmetic and copies ran while one was open for 8% -> 8% of each run, Pallas kernels for 7% -> 8%
where the time goes in v5:
time: 227 us; the launch traced here: 226 us
  waiting for transfers between devices  91.2 us (40%)
  starting transfers between devices  71.2 us (31%)
  Pallas kernels  23.6 us (10%)
  blocking collectives  16.3 us (7%)
  local copies, waits for them, and re-layouts  12.8 us (6%)
  other arithmetic  7.89 us (3%)
  matrix products  2.42 us (1%)
    all_to_all x2, waiting for transfers between devices, exchange(): return lax.all_to_all(value, axes, 0, 0, tiled=True)  35.7 us
    pallas_call x7, Pallas kernels, on_chip(): pl.pallas_call(kernel, out_shape=[jax.ShapeDtypeStruct(shape, dtype) for...  23.6 us
    ppermute x15, starting transfers between devices, along_line(): lax.ppermute(parts[k], 'zlo', shift(sign * k))  20.5 us
    ppermute x15, waiting for transfers between devices, along_line(): lax.ppermute(parts[k], 'zlo', shift(sign * k))  18.4 us
    all_to_all x1, blocking collectives, exchange(): return lax.all_to_all(value, axes, 0, 0, tiled=True)  16.3 us
    ppermute x3, waiting for transfers between devices, body(): lax.ppermute(first[k], ALL, plane_shift(k, 0))  13.8 us
    all_to_all x2, starting transfers between devices, exchange(): return lax.all_to_all(value, axes, 0, 0, tiled=True)  13.3 us
    ppermute x1, starting transfers between devices, body(): lax.ppermute(up_sums[line_rows:].astype(BF), 'zlo', flips(LINES, 2))  6.9 us
  transfers between devices with their start and end apart: 34, of which 21 were waited for; matrix products, arithmetic and copies ran while one was open for 8% of the time, Pallas kernels for 8%

profile of v5, /device:TPU:32, one launch (start us, length us, event | category | flops | bytes accessed | tf_op | source)
XLA Modules:
  0.0 226.4 jit_solution(5657765590398613955)
XLA Ops:
  0.7 0.8 reshape.335
  2.0 1.0 copy-done
  3.0 0.8 copy-done.5
  3.9 2.1 shard_map.167
  6.0 1.9 collective-permute-start
  7.9 2.3 %collective-permute-start.1 = (bf16[64,1152]{1,0:T(8,128)(2,1)}, bf16[64,1152]{1,0:T(8,128)(2,1)}, u32[]{:S(2)}, u32[]{:S(2)}) collective-permute-start(bf16[64,1152]{1,0:T(8,128)(2,1)} %get-tuple-element.29), channel_id=1, source_target_pairs={{0,128},{64,192},{128,0},{192,64},{1,129},{65,193},{129,1},{193,65... | collective-permute-start | bytes 442376 | tf_op jit(solution)/shard_map/ppermute | solution.py:83
  10.2 1.1 collective-permute-start.2
  11.8 3.3 %fusion.66 = (bf16[256,1,512]{2,1,0:T(2,128)(2,1)}, bf16[256,1,512]{2,1,0:T(2,128)(2,1)}) fusion(bf16[256,2,512]{2,1,0:T(2,128)(2,1)} %q_latent_ref.1), kind=kLoop, calls=%fused_computation.162 | loop fusion | bytes 1048576 | tf_op jit(solution)/shard_map/slice | solution.py:402
  15.6 1.4 fusion.3
  17.0 0.8 fusion.24
  17.8 0.8 copy.62
  18.7 0.9 broadcast_multiply_fusion.refs_6_
  20.8 2.1 collective-permute-done.2.refs_3_
  22.9 0.8 copy-done.9
  23.7 3.7 %shard_map.168 = (bf16[64,384]{1,0:T(8,128)(2,1)S(1)}, bf16[64,384]{1,0:T(8,128)(2,1)S(1)}, bf16[64,384]{1,0:T(8,128)(2,1)S(1)}, bf16[64,384]{1,0:T(8,128)(2,1)S(1)}) custom-call(bf16[64,1152]{1,0:T(8,128)(2,1)S(1)} %get-tuple-element.27.refs_0_, bf16[64,1152]{1,0:T(8,128)(2,1)S(1)} %collective-permute-done.refs_1_, ...), custom_call_target="tpu_custom_call" | custom-call | tf_op jit(solution)/shard_map/pallas_call | solution.py:316
  27.6 1.4 collective-permute-start.6
  29.0 2.8 %collective-permute-start.7 = (bf16[64,384]{1,0:T(8,128)(2,1)S(1)}, bf16[64,384]{1,0:T(8,128)(2,1)S(1)}, u32[]{:S(2)}, u32[]{:S(2)}) collective-permute-start(bf16[64,384]{1,0:T(8,128)(2,1)S(1)} %get-tuple-element.34), channel_id=1, source_target_pairs={{0,64},{64,128},{128,192},{192,0},{1,65},{65,129},{129,193},{193,1... | collective-permute-start | bytes 147464 | tf_op jit(solution)/shard_map/ppermute | solution.py:83
  31.9 1.3 collective-permute-done.5.refs_1_
  33.1 0.8 collective-permute-done.7.refs_3_
  34.0 5.7 %shard_map.169 = (bf16[64,7168]{1,0:T(8,128)(2,1)S(1)}, bf16[64,7168]{1,0:T(8,128)(2,1)}, bf16[64,7168]{1,0:T(8,128)(2,1)}, bf16[64,7168]{1,0:T(8,128)(2,1)}) custom-call(bf16[64,384]{1,0:T(8,128)(2,1)S(1)} %get-tuple-element.31.refs_0_, bf16[64,384]{1,0:T(8,128)(2,1)S(1)} %collective-permute-done.5.refs_1_, ...), custom_call_target="tpu_custom_call" | custom-call | tf_op jit(solution)/shard_map/pallas_call | solution.py:316
  39.6 2.8 %collective-permute-start.10 = (bf16[64,7168]{1,0:T(8,128)(2,1)}, bf16[64,7168]{1,0:T(8,128)(2,1)}, u32[]{:S(2)}, u32[]{:S(2)}) collective-permute-start(bf16[64,7168]{1,0:T(8,128)(2,1)} %get-tuple-element.38), channel_id=1, source_target_pairs={{0,24},{1,25},{2,26},{3,27},{4,28},{5,29},{6,30},{7,31},{8,0},{9,1... | collective-permute-start | bytes 2752520 | tf_op jit(solution)/shard_map/ppermute | solution.py:418
  42.4 2.3 %collective-permute-start.8 = (bf16[64,7168]{1,0:T(8,128)(2,1)}, bf16[64,7168]{1,0:T(8,128)(2,1)}, u32[]{:S(2)}, u32[]{:S(2)}) collective-permute-start(bf16[64,7168]{1,0:T(8,128)(2,1)} %get-tuple-element.36), channel_id=1, source_target_pairs={{0,16},{1,17},{2,18},{3,19},{4,20},{5,21},{6,22},{7,23},{8,24},{9,... | collective-permute-start | bytes 2752520 | tf_op jit(solution)/shard_map/ppermute | solution.py:418
  44.9 6.0 %collective-permute-start.15 = (bf16[4,8,32]{2,1,0:T(8,128)(2,1)S(1)}, bf16[4,8,32]{2,1,0:T(8,128)(2,1)S(1)}, u32[]{:S(2)}, u32[]{:S(2)}) collective-permute-start(bf16[4,8,32]{2,1,0:T(8,128)(2,1)S(1)} %pad_maximum_fusion.2), channel_id=1, source_target_pairs={{0,1},{1,0},{2,3},{3,2},{4,5},{5,4},{6,7},{7,6},{8,9},{9,8},{10,11... | collective-permute-start | bytes 6152 | tf_op jit(solution)/shard_map/ppermute | solution.py:447
  50.9 0.8 broadcast_in_dim.65
  51.8 0.7 broadcast_in_dim.74
  53.4 10.1 %collective-permute-done.10 = bf16[64,7168]{1,0:T(8,128)(2,1)} collective-permute-done((bf16[64,7168]{1,0:T(8,128)(2,1)}, bf16[64,7168]{1,0:T(8,128)(2,1)}, u32[]{:S(2)}, u32[]{:S(2)}) %collective-permute-start.10) | collective-permute-done | bytes 917536 | tf_op jit(solution)/shard_map/ppermute | solution.py:418
  63.5 3.7 %collective-permute-done.9 = bf16[64,7168]{1,0:T(8,128)(2,1)} collective-permute-done((bf16[64,7168]{1,0:T(8,128)(2,1)}, bf16[64,7168]{1,0:T(8,128)(2,1)}, u32[]{:S(2)}, u32[]{:S(2)}) %collective-permute-start.9) | collective-permute-done | bytes 917536 | tf_op jit(solution)/shard_map/ppermute | solution.py:418
  67.1 2.2 add_convert_fusion
  69.3 0.7 fusion.65
  70.1 1.6 collective-permute-start.11
  71.7 2.9 %collective-permute-start.12 = (bf16[16,7168]{1,0:T(8,128)(2,1)S(1)}, bf16[16,7168]{1,0:T(8,128)(2,1)S(1)}, u32[]{:S(2)}, u32[]{:S(2)}) collective-permute-start(bf16[16,7168]{1,0:T(8,128)(2,1)S(1)} %get-tuple-element.57), channel_id=1, source_target_pairs={{0,4},{1,5},{2,6},{3,7},{4,0},{5,1},{6,2},{7,3},{8,12},{9,13},{10,... | collective-permute-start | bytes 688136 | tf_op jit(solution)/shard_map/ppermute | solution.py:420
  74.6 1.3 collective-permute-start.13
  76.3 1.2 collective-permute-done.11.refs_1_
  77.5 3.7 %collective-permute-done.12.refs_2_ = bf16[16,7168]{1,0:T(8,128)(2,1)S(1)} collective-permute-done((bf16[16,7168]{1,0:T(8,128)(2,1)S(1)}, bf16[16,7168]{1,0:T(8,128)(2,1)S(1)}, u32[]{:S(2)}, u32[]{:S(2)}) %collective-permute-start.12) | collective-permute-done | bytes 229408 | tf_op jit(solution)/shard_map/ppermute | solution.py:420
  81.2 0.8 shard_map.170
  82.1 5.9 %collective-permute-start.14 = (bf16[16,7168]{1,0:T(8,128)(2,1)}, bf16[16,7168]{1,0:T(8,128)(2,1)S(1)}, u32[]{:S(2)}, u32[]{:S(2)}) collective-permute-start(bf16[16,7168]{1,0:T(8,128)(2,1)} %get-tuple-element.40), channel_id=1, source_target_pairs={{0,1},{1,0},{2,3},{3,2},{4,5},{5,4},{6,7},{7,6},{8,9},{9,8},{10,11... | collective-permute-start | bytes 688136 | tf_op jit(solution)/shard_map/ppermute | solution.py:430
  89.0 6.4 %collective-permute-done.14.far_ref = bf16[16,7168]{1,0:T(8,128)(2,1)S(1)} collective-permute-done((bf16[16,7168]{1,0:T(8,128)(2,1)}, bf16[16,7168]{1,0:T(8,128)(2,1)S(1)}, u32[]{:S(2)}, u32[]{:S(2)}) %collective-permute-start.14) | collective-permute-done | bytes 229408 | tf_op jit(solution)/shard_map/ppermute | solution.py:430
  95.4 0.8 shard_map.171
  96.2 1.9 collective-permute-start.18
  98.1 1.5 collective-permute-start.17
  100.4 2.8 %collective-permute-done.17 = bf16[16,1792]{1,0:T(8,128)(2,1)S(1)} collective-permute-done((bf16[16,1792]{1,0:T(8,128)(2,1)S(1)}, bf16[16,1792]{1,0:T(8,128)(2,1)S(1)}, u32[]{:S(2)}, u32[]{:S(2)}) %collective-permute-start.17) | collective-permute-done | bytes 57376 | tf_op jit(solution)/shard_map/ppermute | solution.py:83
  103.8 1.7 convolution_convert_fusion
  105.5 6.2 %all-to-all-start = ((bf16[16,24,1792]{2,1,0:T(8,128)(2,1)}), bf16[16,24,1792]{2,1,0:T(8,128)(2,1)S(1)}, u32[]{:S(2)}, u32[]{:S(2)}) async-start(bf16[16,24,1792]{2,1,0:T(8,128)(2,1)} %bitcast.79), calls=%async_computation | async-start | bytes 2752512 | tf_op jit(solution)/shard_map/all_to_all | solution.py:64
  112.1 17.4 %all-to-all-done = bf16[16,24,1792]{2,1,0:T(8,128)(2,1)S(1)} async-done(((bf16[16,24,1792]{2,1,0:T(8,128)(2,1)}), bf16[16,24,1792]{2,1,0:T(8,128)(2,1)S(1)}, u32[]{:S(2)}, u32[]{:S(2)}) %all-to-all-start) | async-done | bytes 1376288 | tf_op jit(solution)/shard_map/all_to_all | solution.py:64
  129.4 6.0 %shard_map.172 = (bf16[96,1024]{1,0:T(8,128)(2,1)S(1)}, bf16[96,1024]{1,0:T(8,128)(2,1)S(1)}, bf16[96,1024]{1,0:T(8,128)(2,1)S(1)}, bf16[96,1024]{1,0:T(8,128)(2...) custom-call(s32[1]{0:T(128)} %bitcast.1.line_ref, bf16[384,1792]{1,0:T(8,128)(2,1)S(1)} %bitcast.69, ...), custom_call_target="tpu_custom_call" | custom-call | tf_op jit(solution)/shard_map/pallas_call | solution.py:316
  135.9 1.7 collective-permute-start.23
  137.6 2.3 %collective-permute-start.22 = (bf16[96,1024]{1,0:T(8,128)(2,1)S(1)}, bf16[96,1024]{1,0:T(8,128)(2,1)S(1)}, u32[]{:S(2)}, u32[]{:S(2)}) collective-permute-start(bf16[96,1024]{1,0:T(8,128)(2,1)S(1)} %get-tuple-element.48), channel_id=1, source_target_pairs={{0,128},{64,192},{128,0},{192,64},{1,129},{65,193},{129,1},{193,65... | collective-permute-start | bytes 589832 | tf_op jit(solution)/shard_map/ppermute | solution.py:83
  140.0 1.0 collective-permute-start.21
  140.9 6.7 %collective-permute-done.24 = bf16[192,1024]{1,0:T(8,128)(2,1)S(1)} collective-permute-done((bf16[192,1024]{1,0:T(8,128)(2,1)S(1)}, bf16[192,1024]{1,0:T(8,128)(2,1)S(1)}, u32[]{:S(2)}, u32[]{:S(2)}) %collective-permute-start.24) | collective-permute-done | bytes 393248 | tf_op jit(solution)/shard_map/ppermute | solution.py:474
  147.8 6.9 %collective-permute-start.25 = (bf16[96,1024]{1,0:T(8,128)(2,1)S(1)}, bf16[96,1024]{1,0:T(8,128)(2,1)S(1)}, u32[]{:S(2)}, u32[]{:S(2)}) collective-permute-start(bf16[96,1024]{1,0:T(8,128)(2,1)S(1)} %slice.126), channel_id=1, source_target_pairs={{0,128},{64,192},{128,0},{192,64},{1,129},{65,193},{129,1},{193,65... | collective-permute-start | bytes 589832 | tf_op jit(solution)/shard_map/ppermute | solution.py:476
  154.7 3.7 %collective-permute-done.21 = bf16[96,1024]{1,0:T(8,128)(2,1)S(1)} collective-permute-done((bf16[96,1024]{1,0:T(8,128)(2,1)S(1)}, bf16[96,1024]{1,0:T(8,128)(2,1)S(1)}, u32[]{:S(2)}, u32[]{:S(2)}) %collective-permute-start.21) | collective-permute-done | bytes 196640 | tf_op jit(solution)/shard_map/ppermute | solution.py:83
  158.4 2.1 collective-permute-done.25
  160.8 3.5 %collective-permute-start.29 = (bf16[96,512]{1,0:T(8,128)(2,1)S(1)}, bf16[96,512]{1,0:T(8,128)(2,1)S(1)}, u32[]{:S(2)}, u32[]{:S(2)}) collective-permute-start(bf16[96,512]{1,0:T(8,128)(2,1)S(1)} %get-tuple-element.62), channel_id=1, source_target_pairs={{0,128},{64,192},{128,0},{192,64},{1,129},{65,193},{129,1},{193,65... | collective-permute-start | bytes 294920 | tf_op jit(solution)/shard_map/ppermute | solution.py:480
  164.3 3.1 %collective-permute-done.29 = bf16[96,512]{1,0:T(8,128)(2,1)S(1)} collective-permute-done((bf16[96,512]{1,0:T(8,128)(2,1)S(1)}, bf16[96,512]{1,0:T(8,128)(2,1)S(1)}, u32[]{:S(2)}, u32[]{:S(2)}) %collective-permute-start.29) | collective-permute-done | bytes 98336 | tf_op jit(solution)/shard_map/ppermute | solution.py:480
  167.4 3.1 %collective-permute-start.30 = (bf16[192,512]{1,0:T(8,128)(2,1)S(1)}, bf16[192,512]{1,0:T(8,128)(2,1)S(1)}, u32[]{:S(2)}, u32[]{:S(2)}) collective-permute-start(bf16[192,512]{1,0:T(8,128)(2,1)S(1)} %pad_maximum_fusion.refs_4_), channel_id=1, source_target_pairs={{0,64},{64,0},{128,192},{192,128},{1,65},{65,1},{129,193},{193,129... | collective-permute-start | bytes 589832 | tf_op jit(solution)/shard_map/ppermute | solution.py:482
  170.5 1.0 collective-permute-start.26
  171.5 1.5 collective-permute-start.27
  173.0 2.2 collective-permute-done.26.refs_1_
  175.2 1.8 collective-permute-done.27.refs_2_
  177.0 1.8 collective-permute-done.28.refs_3_
  178.8 4.4 %shard_map.173 = bf16[384,1792]{1,0:T(8,128)(2,1)} custom-call(s32[1]{0:T(128)} %bitcast.1.line_ref, bf16[96,512]{1,0:T(8,128)(2,1)S(1)} %get-tuple-element.63.refs_0_, bf16[96,512]{1,0:T(8,128)(2,1)S(1)} %collective-permute-done.26.refs_1_, bf16[96,512]{1,0:T(8,128)(2,1)S(1)} %collective-permute-done.27.refs_2_, ...), custom_call_target="tpu_custom_call" | custom-call | tf_op jit(solution)/shard_map/pallas_call | solution.py:316
  183.2 7.0 %all-to-all-start.1 = ((bf16[16,24,1792]{2,1,0:T(8,128)(2,1)}), bf16[16,24,1792]{2,1,0:T(8,128)(2,1)S(1)}, u32[]{:S(2)}, u32[]{:S(2)}) async-start(bf16[16,24,1792]{2,1,0:T(8,128)(2,1)} %bitcast.27), calls=%async_computation.1 | async-start | bytes 2752512 | tf_op jit(solution)/shard_map/all_to_all | solution.py:64
  190.3 18.3 %all-to-all-done.1 = bf16[16,24,1792]{2,1,0:T(8,128)(2,1)S(1)} async-done(((bf16[16,24,1792]{2,1,0:T(8,128)(2,1)}), bf16[16,24,1792]{2,1,0:T(8,128)(2,1)S(1)}, u32[]{:S(2)}, u32[]{:S(2)}) %all-to-all-start.1) | async-done | bytes 1376288 | tf_op jit(solution)/shard_map/all_to_all | solution.py:64
  209.5 16.3 %all_to_all.29 = bf16[8,8,1792]{2,1,0:T(8,128)(2,1)S(1)} all-to-all(bf16[8,8,1792]{2,1,0:T(8,128)(2,1)S(1)} %fusion.2), channel_id=1, replica_groups=mesh['zlo'=4,'core'=2,'x'=4,'y'=4,'zhi'=2] {'zlo','zhi'}, dimensions={0} | all-to-all | bytes 458752 | tf_op jit(solution)/shard_map/all_to_all | solution.py:64
  (109 shorter events, 9.7 us)
Async XLA Ops:
  0.6 14.4 %copy-start.6 = (bf16[256,128]{1,0:T(8,128)(2,1)S(1)}, bf16[256,128]{1,0:T(8,128)(2,1)}, u32[]{:S(2)}) copy-start(bf16[256,128]{1,0:T(8,128)(2,1)} %q_rope_ref.1) | copy-start | bytes 196612
  0.6 14.5 %copy-start.12 = (f32[8,8]{1,0:T(8,128)S(1)}, f32[8,8]{1,0:T(8,128)}, u32[]{:S(2)}) copy-start(f32[8,8]{1,0:T(8,128)} %param.28) | copy-start | bytes 772
  0.7 14.5 %copy-start.11 = (s32[8,8]{1,0:T(8,128)S(1)}, s32[8,8]{1,0:T(8,128)}, u32[]{:S(2)}) copy-start(s32[8,8]{1,0:T(8,128)} %param.27) | copy-start | bytes 772
  2.0 1.0 copy-start
  3.0 0.8 copy-start.5
  3.9 11.7 %copy-start.3 = (bf16[256,512]{1,0:T(8,128)(2,1)S(1)}, bf16[256,512]{1,0:T(8,128)(2,1)}, u32[]{:S(2)}) copy-start(bf16[256,512]{1,0:T(8,128)(2,1)} %refs_7_.1) | copy-start | bytes 786436
  6.0 14.3 %collective-permute-start = (bf16[64,1152]{1,0:T(8,128)(2,1)}, bf16[64,1152]{1,0:T(8,128)(2,1)S(1)}, u32[]{:S(2)}, u32[]{:S(2)}) collective-permute-start(bf16[64,1152]{1,0:T(8,128)(2,1)} %get-tuple-element.28), channel_id=1, source_target_pairs={{0,64},{64,128},{128,192},{192,0},{1,65},{65,129},{129,193},{193,1... | collective-permute-start | bytes 442376 | tf_op jit(solution)/shard_map/ppermute | solution.py:83
  7.9 12.9 %collective-permute-start.1 = (bf16[64,1152]{1,0:T(8,128)(2,1)}, bf16[64,1152]{1,0:T(8,128)(2,1)}, u32[]{:S(2)}, u32[]{:S(2)}) collective-permute-start(bf16[64,1152]{1,0:T(8,128)(2,1)} %get-tuple-element.29), channel_id=1, source_target_pairs={{0,128},{64,192},{128,0},{192,64},{1,129},{65,193},{129,1},{193,65... | collective-permute-start | bytes 442376 | tf_op jit(solution)/shard_map/ppermute | solution.py:83
  10.2 12.7 %collective-permute-start.2 = (bf16[64,1152]{1,0:T(8,128)(2,1)}, bf16[64,1152]{1,0:T(8,128)(2,1)}, u32[]{:S(2)}, u32[]{:S(2)}) collective-permute-start(bf16[64,1152]{1,0:T(8,128)(2,1)} %get-tuple-element.30), channel_id=1, source_target_pairs={{0,192},{64,0},{128,64},{192,128},{1,193},{65,1},{129,65},{193,129... | collective-permute-start | bytes 442376 | tf_op jit(solution)/shard_map/ppermute | solution.py:83
  11.3 11.6 %collective-permute-start.3 = (bf16[512,512]{1,0:T(8,128)(2,1)}, bf16[512,512]{1,0:T(8,128)(2,1)}, u32[]{:S(2)}, u32[]{:S(2)}) collective-permute-start(bf16[512,512]{1,0:T(8,128)(2,1)} %bitcast.74), channel_id=1, source_target_pairs={{0,32},{32,0},{1,33},{33,1},{2,34},{34,2},{3,35},{35,3},{4,36},{36... | collective-permute-start | bytes 1572872 | tf_op jit(solution)/shard_map/ppermute | solution.py:374
  11.3 9.0 %collective-permute-start.4 = (bf16[64,512]{1,0:T(8,128)(2,1)}, bf16[64,512]{1,0:T(8,128)(2,1)}, u32[]{:S(2)}, u32[]{:S(2)}) collective-permute-start(bf16[64,512]{1,0:T(8,128)(2,1)} %bitcast.76), channel_id=1, source_target_pairs={{0,32},{32,0},{1,33},{33,1},{2,34},{34,2},{3,35},{35,3},{4,36},{36... | collective-permute-start | bytes 196616 | tf_op jit(solution)/shard_map/ppermute | solution.py:374
  11.8 8.5 %copy-start.1 = (bf16[1,896,1024]{2,1,0:T(8,128)(2,1)S(1)}, bf16[1,896,1024]{2,1,0:T(8,128)(2,1)}, u32[]{:S(2)}) copy-start(bf16[1,896,1024]{2,1,0:T(8,128)(2,1)} %param.29) | copy-start | bytes 5505028
  11.8 11.1 %copy-start.4 = (bf16[2,512,128]{2,1,0:T(8,128)(2,1)S(1)}, bf16[2,512,128]{2,1,0:T(8,128)(2,1)}, u32[]{:S(2)}) copy-start(bf16[2,512,128]{2,1,0:T(8,128)(2,1)} %refs_8_.3) | copy-start | bytes 786436
  11.8 11.1 %copy-start.7 = (bf16[1,512,512]{2,1,0:T(8,128)(2,1)S(1)}, bf16[1,512,512]{2,1,0:T(8,128)(2,1)}, u32[]{:S(2)}) copy-start(bf16[1,512,512]{2,1,0:T(8,128)(2,1)} %param.20) | copy-start | bytes 1572868
  20.2 91.8 %collective-permute-start.19 = (bf16[896,1024]{1,0:T(8,128)(2,1)S(1)}, bf16[896,1024]{1,0:T(8,128)(2,1)}, u32[]{:S(2)}, u32[]{:S(2)}) collective-permute-start(bf16[896,1024]{1,0:T(8,128)(2,1)S(1)} %bitcast.70), channel_id=1, source_target_pairs={{0,32},{32,0},{1,33},{33,1},{2,34},{34,2},{3,35},{35,3},{4,36},{36... | collective-permute-start | bytes 5505032 | tf_op jit(solution)/shard_map/ppermute | solution.py:374
  22.9 0.8 copy-start.9
  27.5 5.7 %collective-permute-start.5 = (bf16[64,384]{1,0:T(8,128)(2,1)S(1)}, bf16[64,384]{1,0:T(8,128)(2,1)S(1)}, u32[]{:S(2)}, u32[]{:S(2)}) collective-permute-start(bf16[64,384]{1,0:T(8,128)(2,1)S(1)} %get-tuple-element.32), channel_id=1, source_target_pairs={{0,192},{64,0},{128,64},{192,128},{1,193},{65,1},{129,65},{193,129... | collective-permute-start | bytes 147464 | tf_op jit(solution)/shard_map/ppermute | solution.py:83
  27.6 5.6 %collective-permute-start.6 = (bf16[64,384]{1,0:T(8,128)(2,1)S(1)}, bf16[64,384]{1,0:T(8,128)(2,1)S(1)}, u32[]{:S(2)}, u32[]{:S(2)}) collective-permute-start(bf16[64,384]{1,0:T(8,128)(2,1)S(1)} %get-tuple-element.33), channel_id=1, source_target_pairs={{0,128},{64,192},{128,0},{192,64},{1,129},{65,193},{129,1},{193,65... | collective-permute-start | bytes 147464 | tf_op jit(solution)/shard_map/ppermute | solution.py:83
  29.0 5.0 %collective-permute-start.7 = (bf16[64,384]{1,0:T(8,128)(2,1)S(1)}, bf16[64,384]{1,0:T(8,128)(2,1)S(1)}, u32[]{:S(2)}, u32[]{:S(2)}) collective-permute-start(bf16[64,384]{1,0:T(8,128)(2,1)S(1)} %get-tuple-element.34), channel_id=1, source_target_pairs={{0,64},{64,128},{128,192},{192,0},{1,65},{65,129},{129,193},{193,1... | collective-permute-start | bytes 147464 | tf_op jit(solution)/shard_map/ppermute | solution.py:83
  39.6 23.9 %collective-permute-start.10 = (bf16[64,7168]{1,0:T(8,128)(2,1)}, bf16[64,7168]{1,0:T(8,128)(2,1)}, u32[]{:S(2)}, u32[]{:S(2)}) collective-permute-start(bf16[64,7168]{1,0:T(8,128)(2,1)} %get-tuple-element.38), channel_id=1, source_target_pairs={{0,24},{1,25},{2,26},{3,27},{4,28},{5,29},{6,30},{7,31},{8,0},{9,1... | collective-permute-start | bytes 2752520 | tf_op jit(solution)/shard_map/ppermute | solution.py:418
  42.4 24.8 %collective-permute-start.9 = (bf16[64,7168]{1,0:T(8,128)(2,1)}, bf16[64,7168]{1,0:T(8,128)(2,1)}, u32[]{:S(2)}, u32[]{:S(2)}) collective-permute-start(bf16[64,7168]{1,0:T(8,128)(2,1)} %get-tuple-element.37), channel_id=1, source_target_pairs={{0,8},{1,9},{2,10},{3,11},{4,12},{5,13},{6,14},{7,15},{8,16},{9,17... | collective-permute-start | bytes 2752520 | tf_op jit(solution)/shard_map/ppermute | solution.py:418
  42.4 24.8 %collective-permute-start.8 = (bf16[64,7168]{1,0:T(8,128)(2,1)}, bf16[64,7168]{1,0:T(8,128)(2,1)}, u32[]{:S(2)}, u32[]{:S(2)}) collective-permute-start(bf16[64,7168]{1,0:T(8,128)(2,1)} %get-tuple-element.36), channel_id=1, source_target_pairs={{0,16},{1,17},{2,18},{3,19},{4,20},{5,21},{6,22},{7,23},{8,24},{9,... | collective-permute-start | bytes 2752520 | tf_op jit(solution)/shard_map/ppermute | solution.py:418
  44.9 7.7 %collective-permute-start.15 = (bf16[4,8,32]{2,1,0:T(8,128)(2,1)S(1)}, bf16[4,8,32]{2,1,0:T(8,128)(2,1)S(1)}, u32[]{:S(2)}, u32[]{:S(2)}) collective-permute-start(bf16[4,8,32]{2,1,0:T(8,128)(2,1)S(1)} %pad_maximum_fusion.2), channel_id=1, source_target_pairs={{0,1},{1,0},{2,3},{3,2},{4,5},{5,4},{6,7},{7,6},{8,9},{9,8},{10,11... | collective-permute-start | bytes 6152 | tf_op jit(solution)/shard_map/ppermute | solution.py:447
  52.6 59.4 %collective-permute-start.20 = (bf16[896,1024]{1,0:T(8,128)(2,1)}, bf16[896,1024]{1,0:T(8,128)(2,1)}, u32[]{:S(2)}, u32[]{:S(2)}) collective-permute-start(bf16[896,1024]{1,0:T(8,128)(2,1)} %bitcast.80), channel_id=1, source_target_pairs={{0,32},{32,0},{1,33},{33,1},{2,34},{34,2},{3,35},{35,3},{4,36},{36... | collective-permute-start | bytes 5505032 | tf_op jit(solution)/shard_map/ppermute | solution.py:374
  69.3 11.9 %copy-start.8 = (bf16[8,7168]{1,0:T(8,128)(2,1)S(1)}, bf16[8,7168]{1,0:T(8,128)(2,1)}, u32[]{:S(2)}) copy-start(bf16[8,7168]{1,0:T(8,128)(2,1)} %residual_ref.1) | copy-start | bytes 344068
  70.1 25.3 %copy-start.10 = (f32[7168]{0:T(1024)S(1)}, f32[7168]{0:T(1024)}, u32[]{:S(2)}) copy-start(f32[7168]{0:T(1024)} %param.26) | copy-start | bytes 86020
  70.1 7.4 %collective-permute-start.11 = (bf16[16,7168]{1,0:T(8,128)(2,1)}, bf16[16,7168]{1,0:T(8,128)(2,1)S(1)}, u32[]{:S(2)}, u32[]{:S(2)}) collective-permute-start(bf16[16,7168]{1,0:T(8,128)(2,1)} %get-tuple-element.58), channel_id=1, source_target_pairs={{0,2},{1,3},{2,4},{3,5},{4,6},{5,7},{6,0},{7,1},{8,10},{9,11},{10,... | collective-permute-start | bytes 688136 | tf_op jit(solution)/shard_map/ppermute | solution.py:420
  71.7 9.6 %collective-permute-start.12 = (bf16[16,7168]{1,0:T(8,128)(2,1)S(1)}, bf16[16,7168]{1,0:T(8,128)(2,1)S(1)}, u32[]{:S(2)}, u32[]{:S(2)}) collective-permute-start(bf16[16,7168]{1,0:T(8,128)(2,1)S(1)} %get-tuple-element.57), channel_id=1, source_target_pairs={{0,4},{1,5},{2,6},{3,7},{4,0},{5,1},{6,2},{7,3},{8,12},{9,13},{10,... | collective-permute-start | bytes 688136 | tf_op jit(solution)/shard_map/ppermute | solution.py:420
  74.6 6.7 %collective-permute-start.13 = (bf16[16,7168]{1,0:T(8,128)(2,1)S(1)}, bf16[16,7168]{1,0:T(8,128)(2,1)S(1)}, u32[]{:S(2)}, u32[]{:S(2)}) collective-permute-start(bf16[16,7168]{1,0:T(8,128)(2,1)S(1)} %get-tuple-element.56), channel_id=1, source_target_pairs={{0,6},{1,7},{2,0},{3,1},{4,2},{5,3},{6,4},{7,5},{8,14},{9,15},{10,... | collective-permute-start | bytes 688136 | tf_op jit(solution)/shard_map/ppermute | solution.py:420
  82.1 13.3 %collective-permute-start.14 = (bf16[16,7168]{1,0:T(8,128)(2,1)}, bf16[16,7168]{1,0:T(8,128)(2,1)S(1)}, u32[]{:S(2)}, u32[]{:S(2)}) collective-permute-start(bf16[16,7168]{1,0:T(8,128)(2,1)} %get-tuple-element.40), channel_id=1, source_target_pairs={{0,1},{1,0},{2,3},{3,2},{4,5},{5,4},{6,7},{7,6},{8,9},{9,8},{10,11... | collective-permute-start | bytes 688136 | tf_op jit(solution)/shard_map/ppermute | solution.py:430
  96.2 4.2 %collective-permute-start.18 = (bf16[16,1792]{1,0:T(8,128)(2,1)S(1)}, bf16[16,1792]{1,0:T(8,128)(2,1)S(1)}, u32[]{:S(2)}, u32[]{:S(2)}) collective-permute-start(bf16[16,1792]{1,0:T(8,128)(2,1)S(1)} %get-tuple-element.45), channel_id=1, source_target_pairs={{0,64},{64,128},{128,192},{192,0},{1,65},{65,129},{129,193},{193,1... | collective-permute-start | bytes 172040 | tf_op jit(solution)/shard_map/ppermute | solution.py:83
  98.1 5.1 %collective-permute-start.17 = (bf16[16,1792]{1,0:T(8,128)(2,1)S(1)}, bf16[16,1792]{1,0:T(8,128)(2,1)S(1)}, u32[]{:S(2)}, u32[]{:S(2)}) collective-permute-start(bf16[16,1792]{1,0:T(8,128)(2,1)S(1)} %get-tuple-element.44), channel_id=1, source_target_pairs={{0,128},{64,192},{128,0},{192,64},{1,129},{65,193},{129,1},{193,65... | collective-permute-start | bytes 172040 | tf_op jit(solution)/shard_map/ppermute | solution.py:83
  99.6 4.2 %collective-permute-start.16 = (bf16[16,1792]{1,0:T(8,128)(2,1)S(1)}, bf16[16,1792]{1,0:T(8,128)(2,1)S(1)}, u32[]{:S(2)}, u32[]{:S(2)}) collective-permute-start(bf16[16,1792]{1,0:T(8,128)(2,1)S(1)} %get-tuple-element.43), channel_id=1, source_target_pairs={{0,192},{64,0},{128,64},{192,128},{1,193},{65,1},{129,65},{193,129... | collective-permute-start | bytes 172040 | tf_op jit(solution)/shard_map/ppermute | solution.py:83
  105.5 24.0 %all-to-all-start = ((bf16[16,24,1792]{2,1,0:T(8,128)(2,1)}), bf16[16,24,1792]{2,1,0:T(8,128)(2,1)S(1)}, u32[]{:S(2)}, u32[]{:S(2)}) async-start(bf16[16,24,1792]{2,1,0:T(8,128)(2,1)} %bitcast.79), calls=%async_computation | async-start | bytes 2752512 | tf_op jit(solution)/shard_map/all_to_all | solution.py:64
  111.7 61.3 %collective-permute-start.31 = (bf16[1024,896]{1,0:T(8,128)(2,1)}, bf16[1024,896]{1,0:T(8,128)(2,1)}, u32[]{:S(2)}, u32[]{:S(2)}) collective-permute-start(bf16[1024,896]{1,0:T(8,128)(2,1)} %bitcast.72), channel_id=1, source_target_pairs={{0,32},{32,0},{1,33},{33,1},{2,34},{34,2},{3,35},{35,3},{4,36},{36... | collective-permute-start | bytes 5505032 | tf_op jit(solution)/shard_map/ppermute | solution.py:374
  135.5 12.1 %collective-permute-start.24 = (bf16[192,1024]{1,0:T(8,128)(2,1)S(1)}, bf16[192,1024]{1,0:T(8,128)(2,1)S(1)}, u32[]{:S(2)}, u32[]{:S(2)}) collective-permute-start(bf16[192,1024]{1,0:T(8,128)(2,1)S(1)} %get-tuple-element.51), channel_id=1, source_target_pairs={{0,64},{64,0},{128,192},{192,128},{1,65},{65,1},{129,193},{193,129... | collective-permute-start | bytes 1179656 | tf_op jit(solution)/shard_map/ppermute | solution.py:474
  135.9 18.8 %collective-permute-start.23 = (bf16[96,1024]{1,0:T(8,128)(2,1)S(1)}, bf16[96,1024]{1,0:T(8,128)(2,1)S(1)}, u32[]{:S(2)}, u32[]{:S(2)}) collective-permute-start(bf16[96,1024]{1,0:T(8,128)(2,1)S(1)} %get-tuple-element.49), channel_id=1, source_target_pairs={{0,192},{64,0},{128,64},{192,128},{1,193},{65,1},{129,65},{193,129... | collective-permute-start | bytes 589832 | tf_op jit(solution)/shard_map/ppermute | solution.py:83
  137.6 17.1 %collective-permute-start.22 = (bf16[96,1024]{1,0:T(8,128)(2,1)S(1)}, bf16[96,1024]{1,0:T(8,128)(2,1)S(1)}, u32[]{:S(2)}, u32[]{:S(2)}) collective-permute-start(bf16[96,1024]{1,0:T(8,128)(2,1)S(1)} %get-tuple-element.48), channel_id=1, source_target_pairs={{0,128},{64,192},{128,0},{192,64},{1,129},{65,193},{129,1},{193,65... | collective-permute-start | bytes 589832 | tf_op jit(solution)/shard_map/ppermute | solution.py:83
  140.0 18.5 %collective-permute-start.21 = (bf16[96,1024]{1,0:T(8,128)(2,1)S(1)}, bf16[96,1024]{1,0:T(8,128)(2,1)S(1)}, u32[]{:S(2)}, u32[]{:S(2)}) collective-permute-start(bf16[96,1024]{1,0:T(8,128)(2,1)S(1)} %get-tuple-element.47), channel_id=1, source_target_pairs={{0,64},{64,128},{128,192},{192,0},{1,65},{65,129},{129,193},{193,1... | collective-permute-start | bytes 589832 | tf_op jit(solution)/shard_map/ppermute | solution.py:83
  147.6 31.2 %copy-start.2 = (bf16[1,1024,896]{2,1,0:T(8,128)(2,1)S(1)}, bf16[1,1024,896]{2,1,0:T(8,128)(2,1)}, u32[]{:S(2)}) copy-start(bf16[1,1024,896]{2,1,0:T(8,128)(2,1)} %param.31) | copy-start | bytes 5505028
  147.8 12.7 %collective-permute-start.25 = (bf16[96,1024]{1,0:T(8,128)(2,1)S(1)}, bf16[96,1024]{1,0:T(8,128)(2,1)S(1)}, u32[]{:S(2)}, u32[]{:S(2)}) collective-permute-start(bf16[96,1024]{1,0:T(8,128)(2,1)S(1)} %slice.126), channel_id=1, source_target_pairs={{0,128},{64,192},{128,0},{192,64},{1,129},{65,193},{129,1},{193,65... | collective-permute-start | bytes 589832 | tf_op jit(solution)/shard_map/ppermute | solution.py:476
  160.8 6.6 %collective-permute-start.29 = (bf16[96,512]{1,0:T(8,128)(2,1)S(1)}, bf16[96,512]{1,0:T(8,128)(2,1)S(1)}, u32[]{:S(2)}, u32[]{:S(2)}) collective-permute-start(bf16[96,512]{1,0:T(8,128)(2,1)S(1)} %get-tuple-element.62), channel_id=1, source_target_pairs={{0,128},{64,192},{128,0},{192,64},{1,129},{65,193},{129,1},{193,65... | collective-permute-start | bytes 294920 | tf_op jit(solution)/shard_map/ppermute | solution.py:480
  167.4 11.4 %collective-permute-start.30 = (bf16[192,512]{1,0:T(8,128)(2,1)S(1)}, bf16[192,512]{1,0:T(8,128)(2,1)S(1)}, u32[]{:S(2)}, u32[]{:S(2)}) collective-permute-start(bf16[192,512]{1,0:T(8,128)(2,1)S(1)} %pad_maximum_fusion.refs_4_), channel_id=1, source_target_pairs={{0,64},{64,0},{128,192},{192,128},{1,65},{65,1},{129,193},{193,129... | collective-permute-start | bytes 589832 | tf_op jit(solution)/shard_map/ppermute | solution.py:482
  170.5 4.7 %collective-permute-start.26 = (bf16[96,512]{1,0:T(8,128)(2,1)S(1)}, bf16[96,512]{1,0:T(8,128)(2,1)S(1)}, u32[]{:S(2)}, u32[]{:S(2)}) collective-permute-start(bf16[96,512]{1,0:T(8,128)(2,1)S(1)} %get-tuple-element.63.refs_0_), channel_id=1, source_target_pairs={{0,64},{64,128},{128,192},{192,0},{1,65},{65,129},{129,193},{193,1... | collective-permute-start | bytes 294920 | tf_op jit(solution)/shard_map/ppermute | solution.py:83
  171.5 5.5 %collective-permute-start.27 = (bf16[96,512]{1,0:T(8,128)(2,1)S(1)}, bf16[96,512]{1,0:T(8,128)(2,1)S(1)}, u32[]{:S(2)}, u32[]{:S(2)}) collective-permute-start(bf16[96,512]{1,0:T(8,128)(2,1)S(1)} %get-tuple-element.63.refs_0_), channel_id=1, source_target_pairs={{0,128},{64,192},{128,0},{192,64},{1,129},{65,193},{129,1},{193,65... | collective-permute-start | bytes 294920 | tf_op jit(solution)/shard_map/ppermute | solution.py:83
  173.0 5.8 %collective-permute-start.28 = (bf16[96,512]{1,0:T(8,128)(2,1)S(1)}, bf16[96,512]{1,0:T(8,128)(2,1)S(1)}, u32[]{:S(2)}, u32[]{:S(2)}) collective-permute-start(bf16[96,512]{1,0:T(8,128)(2,1)S(1)} %get-tuple-element.63.refs_0_), channel_id=1, source_target_pairs={{0,192},{64,0},{128,64},{192,128},{1,193},{65,1},{129,65},{193,129... | collective-permute-start | bytes 294920 | tf_op jit(solution)/shard_map/ppermute | solution.py:83
  183.2 25.5 %all-to-all-start.1 = ((bf16[16,24,1792]{2,1,0:T(8,128)(2,1)}), bf16[16,24,1792]{2,1,0:T(8,128)(2,1)S(1)}, u32[]{:S(2)}, u32[]{:S(2)}) async-start(bf16[16,24,1792]{2,1,0:T(8,128)(2,1)} %bitcast.27), calls=%async_computation.1 | async-start | bytes 2752512 | tf_op jit(solution)/shard_map/all_to_all | solution.py:64

commit v6 on v5

--- a/solution.py
+++ b/solution.py
@@ -15,7 +15,7 @@
 CAP = 3
 ROWS = 8
 LINE_ORDER = (2, 1, 3)
-UP_STEPS = 4
+UP_STEPS = 2
 FLIP_ORDER = (0, 2, 1, 3)
 
 SIDE = 4

time: 227 us -> 227 us (level)
  transfers between devices with their start and end apart: 34 -> 34, of which waited for: 21 -> 21; matrix products, arithmetic and copies ran while one was open for 8% -> 8% of each run, Pallas kernels for 8% -> 7%
where the time goes in v6:
time: 227 us; the launch traced here: 226 us
  waiting for transfers between devices  91.2 us (40%)
  starting transfers between devices  71.2 us (31%)
  Pallas kernels  23.1 us (10%)
  blocking collectives  16.3 us (7%)
  local copies, waits for them, and re-layouts  12.8 us (6%)
  other arithmetic  7.89 us (3%)
  matrix products  2.42 us (1%)
    all_to_all x2, waiting for transfers between devices, exchange(): return lax.all_to_all(value, axes, 0, 0, tiled=True)  35.7 us
    pallas_call x7, Pallas kernels, on_chip(): pl.pallas_call(kernel, out_shape=[jax.ShapeDtypeStruct(shape, dtype) for...  23.1 us
    ppermute x15, starting transfers between devices, along_line(): lax.ppermute(parts[k], 'zlo', shift(sign * k))  20.5 us
    ppermute x15, waiting for transfers between devices, along_line(): lax.ppermute(parts[k], 'zlo', shift(sign * k))  18.4 us
    all_to_all x1, blocking collectives, exchange(): return lax.all_to_all(value, axes, 0, 0, tiled=True)  16.3 us
    ppermute x3, waiting for transfers between devices, body(): lax.ppermute(first[k], ALL, plane_shift(k, 0))  13.8 us
    all_to_all x2, starting transfers between devices, exchange(): return lax.all_to_all(value, axes, 0, 0, tiled=True)  13.3 us
    ppermute x1, starting transfers between devices, body(): lax.ppermute(up_sums[line_rows:].astype(BF), 'zlo', flips(LINES, 2))  6.9 us
  transfers between devices with their start and end apart: 34, of which 21 were waited for; matrix products, arithmetic and copies ran while one was open for 8% of the time, Pallas kernels for 7%

profile of v6, /device:TPU:32, one launch (start us, length us, event | category | flops | bytes accessed | tf_op | source)
XLA Modules:
  0.0 226.0 jit_solution(9704012886020244481)
XLA Ops:
  0.7 0.8 reshape.335
  2.0 1.0 copy-done
  3.0 0.8 copy-done.5
  3.9 2.1 shard_map.167
  6.0 1.9 collective-permute-start
  7.9 2.3 %collective-permute-start.1 = (bf16[64,1152]{1,0:T(8,128)(2,1)}, bf16[64,1152]{1,0:T(8,128)(2,1)}, u32[]{:S(2)}, u32[]{:S(2)}) collective-permute-start(bf16[64,1152]{1,0:T(8,128)(2,1)} %get-tuple-element.29), channel_id=1, source_target_pairs={{0,128},{64,192},{128,0},{192,64},{1,129},{65,193},{129,1},{193,65... | collective-permute-start | bytes 442376 | tf_op jit(solution)/shard_map/ppermute | solution.py:83
  10.2 1.1 collective-permute-start.2
  11.8 3.3 %fusion.66 = (bf16[256,1,512]{2,1,0:T(2,128)(2,1)}, bf16[256,1,512]{2,1,0:T(2,128)(2,1)}) fusion(bf16[256,2,512]{2,1,0:T(2,128)(2,1)} %q_latent_ref.1), kind=kLoop, calls=%fused_computation.162 | loop fusion | bytes 1048576 | tf_op jit(solution)/shard_map/slice | solution.py:402
  15.6 1.4 fusion.3
  17.0 0.8 fusion.24
  17.8 0.8 copy.62
  18.7 0.9 broadcast_multiply_fusion.refs_6_
  20.8 2.1 collective-permute-done.2.refs_3_
  22.9 0.8 copy-done.9
  23.7 3.7 %shard_map.168 = (bf16[64,384]{1,0:T(8,128)(2,1)S(1)}, bf16[64,384]{1,0:T(8,128)(2,1)S(1)}, bf16[64,384]{1,0:T(8,128)(2,1)S(1)}, bf16[64,384]{1,0:T(8,128)(2,1)S(1)}) custom-call(bf16[64,1152]{1,0:T(8,128)(2,1)S(1)} %get-tuple-element.27.refs_0_, bf16[64,1152]{1,0:T(8,128)(2,1)S(1)} %collective-permute-done.refs_1_, ...), custom_call_target="tpu_custom_call" | custom-call | tf_op jit(solution)/shard_map/pallas_call | solution.py:316
  27.6 1.4 collective-permute-start.6
  29.0 2.8 %collective-permute-start.7 = (bf16[64,384]{1,0:T(8,128)(2,1)S(1)}, bf16[64,384]{1,0:T(8,128)(2,1)S(1)}, u32[]{:S(2)}, u32[]{:S(2)}) collective-permute-start(bf16[64,384]{1,0:T(8,128)(2,1)S(1)} %get-tuple-element.34), channel_id=1, source_target_pairs={{0,64},{64,128},{128,192},{192,0},{1,65},{65,129},{129,193},{193,1... | collective-permute-start | bytes 147464 | tf_op jit(solution)/shard_map/ppermute | solution.py:83
  31.9 1.3 collective-permute-done.5.refs_1_
  33.1 0.8 collective-permute-done.7.refs_3_
  34.0 5.7 %shard_map.169 = (bf16[64,7168]{1,0:T(8,128)(2,1)S(1)}, bf16[64,7168]{1,0:T(8,128)(2,1)}, bf16[64,7168]{1,0:T(8,128)(2,1)}, bf16[64,7168]{1,0:T(8,128)(2,1)}) custom-call(bf16[64,384]{1,0:T(8,128)(2,1)S(1)} %get-tuple-element.31.refs_0_, bf16[64,384]{1,0:T(8,128)(2,1)S(1)} %collective-permute-done.5.refs_1_, ...), custom_call_target="tpu_custom_call" | custom-call | tf_op jit(solution)/shard_map/pallas_call | solution.py:316
  39.6 2.8 %collective-permute-start.10 = (bf16[64,7168]{1,0:T(8,128)(2,1)}, bf16[64,7168]{1,0:T(8,128)(2,1)}, u32[]{:S(2)}, u32[]{:S(2)}) collective-permute-start(bf16[64,7168]{1,0:T(8,128)(2,1)} %get-tuple-element.38), channel_id=1, source_target_pairs={{0,24},{1,25},{2,26},{3,27},{4,28},{5,29},{6,30},{7,31},{8,0},{9,1... | collective-permute-start | bytes 2752520 | tf_op jit(solution)/shard_map/ppermute | solution.py:418
  42.4 2.3 %collective-permute-start.8 = (bf16[64,7168]{1,0:T(8,128)(2,1)}, bf16[64,7168]{1,0:T(8,128)(2,1)}, u32[]{:S(2)}, u32[]{:S(2)}) collective-permute-start(bf16[64,7168]{1,0:T(8,128)(2,1)} %get-tuple-element.36), channel_id=1, source_target_pairs={{0,16},{1,17},{2,18},{3,19},{4,20},{5,21},{6,22},{7,23},{8,24},{9,... | collective-permute-start | bytes 2752520 | tf_op jit(solution)/shard_map/ppermute | solution.py:418
  44.9 6.0 %collective-permute-start.15 = (bf16[4,8,32]{2,1,0:T(8,128)(2,1)S(1)}, bf16[4,8,32]{2,1,0:T(8,128)(2,1)S(1)}, u32[]{:S(2)}, u32[]{:S(2)}) collective-permute-start(bf16[4,8,32]{2,1,0:T(8,128)(2,1)S(1)} %pad_maximum_fusion.2), channel_id=1, source_target_pairs={{0,1},{1,0},{2,3},{3,2},{4,5},{5,4},{6,7},{7,6},{8,9},{9,8},{10,11... | collective-permute-start | bytes 6152 | tf_op jit(solution)/shard_map/ppermute | solution.py:447
  50.9 0.8 broadcast_in_dim.65
  51.8 0.7 broadcast_in_dim.74
  53.4 10.1 %collective-permute-done.10 = bf16[64,7168]{1,0:T(8,128)(2,1)} collective-permute-done((bf16[64,7168]{1,0:T(8,128)(2,1)}, bf16[64,7168]{1,0:T(8,128)(2,1)}, u32[]{:S(2)}, u32[]{:S(2)}) %collective-permute-start.10) | collective-permute-done | bytes 917536 | tf_op jit(solution)/shard_map/ppermute | solution.py:418
  63.5 3.7 %collective-permute-done.9 = bf16[64,7168]{1,0:T(8,128)(2,1)} collective-permute-done((bf16[64,7168]{1,0:T(8,128)(2,1)}, bf16[64,7168]{1,0:T(8,128)(2,1)}, u32[]{:S(2)}, u32[]{:S(2)}) %collective-permute-start.9) | collective-permute-done | bytes 917536 | tf_op jit(solution)/shard_map/ppermute | solution.py:418
  67.1 2.2 add_convert_fusion
  69.3 0.7 fusion.65
  70.1 1.6 collective-permute-start.11
  71.7 2.9 %collective-permute-start.12 = (bf16[16,7168]{1,0:T(8,128)(2,1)S(1)}, bf16[16,7168]{1,0:T(8,128)(2,1)S(1)}, u32[]{:S(2)}, u32[]{:S(2)}) collective-permute-start(bf16[16,7168]{1,0:T(8,128)(2,1)S(1)} %get-tuple-element.57), channel_id=1, source_target_pairs={{0,4},{1,5},{2,6},{3,7},{4,0},{5,1},{6,2},{7,3},{8,12},{9,13},{10,... | collective-permute-start | bytes 688136 | tf_op jit(solution)/shard_map/ppermute | solution.py:420
  74.6 1.3 collective-permute-start.13
  76.3 1.2 collective-permute-done.11.refs_1_
  77.5 3.7 %collective-permute-done.12.refs_2_ = bf16[16,7168]{1,0:T(8,128)(2,1)S(1)} collective-permute-done((bf16[16,7168]{1,0:T(8,128)(2,1)S(1)}, bf16[16,7168]{1,0:T(8,128)(2,1)S(1)}, u32[]{:S(2)}, u32[]{:S(2)}) %collective-permute-start.12) | collective-permute-done | bytes 229408 | tf_op jit(solution)/shard_map/ppermute | solution.py:420
  81.2 0.8 shard_map.170
  82.1 5.9 %collective-permute-start.14 = (bf16[16,7168]{1,0:T(8,128)(2,1)}, bf16[16,7168]{1,0:T(8,128)(2,1)S(1)}, u32[]{:S(2)}, u32[]{:S(2)}) collective-permute-start(bf16[16,7168]{1,0:T(8,128)(2,1)} %get-tuple-element.40), channel_id=1, source_target_pairs={{0,1},{1,0},{2,3},{3,2},{4,5},{5,4},{6,7},{7,6},{8,9},{9,8},{10,11... | collective-permute-start | bytes 688136 | tf_op jit(solution)/shard_map/ppermute | solution.py:430
  89.0 6.4 %collective-permute-done.14.far_ref = bf16[16,7168]{1,0:T(8,128)(2,1)S(1)} collective-permute-done((bf16[16,7168]{1,0:T(8,128)(2,1)}, bf16[16,7168]{1,0:T(8,128)(2,1)S(1)}, u32[]{:S(2)}, u32[]{:S(2)}) %collective-permute-start.14) | collective-permute-done | bytes 229408 | tf_op jit(solution)/shard_map/ppermute | solution.py:430
  95.4 0.8 shard_map.171
  96.2 1.9 collective-permute-start.18
  98.1 1.5 collective-permute-start.17
  100.4 2.8 %collective-permute-done.17 = bf16[16,1792]{1,0:T(8,128)(2,1)S(1)} collective-permute-done((bf16[16,1792]{1,0:T(8,128)(2,1)S(1)}, bf16[16,1792]{1,0:T(8,128)(2,1)S(1)}, u32[]{:S(2)}, u32[]{:S(2)}) %collective-permute-start.17) | collective-permute-done | bytes 57376 | tf_op jit(solution)/shard_map/ppermute | solution.py:83
  103.8 1.7 convolution_convert_fusion
  105.5 6.2 %all-to-all-start = ((bf16[16,24,1792]{2,1,0:T(8,128)(2,1)}), bf16[16,24,1792]{2,1,0:T(8,128)(2,1)S(1)}, u32[]{:S(2)}, u32[]{:S(2)}) async-start(bf16[16,24,1792]{2,1,0:T(8,128)(2,1)} %bitcast.79), calls=%async_computation | async-start | bytes 2752512 | tf_op jit(solution)/shard_map/all_to_all | solution.py:64
  112.1 17.4 %all-to-all-done = bf16[16,24,1792]{2,1,0:T(8,128)(2,1)S(1)} async-done(((bf16[16,24,1792]{2,1,0:T(8,128)(2,1)}), bf16[16,24,1792]{2,1,0:T(8,128)(2,1)S(1)}, u32[]{:S(2)}, u32[]{:S(2)}) %all-to-all-start) | async-done | bytes 1376288 | tf_op jit(solution)/shard_map/all_to_all | solution.py:64
  129.4 5.6 %shard_map.172 = (bf16[96,1024]{1,0:T(8,128)(2,1)S(1)}, bf16[96,1024]{1,0:T(8,128)(2,1)S(1)}, bf16[96,1024]{1,0:T(8,128)(2,1)S(1)}, bf16[96,1024]{1,0:T(8,128)(2...) custom-call(s32[1]{0:T(128)} %bitcast.1.line_ref, bf16[384,1792]{1,0:T(8,128)(2,1)S(1)} %bitcast.69, ...), custom_call_target="tpu_custom_call" | custom-call | tf_op jit(solution)/shard_map/pallas_call | solution.py:316
  135.4 1.7 collective-permute-start.23
  137.2 2.3 %collective-permute-start.22 = (bf16[96,1024]{1,0:T(8,128)(2,1)S(1)}, bf16[96,1024]{1,0:T(8,128)(2,1)S(1)}, u32[]{:S(2)}, u32[]{:S(2)}) collective-permute-start(bf16[96,1024]{1,0:T(8,128)(2,1)S(1)} %get-tuple-element.48), channel_id=1, source_target_pairs={{0,128},{64,192},{128,0},{192,64},{1,129},{65,193},{129,1},{193,65... | collective-permute-start | bytes 589832 | tf_op jit(solution)/shard_map/ppermute | solution.py:83
  139.5 1.0 collective-permute-start.21
  140.5 6.7 %collective-permute-done.24 = bf16[192,1024]{1,0:T(8,128)(2,1)S(1)} collective-permute-done((bf16[192,1024]{1,0:T(8,128)(2,1)S(1)}, bf16[192,1024]{1,0:T(8,128)(2,1)S(1)}, u32[]{:S(2)}, u32[]{:S(2)}) %collective-permute-start.24) | collective-permute-done | bytes 393248 | tf_op jit(solution)/shard_map/ppermute | solution.py:474
  147.3 6.9 %collective-permute-start.25 = (bf16[96,1024]{1,0:T(8,128)(2,1)S(1)}, bf16[96,1024]{1,0:T(8,128)(2,1)S(1)}, u32[]{:S(2)}, u32[]{:S(2)}) collective-permute-start(bf16[96,1024]{1,0:T(8,128)(2,1)S(1)} %slice.126), channel_id=1, source_target_pairs={{0,128},{64,192},{128,0},{192,64},{1,129},{65,193},{129,1},{193,65... | collective-permute-start | bytes 589832 | tf_op jit(solution)/shard_map/ppermute | solution.py:476
  154.2 3.7 %collective-permute-done.21 = bf16[96,1024]{1,0:T(8,128)(2,1)S(1)} collective-permute-done((bf16[96,1024]{1,0:T(8,128)(2,1)S(1)}, bf16[96,1024]{1,0:T(8,128)(2,1)S(1)}, u32[]{:S(2)}, u32[]{:S(2)}) %collective-permute-start.21) | collective-permute-done | bytes 196640 | tf_op jit(solution)/shard_map/ppermute | solution.py:83
  158.0 2.1 collective-permute-done.25
  160.3 3.5 %collective-permute-start.29 = (bf16[96,512]{1,0:T(8,128)(2,1)S(1)}, bf16[96,512]{1,0:T(8,128)(2,1)S(1)}, u32[]{:S(2)}, u32[]{:S(2)}) collective-permute-start(bf16[96,512]{1,0:T(8,128)(2,1)S(1)} %get-tuple-element.62), channel_id=1, source_target_pairs={{0,128},{64,192},{128,0},{192,64},{1,129},{65,193},{129,1},{193,65... | collective-permute-start | bytes 294920 | tf_op jit(solution)/shard_map/ppermute | solution.py:480
  163.8 3.1 %collective-permute-done.29 = bf16[96,512]{1,0:T(8,128)(2,1)S(1)} collective-permute-done((bf16[96,512]{1,0:T(8,128)(2,1)S(1)}, bf16[96,512]{1,0:T(8,128)(2,1)S(1)}, u32[]{:S(2)}, u32[]{:S(2)}) %collective-permute-start.29) | collective-permute-done | bytes 98336 | tf_op jit(solution)/shard_map/ppermute | solution.py:480
  167.0 3.1 %collective-permute-start.30 = (bf16[192,512]{1,0:T(8,128)(2,1)S(1)}, bf16[192,512]{1,0:T(8,128)(2,1)S(1)}, u32[]{:S(2)}, u32[]{:S(2)}) collective-permute-start(bf16[192,512]{1,0:T(8,128)(2,1)S(1)} %pad_maximum_fusion.refs_4_), channel_id=1, source_target_pairs={{0,64},{64,0},{128,192},{192,128},{1,65},{65,1},{129,193},{193,129... | collective-permute-start | bytes 589832 | tf_op jit(solution)/shard_map/ppermute | solution.py:482
  170.0 1.0 collective-permute-start.26
  171.0 1.5 collective-permute-start.27
  172.6 2.2 collective-permute-done.26.refs_1_
  174.7 1.8 collective-permute-done.27.refs_2_
  176.5 1.8 collective-permute-done.28.refs_3_
  178.3 4.4 %shard_map.173 = bf16[384,1792]{1,0:T(8,128)(2,1)} custom-call(s32[1]{0:T(128)} %bitcast.1.line_ref, bf16[96,512]{1,0:T(8,128)(2,1)S(1)} %get-tuple-element.63.refs_0_, bf16[96,512]{1,0:T(8,128)(2,1)S(1)} %collective-permute-done.26.refs_1_, bf16[96,512]{1,0:T(8,128)(2,1)S(1)} %collective-permute-done.27.refs_2_, ...), custom_call_target="tpu_custom_call" | custom-call | tf_op jit(solution)/shard_map/pallas_call | solution.py:316
  182.7 7.0 %all-to-all-start.1 = ((bf16[16,24,1792]{2,1,0:T(8,128)(2,1)}), bf16[16,24,1792]{2,1,0:T(8,128)(2,1)S(1)}, u32[]{:S(2)}, u32[]{:S(2)}) async-start(bf16[16,24,1792]{2,1,0:T(8,128)(2,1)} %bitcast.27), calls=%async_computation.1 | async-start | bytes 2752512 | tf_op jit(solution)/shard_map/all_to_all | solution.py:64
  189.9 18.3 %all-to-all-done.1 = bf16[16,24,1792]{2,1,0:T(8,128)(2,1)S(1)} async-done(((bf16[16,24,1792]{2,1,0:T(8,128)(2,1)}), bf16[16,24,1792]{2,1,0:T(8,128)(2,1)S(1)}, u32[]{:S(2)}, u32[]{:S(2)}) %all-to-all-start.1) | async-done | bytes 1376288 | tf_op jit(solution)/shard_map/all_to_all | solution.py:64
  209.0 16.3 %all_to_all.29 = bf16[8,8,1792]{2,1,0:T(8,128)(2,1)S(1)} all-to-all(bf16[8,8,1792]{2,1,0:T(8,128)(2,1)S(1)} %fusion.2), channel_id=1, replica_groups=mesh['zlo'=4,'core'=2,'x'=4,'y'=4,'zhi'=2] {'zlo','zhi'}, dimensions={0} | all-to-all | bytes 458752 | tf_op jit(solution)/shard_map/all_to_all | solution.py:64
  (109 shorter events, 9.7 us)
Async XLA Ops:
  0.6 14.4 %copy-start.6 = (bf16[256,128]{1,0:T(8,128)(2,1)S(1)}, bf16[256,128]{1,0:T(8,128)(2,1)}, u32[]{:S(2)}) copy-start(bf16[256,128]{1,0:T(8,128)(2,1)} %q_rope_ref.1) | copy-start | bytes 196612
  0.6 14.5 %copy-start.12 = (f32[8,8]{1,0:T(8,128)S(1)}, f32[8,8]{1,0:T(8,128)}, u32[]{:S(2)}) copy-start(f32[8,8]{1,0:T(8,128)} %param.28) | copy-start | bytes 772
  0.7 14.5 %copy-start.11 = (s32[8,8]{1,0:T(8,128)S(1)}, s32[8,8]{1,0:T(8,128)}, u32[]{:S(2)}) copy-start(s32[8,8]{1,0:T(8,128)} %param.27) | copy-start | bytes 772
  2.0 1.0 copy-start
  3.0 0.8 copy-start.5
  3.9 11.7 %copy-start.3 = (bf16[256,512]{1,0:T(8,128)(2,1)S(1)}, bf16[256,512]{1,0:T(8,128)(2,1)}, u32[]{:S(2)}) copy-start(bf16[256,512]{1,0:T(8,128)(2,1)} %refs_7_.1) | copy-start | bytes 786436
  6.0 14.3 %collective-permute-start = (bf16[64,1152]{1,0:T(8,128)(2,1)}, bf16[64,1152]{1,0:T(8,128)(2,1)S(1)}, u32[]{:S(2)}, u32[]{:S(2)}) collective-permute-start(bf16[64,1152]{1,0:T(8,128)(2,1)} %get-tuple-element.28), channel_id=1, source_target_pairs={{0,64},{64,128},{128,192},{192,0},{1,65},{65,129},{129,193},{193,1... | collective-permute-start | bytes 442376 | tf_op jit(solution)/shard_map/ppermute | solution.py:83
  7.9 12.9 %collective-permute-start.1 = (bf16[64,1152]{1,0:T(8,128)(2,1)}, bf16[64,1152]{1,0:T(8,128)(2,1)}, u32[]{:S(2)}, u32[]{:S(2)}) collective-permute-start(bf16[64,1152]{1,0:T(8,128)(2,1)} %get-tuple-element.29), channel_id=1, source_target_pairs={{0,128},{64,192},{128,0},{192,64},{1,129},{65,193},{129,1},{193,65... | collective-permute-start | bytes 442376 | tf_op jit(solution)/shard_map/ppermute | solution.py:83
  10.2 12.7 %collective-permute-start.2 = (bf16[64,1152]{1,0:T(8,128)(2,1)}, bf16[64,1152]{1,0:T(8,128)(2,1)}, u32[]{:S(2)}, u32[]{:S(2)}) collective-permute-start(bf16[64,1152]{1,0:T(8,128)(2,1)} %get-tuple-element.30), channel_id=1, source_target_pairs={{0,192},{64,0},{128,64},{192,128},{1,193},{65,1},{129,65},{193,129... | collective-permute-start | bytes 442376 | tf_op jit(solution)/shard_map/ppermute | solution.py:83
  11.3 11.6 %collective-permute-start.3 = (bf16[512,512]{1,0:T(8,128)(2,1)}, bf16[512,512]{1,0:T(8,128)(2,1)}, u32[]{:S(2)}, u32[]{:S(2)}) collective-permute-start(bf16[512,512]{1,0:T(8,128)(2,1)} %bitcast.74), channel_id=1, source_target_pairs={{0,32},{32,0},{1,33},{33,1},{2,34},{34,2},{3,35},{35,3},{4,36},{36... | collective-permute-start | bytes 1572872 | tf_op jit(solution)/shard_map/ppermute | solution.py:374
  11.3 9.0 %collective-permute-start.4 = (bf16[64,512]{1,0:T(8,128)(2,1)}, bf16[64,512]{1,0:T(8,128)(2,1)}, u32[]{:S(2)}, u32[]{:S(2)}) collective-permute-start(bf16[64,512]{1,0:T(8,128)(2,1)} %bitcast.76), channel_id=1, source_target_pairs={{0,32},{32,0},{1,33},{33,1},{2,34},{34,2},{3,35},{35,3},{4,36},{36... | collective-permute-start | bytes 196616 | tf_op jit(solution)/shard_map/ppermute | solution.py:374
  11.8 8.5 %copy-start.1 = (bf16[1,896,1024]{2,1,0:T(8,128)(2,1)S(1)}, bf16[1,896,1024]{2,1,0:T(8,128)(2,1)}, u32[]{:S(2)}) copy-start(bf16[1,896,1024]{2,1,0:T(8,128)(2,1)} %param.29) | copy-start | bytes 5505028
  11.8 11.1 %copy-start.4 = (bf16[2,512,128]{2,1,0:T(8,128)(2,1)S(1)}, bf16[2,512,128]{2,1,0:T(8,128)(2,1)}, u32[]{:S(2)}) copy-start(bf16[2,512,128]{2,1,0:T(8,128)(2,1)} %refs_8_.3) | copy-start | bytes 786436
  11.8 11.1 %copy-start.7 = (bf16[1,512,512]{2,1,0:T(8,128)(2,1)S(1)}, bf16[1,512,512]{2,1,0:T(8,128)(2,1)}, u32[]{:S(2)}) copy-start(bf16[1,512,512]{2,1,0:T(8,128)(2,1)} %param.20) | copy-start | bytes 1572868
  20.2 91.8 %collective-permute-start.19 = (bf16[896,1024]{1,0:T(8,128)(2,1)S(1)}, bf16[896,1024]{1,0:T(8,128)(2,1)}, u32[]{:S(2)}, u32[]{:S(2)}) collective-permute-start(bf16[896,1024]{1,0:T(8,128)(2,1)S(1)} %bitcast.70), channel_id=1, source_target_pairs={{0,32},{32,0},{1,33},{33,1},{2,34},{34,2},{3,35},{35,3},{4,36},{36... | collective-permute-start | bytes 5505032 | tf_op jit(solution)/shard_map/ppermute | solution.py:374
  22.9 0.8 copy-start.9
  27.5 5.7 %collective-permute-start.5 = (bf16[64,384]{1,0:T(8,128)(2,1)S(1)}, bf16[64,384]{1,0:T(8,128)(2,1)S(1)}, u32[]{:S(2)}, u32[]{:S(2)}) collective-permute-start(bf16[64,384]{1,0:T(8,128)(2,1)S(1)} %get-tuple-element.32), channel_id=1, source_target_pairs={{0,192},{64,0},{128,64},{192,128},{1,193},{65,1},{129,65},{193,129... | collective-permute-start | bytes 147464 | tf_op jit(solution)/shard_map/ppermute | solution.py:83
  27.6 5.6 %collective-permute-start.6 = (bf16[64,384]{1,0:T(8,128)(2,1)S(1)}, bf16[64,384]{1,0:T(8,128)(2,1)S(1)}, u32[]{:S(2)}, u32[]{:S(2)}) collective-permute-start(bf16[64,384]{1,0:T(8,128)(2,1)S(1)} %get-tuple-element.33), channel_id=1, source_target_pairs={{0,128},{64,192},{128,0},{192,64},{1,129},{65,193},{129,1},{193,65... | collective-permute-start | bytes 147464 | tf_op jit(solution)/shard_map/ppermute | solution.py:83
  29.0 5.0 %collective-permute-start.7 = (bf16[64,384]{1,0:T(8,128)(2,1)S(1)}, bf16[64,384]{1,0:T(8,128)(2,1)S(1)}, u32[]{:S(2)}, u32[]{:S(2)}) collective-permute-start(bf16[64,384]{1,0:T(8,128)(2,1)S(1)} %get-tuple-element.34), channel_id=1, source_target_pairs={{0,64},{64,128},{128,192},{192,0},{1,65},{65,129},{129,193},{193,1... | collective-permute-start | bytes 147464 | tf_op jit(solution)/shard_map/ppermute | solution.py:83
  39.6 23.9 %collective-permute-start.10 = (bf16[64,7168]{1,0:T(8,128)(2,1)}, bf16[64,7168]{1,0:T(8,128)(2,1)}, u32[]{:S(2)}, u32[]{:S(2)}) collective-permute-start(bf16[64,7168]{1,0:T(8,128)(2,1)} %get-tuple-element.38), channel_id=1, source_target_pairs={{0,24},{1,25},{2,26},{3,27},{4,28},{5,29},{6,30},{7,31},{8,0},{9,1... | collective-permute-start | bytes 2752520 | tf_op jit(solution)/shard_map/ppermute | solution.py:418
  42.4 24.8 %collective-permute-start.9 = (bf16[64,7168]{1,0:T(8,128)(2,1)}, bf16[64,7168]{1,0:T(8,128)(2,1)}, u32[]{:S(2)}, u32[]{:S(2)}) collective-permute-start(bf16[64,7168]{1,0:T(8,128)(2,1)} %get-tuple-element.37), channel_id=1, source_target_pairs={{0,8},{1,9},{2,10},{3,11},{4,12},{5,13},{6,14},{7,15},{8,16},{9,17... | collective-permute-start | bytes 2752520 | tf_op jit(solution)/shard_map/ppermute | solution.py:418
  42.4 24.8 %collective-permute-start.8 = (bf16[64,7168]{1,0:T(8,128)(2,1)}, bf16[64,7168]{1,0:T(8,128)(2,1)}, u32[]{:S(2)}, u32[]{:S(2)}) collective-permute-start(bf16[64,7168]{1,0:T(8,128)(2,1)} %get-tuple-element.36), channel_id=1, source_target_pairs={{0,16},{1,17},{2,18},{3,19},{4,20},{5,21},{6,22},{7,23},{8,24},{9,... | collective-permute-start | bytes 2752520 | tf_op jit(solution)/shard_map/ppermute | solution.py:418
  44.9 7.7 %collective-permute-start.15 = (bf16[4,8,32]{2,1,0:T(8,128)(2,1)S(1)}, bf16[4,8,32]{2,1,0:T(8,128)(2,1)S(1)}, u32[]{:S(2)}, u32[]{:S(2)}) collective-permute-start(bf16[4,8,32]{2,1,0:T(8,128)(2,1)S(1)} %pad_maximum_fusion.2), channel_id=1, source_target_pairs={{0,1},{1,0},{2,3},{3,2},{4,5},{5,4},{6,7},{7,6},{8,9},{9,8},{10,11... | collective-permute-start | bytes 6152 | tf_op jit(solution)/shard_map/ppermute | solution.py:447
  52.6 59.4 %collective-permute-start.20 = (bf16[896,1024]{1,0:T(8,128)(2,1)}, bf16[896,1024]{1,0:T(8,128)(2,1)}, u32[]{:S(2)}, u32[]{:S(2)}) collective-permute-start(bf16[896,1024]{1,0:T(8,128)(2,1)} %bitcast.80), channel_id=1, source_target_pairs={{0,32},{32,0},{1,33},{33,1},{2,34},{34,2},{3,35},{35,3},{4,36},{36... | collective-permute-start | bytes 5505032 | tf_op jit(solution)/shard_map/ppermute | solution.py:374
  69.3 11.9 %copy-start.8 = (bf16[8,7168]{1,0:T(8,128)(2,1)S(1)}, bf16[8,7168]{1,0:T(8,128)(2,1)}, u32[]{:S(2)}) copy-start(bf16[8,7168]{1,0:T(8,128)(2,1)} %residual_ref.1) | copy-start | bytes 344068
  70.1 25.3 %copy-start.10 = (f32[7168]{0:T(1024)S(1)}, f32[7168]{0:T(1024)}, u32[]{:S(2)}) copy-start(f32[7168]{0:T(1024)} %param.26) | copy-start | bytes 86020
  70.1 7.4 %collective-permute-start.11 = (bf16[16,7168]{1,0:T(8,128)(2,1)}, bf16[16,7168]{1,0:T(8,128)(2,1)S(1)}, u32[]{:S(2)}, u32[]{:S(2)}) collective-permute-start(bf16[16,7168]{1,0:T(8,128)(2,1)} %get-tuple-element.58), channel_id=1, source_target_pairs={{0,2},{1,3},{2,4},{3,5},{4,6},{5,7},{6,0},{7,1},{8,10},{9,11},{10,... | collective-permute-start | bytes 688136 | tf_op jit(solution)/shard_map/ppermute | solution.py:420
  71.7 9.6 %collective-permute-start.12 = (bf16[16,7168]{1,0:T(8,128)(2,1)S(1)}, bf16[16,7168]{1,0:T(8,128)(2,1)S(1)}, u32[]{:S(2)}, u32[]{:S(2)}) collective-permute-start(bf16[16,7168]{1,0:T(8,128)(2,1)S(1)} %get-tuple-element.57), channel_id=1, source_target_pairs={{0,4},{1,5},{2,6},{3,7},{4,0},{5,1},{6,2},{7,3},{8,12},{9,13},{10,... | collective-permute-start | bytes 688136 | tf_op jit(solution)/shard_map/ppermute | solution.py:420
  74.6 6.7 %collective-permute-start.13 = (bf16[16,7168]{1,0:T(8,128)(2,1)S(1)}, bf16[16,7168]{1,0:T(8,128)(2,1)S(1)}, u32[]{:S(2)}, u32[]{:S(2)}) collective-permute-start(bf16[16,7168]{1,0:T(8,128)(2,1)S(1)} %get-tuple-element.56), channel_id=1, source_target_pairs={{0,6},{1,7},{2,0},{3,1},{4,2},{5,3},{6,4},{7,5},{8,14},{9,15},{10,... | collective-permute-start | bytes 688136 | tf_op jit(solution)/shard_map/ppermute | solution.py:420
  82.1 13.3 %collective-permute-start.14 = (bf16[16,7168]{1,0:T(8,128)(2,1)}, bf16[16,7168]{1,0:T(8,128)(2,1)S(1)}, u32[]{:S(2)}, u32[]{:S(2)}) collective-permute-start(bf16[16,7168]{1,0:T(8,128)(2,1)} %get-tuple-element.40), channel_id=1, source_target_pairs={{0,1},{1,0},{2,3},{3,2},{4,5},{5,4},{6,7},{7,6},{8,9},{9,8},{10,11... | collective-permute-start | bytes 688136 | tf_op jit(solution)/shard_map/ppermute | solution.py:430
  96.2 4.2 %collective-permute-start.18 = (bf16[16,1792]{1,0:T(8,128)(2,1)S(1)}, bf16[16,1792]{1,0:T(8,128)(2,1)S(1)}, u32[]{:S(2)}, u32[]{:S(2)}) collective-permute-start(bf16[16,1792]{1,0:T(8,128)(2,1)S(1)} %get-tuple-element.45), channel_id=1, source_target_pairs={{0,64},{64,128},{128,192},{192,0},{1,65},{65,129},{129,193},{193,1... | collective-permute-start | bytes 172040 | tf_op jit(solution)/shard_map/ppermute | solution.py:83
  98.1 5.1 %collective-permute-start.17 = (bf16[16,1792]{1,0:T(8,128)(2,1)S(1)}, bf16[16,1792]{1,0:T(8,128)(2,1)S(1)}, u32[]{:S(2)}, u32[]{:S(2)}) collective-permute-start(bf16[16,1792]{1,0:T(8,128)(2,1)S(1)} %get-tuple-element.44), channel_id=1, source_target_pairs={{0,128},{64,192},{128,0},{192,64},{1,129},{65,193},{129,1},{193,65... | collective-permute-start | bytes 172040 | tf_op jit(solution)/shard_map/ppermute | solution.py:83
  99.6 4.2 %collective-permute-start.16 = (bf16[16,1792]{1,0:T(8,128)(2,1)S(1)}, bf16[16,1792]{1,0:T(8,128)(2,1)S(1)}, u32[]{:S(2)}, u32[]{:S(2)}) collective-permute-start(bf16[16,1792]{1,0:T(8,128)(2,1)S(1)} %get-tuple-element.43), channel_id=1, source_target_pairs={{0,192},{64,0},{128,64},{192,128},{1,193},{65,1},{129,65},{193,129... | collective-permute-start | bytes 172040 | tf_op jit(solution)/shard_map/ppermute | solution.py:83
  105.5 24.0 %all-to-all-start = ((bf16[16,24,1792]{2,1,0:T(8,128)(2,1)}), bf16[16,24,1792]{2,1,0:T(8,128)(2,1)S(1)}, u32[]{:S(2)}, u32[]{:S(2)}) async-start(bf16[16,24,1792]{2,1,0:T(8,128)(2,1)} %bitcast.79), calls=%async_computation | async-start | bytes 2752512 | tf_op jit(solution)/shard_map/all_to_all | solution.py:64
  111.7 60.8 %collective-permute-start.31 = (bf16[1024,896]{1,0:T(8,128)(2,1)}, bf16[1024,896]{1,0:T(8,128)(2,1)}, u32[]{:S(2)}, u32[]{:S(2)}) collective-permute-start(bf16[1024,896]{1,0:T(8,128)(2,1)} %bitcast.72), channel_id=1, source_target_pairs={{0,32},{32,0},{1,33},{33,1},{2,34},{34,2},{3,35},{35,3},{4,36},{36... | collective-permute-start | bytes 5505032 | tf_op jit(solution)/shard_map/ppermute | solution.py:374
  135.0 12.1 %collective-permute-start.24 = (bf16[192,1024]{1,0:T(8,128)(2,1)S(1)}, bf16[192,1024]{1,0:T(8,128)(2,1)S(1)}, u32[]{:S(2)}, u32[]{:S(2)}) collective-permute-start(bf16[192,1024]{1,0:T(8,128)(2,1)S(1)} %get-tuple-element.51), channel_id=1, source_target_pairs={{0,64},{64,0},{128,192},{192,128},{1,65},{65,1},{129,193},{193,129... | collective-permute-start | bytes 1179656 | tf_op jit(solution)/shard_map/ppermute | solution.py:474
  135.4 18.8 %collective-permute-start.23 = (bf16[96,1024]{1,0:T(8,128)(2,1)S(1)}, bf16[96,1024]{1,0:T(8,128)(2,1)S(1)}, u32[]{:S(2)}, u32[]{:S(2)}) collective-permute-start(bf16[96,1024]{1,0:T(8,128)(2,1)S(1)} %get-tuple-element.49), channel_id=1, source_target_pairs={{0,192},{64,0},{128,64},{192,128},{1,193},{65,1},{129,65},{193,129... | collective-permute-start | bytes 589832 | tf_op jit(solution)/shard_map/ppermute | solution.py:83
  137.2 17.1 %collective-permute-start.22 = (bf16[96,1024]{1,0:T(8,128)(2,1)S(1)}, bf16[96,1024]{1,0:T(8,128)(2,1)S(1)}, u32[]{:S(2)}, u32[]{:S(2)}) collective-permute-start(bf16[96,1024]{1,0:T(8,128)(2,1)S(1)} %get-tuple-element.48), channel_id=1, source_target_pairs={{0,128},{64,192},{128,0},{192,64},{1,129},{65,193},{129,1},{193,65... | collective-permute-start | bytes 589832 | tf_op jit(solution)/shard_map/ppermute | solution.py:83
  139.5 18.5 %collective-permute-start.21 = (bf16[96,1024]{1,0:T(8,128)(2,1)S(1)}, bf16[96,1024]{1,0:T(8,128)(2,1)S(1)}, u32[]{:S(2)}, u32[]{:S(2)}) collective-permute-start(bf16[96,1024]{1,0:T(8,128)(2,1)S(1)} %get-tuple-element.47), channel_id=1, source_target_pairs={{0,64},{64,128},{128,192},{192,0},{1,65},{65,129},{129,193},{193,1... | collective-permute-start | bytes 589832 | tf_op jit(solution)/shard_map/ppermute | solution.py:83
  147.2 31.2 %copy-start.2 = (bf16[1,1024,896]{2,1,0:T(8,128)(2,1)S(1)}, bf16[1,1024,896]{2,1,0:T(8,128)(2,1)}, u32[]{:S(2)}) copy-start(bf16[1,1024,896]{2,1,0:T(8,128)(2,1)} %param.31) | copy-start | bytes 5505028
  147.3 12.7 %collective-permute-start.25 = (bf16[96,1024]{1,0:T(8,128)(2,1)S(1)}, bf16[96,1024]{1,0:T(8,128)(2,1)S(1)}, u32[]{:S(2)}, u32[]{:S(2)}) collective-permute-start(bf16[96,1024]{1,0:T(8,128)(2,1)S(1)} %slice.126), channel_id=1, source_target_pairs={{0,128},{64,192},{128,0},{192,64},{1,129},{65,193},{129,1},{193,65... | collective-permute-start | bytes 589832 | tf_op jit(solution)/shard_map/ppermute | solution.py:476
  160.3 6.6 %collective-permute-start.29 = (bf16[96,512]{1,0:T(8,128)(2,1)S(1)}, bf16[96,512]{1,0:T(8,128)(2,1)S(1)}, u32[]{:S(2)}, u32[]{:S(2)}) collective-permute-start(bf16[96,512]{1,0:T(8,128)(2,1)S(1)} %get-tuple-element.62), channel_id=1, source_target_pairs={{0,128},{64,192},{128,0},{192,64},{1,129},{65,193},{129,1},{193,65... | collective-permute-start | bytes 294920 | tf_op jit(solution)/shard_map/ppermute | solution.py:480
  167.0 11.4 %collective-permute-start.30 = (bf16[192,512]{1,0:T(8,128)(2,1)S(1)}, bf16[192,512]{1,0:T(8,128)(2,1)S(1)}, u32[]{:S(2)}, u32[]{:S(2)}) collective-permute-start(bf16[192,512]{1,0:T(8,128)(2,1)S(1)} %pad_maximum_fusion.refs_4_), channel_id=1, source_target_pairs={{0,64},{64,0},{128,192},{192,128},{1,65},{65,1},{129,193},{193,129... | collective-permute-start | bytes 589832 | tf_op jit(solution)/shard_map/ppermute | solution.py:482
  170.0 4.7 %collective-permute-start.26 = (bf16[96,512]{1,0:T(8,128)(2,1)S(1)}, bf16[96,512]{1,0:T(8,128)(2,1)S(1)}, u32[]{:S(2)}, u32[]{:S(2)}) collective-permute-start(bf16[96,512]{1,0:T(8,128)(2,1)S(1)} %get-tuple-element.63.refs_0_), channel_id=1, source_target_pairs={{0,64},{64,128},{128,192},{192,0},{1,65},{65,129},{129,193},{193,1... | collective-permute-start | bytes 294920 | tf_op jit(solution)/shard_map/ppermute | solution.py:83
  171.0 5.5 %collective-permute-start.27 = (bf16[96,512]{1,0:T(8,128)(2,1)S(1)}, bf16[96,512]{1,0:T(8,128)(2,1)S(1)}, u32[]{:S(2)}, u32[]{:S(2)}) collective-permute-start(bf16[96,512]{1,0:T(8,128)(2,1)S(1)} %get-tuple-element.63.refs_0_), channel_id=1, source_target_pairs={{0,128},{64,192},{128,0},{192,64},{1,129},{65,193},{129,1},{193,65... | collective-permute-start | bytes 294920 | tf_op jit(solution)/shard_map/ppermute | solution.py:83
  172.5 5.8 %collective-permute-start.28 = (bf16[96,512]{1,0:T(8,128)(2,1)S(1)}, bf16[96,512]{1,0:T(8,128)(2,1)S(1)}, u32[]{:S(2)}, u32[]{:S(2)}) collective-permute-start(bf16[96,512]{1,0:T(8,128)(2,1)S(1)} %get-tuple-element.63.refs_0_), channel_id=1, source_target_pairs={{0,192},{64,0},{128,64},{192,128},{1,193},{65,1},{129,65},{193,129... | collective-permute-start | bytes 294920 | tf_op jit(solution)/shard_map/ppermute | solution.py:83
  182.7 25.5 %all-to-all-start.1 = ((bf16[16,24,1792]{2,1,0:T(8,128)(2,1)}), bf16[16,24,1792]{2,1,0:T(8,128)(2,1)S(1)}, u32[]{:S(2)}, u32[]{:S(2)}) async-start(bf16[16,24,1792]{2,1,0:T(8,128)(2,1)} %bitcast.27), calls=%async_computation.1 | async-start | bytes 2752512 | tf_op jit(solution)/shard_map/all_to_all | solution.py:64
